TPU v7x, 32 devices: a whole 2x2x4 slice. The times are simulated.
32 devices in a mesh: dp: 8 (over y, x, core), tensor: 4 (over z).
Axes of the slice: x: 2, y: 2, z: 4, core: 2. Of those that a mesh axis runs over, the one named last changes fastest.
Arguments:
- hidden_in: bfloat16 [2048, 2048], P('dp'), may hold values from -6 to 6
- out_grad: bfloat16 [2048, 2048], P('dp'), may hold values from -6 to 6
- parents: int32 [8], replicated, may hold values from -1 to 3, as said below
- routes: int32 [2048, 4], P('dp'), may hold values from 0 to 7, all different within a row; in each aligned block of 256 rows (0 to 255, 256 to 511, ...) at most 256 rows name the same one
- attn_gain: float32 [2048], replicated, may hold values from 0.5 to 1.5
- w_query: bfloat16 [2048, 2048], P(None, 'tensor'), may hold values from -0.1875 to 0.1875
- w_key: bfloat16 [2048, 2048], P(None, 'tensor'), may hold values from -0.125 to 0.125
- w_value: bfloat16 [2048, 2048], P(None, 'tensor'), may hold values from -0.125 to 0.125
- b_query: float32 [16, 128], P('tensor'), may hold values from -0.625 to 0.625
- b_key: float32 [16, 128], P('tensor'), may hold values from -0.625 to 0.625
- b_value: float32 [16, 128], P('tensor'), may hold values from -0.125 to 0.125
- w_out: bfloat16 [2048, 2048], P(None, 'tensor'), may hold values from -2 to 2
- ffn_gain: float32 [2048], replicated, may hold values from 0.5 to 1.5
- w_router: bfloat16 [2048, 8], replicated, may hold values from -0.0625 to 0.0625
- shared_gate: bfloat16 [2048], replicated, may hold values from -0.125 to 0.125
- shared_w_gate: bfloat16 [2048, 5632], P(None, 'tensor'), may hold values from -0.125 to 0.125
- shared_w_up: bfloat16 [2048, 5632], P(None, 'tensor'), may hold values from -0.125 to 0.125
- shared_w_down: bfloat16 [2048, 5632], P(None, 'tensor'), may hold values from -0.25 to 0.25
- expert_w_gate: bfloat16 [8, 2048, 1408], P('dp', None, 'tensor'), may hold values from -0.125 to 0.125
- expert_w_up: bfloat16 [8, 2048, 1408], P('dp', None, 'tensor'), may hold values from -0.125 to 0.125
- expert_w_down: bfloat16 [8, 2048, 1408], P('dp', None, 'tensor'), may hold values from -1 to 1
Outputs:
- hidden_out: bfloat16 [2048, 2048], P('dp')
- hidden_in_grad: bfloat16 [2048, 2048], P('dp')
- attn_gain_grad: float32 [2048], P('dp')
- w_query_grad: float32 [2048, 2048], P('dp', 'tensor')
- w_key_grad: float32 [2048, 2048], P('dp', 'tensor')
- w_value_grad: float32 [2048, 2048], P('dp', 'tensor')
- b_query_grad: float32 [16, 128], P('tensor', 'dp')
- b_key_grad: float32 [16, 128], P('tensor', 'dp')
- b_value_grad: float32 [16, 128], P('tensor', 'dp')
- w_out_grad: float32 [2048, 2048], P('dp', 'tensor')
- ffn_gain_grad: float32 [2048], P('dp')
- w_router_grad: float32 [2048, 8], P('dp')
- shared_gate_grad: float32 [2048], P('dp')
- shared_w_gate_grad: float32 [2048, 5632], P('dp', 'tensor')
- shared_w_up_grad: float32 [2048, 5632], P('dp', 'tensor')
- shared_w_down_grad: float32 [2048, 5632], P('dp', 'tensor')
- expert_w_gate_grad: float32 [8, 2048, 1408], P('dp', None, 'tensor')
- expert_w_up_grad: float32 [8, 2048, 1408], P('dp', None, 'tensor')
- expert_w_down_grad: float32 [8, 2048, 1408], P('dp', None, 'tensor')
Inputs may be any that keep to these rules, and one draw needn't show every extreme that they name: `parents`: the segments form 1 trees. Each tree has a chain of 2 trunk segments whose first has parent -1, 2 branch segments whose parent is the tree's last trunk segment, and 2 leaf segments under each branch. The trunks come first, tree after tree, then the branches in the same order of trees, then the leaves in the reversed order of trees. `routes`: each row names 4 different experts. Among the rows of one index of dp no expert is named more than 256 times, and in every draw some expert is named exactly that often by the rows of some index.
All inputs are finite; a program needn't handle non-finite values.
Results may differ from a plain program's by a relative error of at most 0.019.
Values may be sent and summed in bfloat16 or wider, within the bound.
A program may use at most 384 MiB of HBM per device.

v0:
```python
import jax
import jax.numpy as jnp
from jax import lax
from jax.sharding import PartitionSpec as P

HEAD_DIM = 128
SEG = 256


epsilon = 1e-06
rope_base = 1000000.0
highest = lax.Precision.HIGHEST


def prefix(part, axis, combine, identity):
    place = lax.axis_index(axis)
    gathered = lax.all_gather(part, axis)
    state = jnp.zeros_like(part) + jnp.asarray(identity, part.dtype)

    def one(step, state):
        return combine(state, lax.dynamic_index_in_dim(gathered, step, 0, False))

    return lax.fori_loop(0, place, one, state)


def product(left, right):
    return jnp.dot(left, right, preferred_element_type=jnp.float32)


def product_tn(left, right):
    return lax.dot_general(
        left, right, (((0,), (0,)), ((), ())), preferred_element_type=jnp.float32
    )


def product_nt(left, right):
    return lax.dot_general(
        left, right, (((1,), (1,)), ((), ())), preferred_element_type=jnp.float32
    )


def ancestry(parents):
    seg_count = parents.shape[0]
    labels = jnp.arange(seg_count, dtype=jnp.int32)

    def climb(level, carry):
        current, reach = carry
        upward = jnp.where(current >= 0, parents[jnp.maximum(current, 0)], -1)
        reach = jnp.maximum(reach, (upward[:, None] == labels[None, :]).astype(jnp.float32))
        return (upward, reach)

    start = (labels, jnp.eye(seg_count, dtype=jnp.float32))
    return lax.fori_loop(0, seg_count, climb, start)[1]


def rope_tables(positions):
    freqs = rope_base ** (-jnp.arange(0, HEAD_DIM, 2, dtype=jnp.float32) / HEAD_DIM)
    angles = positions[:, None] * freqs[None, :]
    angles = jnp.concatenate([angles, angles], 1)
    return (jnp.cos(angles)[:, None, :], jnp.sin(angles)[:, None, :])


def turn_heads(matrix, cosine, sine, sign_value):
    shaped = matrix.reshape(matrix.shape[0], matrix.shape[1] // HEAD_DIM, HEAD_DIM)
    half = HEAD_DIM // 2
    turned = jnp.concatenate([-shaped[..., half:], shaped[..., :half]], -1)
    return (shaped * cosine + sign_value * turned * sine).reshape(matrix.shape)


def norm_parts(values):
    scale_rows = lax.rsqrt(jnp.mean(values * values, 1, keepdims=True) + epsilon)
    return (scale_rows, values * scale_rows)


def norm_back(grad_rows, unit_rows, scale_rows, gain):
    unit_grad = grad_rows * gain
    return scale_rows * (unit_grad - unit_rows * jnp.mean(unit_grad * unit_rows, 1, keepdims=True))


def swiglu(pre_gate, pre_up):
    return (pre_gate * jax.nn.sigmoid(pre_gate) * pre_up).astype(jnp.bfloat16)


def swiglu_back(hidden_grad, pre_gate, pre_up):
    sigmoid_gate = jax.nn.sigmoid(pre_gate)
    up_grad = (hidden_grad * pre_gate * sigmoid_gate).astype(jnp.bfloat16)
    gate_grad = (
        hidden_grad * pre_up * sigmoid_gate * (1.0 + pre_gate * (1.0 - sigmoid_gate))
    ).astype(jnp.bfloat16)
    return (gate_grad, up_grad)


def fetch_keys(key_value):
    return lax.all_gather(key_value, "dp", axis=0, tiled=True)


def add_counts(earlier_part, later_part):
    return earlier_part + later_part


def attend_forward(query_rot, key_value, allowed, score_scale):
    tok_rows, local_width = query_rot.shape
    head_count = local_width // HEAD_DIM

    def one_head(head_index, carry):
        outputs, lse_rows = carry
        offset = head_index * HEAD_DIM
        query_head = lax.dynamic_slice_in_dim(query_rot, offset, HEAD_DIM, 1)
        key_head = lax.dynamic_slice_in_dim(key_value, offset, HEAD_DIM, 1)
        value_head = lax.dynamic_slice_in_dim(key_value, local_width + offset, HEAD_DIM, 1)
        scores = jnp.where(allowed, product_nt(query_head, key_head) * score_scale, -jnp.inf)
        peak = jnp.max(scores, 1, keepdims=True)
        log_total = peak + jnp.log(jnp.sum(jnp.exp(scores - peak), 1, keepdims=True))
        weights = jnp.exp(scores - log_total).astype(jnp.bfloat16)
        outputs = lax.dynamic_update_slice_in_dim(outputs, product(weights, value_head), offset, 1)
        lse_rows = lax.dynamic_update_slice_in_dim(lse_rows, log_total, head_index, 1)
        return (outputs, lse_rows)

    start = (
        jnp.zeros((tok_rows, local_width), jnp.float32),
        jnp.zeros((tok_rows, head_count), jnp.float32),
    )
    return lax.fori_loop(0, head_count, one_head, start)


def attend_backward(query_rot, key_value, allowed, lse_rows, attended_grad, score_scale):
    tok_rows, local_width = query_rot.shape
    head_count = local_width // HEAD_DIM
    key_rows = key_value.shape[0]

    def one_head(head_index, carry):
        query_grad, kv_grad = carry
        offset = head_index * HEAD_DIM
        query_head = lax.dynamic_slice_in_dim(query_rot, offset, HEAD_DIM, 1)
        key_head = lax.dynamic_slice_in_dim(key_value, offset, HEAD_DIM, 1)
        value_head = lax.dynamic_slice_in_dim(key_value, local_width + offset, HEAD_DIM, 1)
        grad_head = lax.dynamic_slice_in_dim(attended_grad, offset, HEAD_DIM, 1)
        log_total = lax.dynamic_slice_in_dim(lse_rows, head_index, 1, 1)
        scores = jnp.where(allowed, product_nt(query_head, key_head) * score_scale, -jnp.inf)
        weights = jnp.exp(scores - log_total)
        weight_grad = product_nt(grad_head, value_head)
        center = jnp.sum(weights * weight_grad, 1, keepdims=True)
        score_grad = (weights * (weight_grad - center)).astype(jnp.bfloat16)
        query_part = product(score_grad, key_head) * score_scale
        key_part = product_tn(score_grad, query_head) * score_scale
        value_part = product_tn(weights.astype(jnp.bfloat16), grad_head)
        query_grad = lax.dynamic_update_slice_in_dim(query_grad, query_part, offset, 1)
        kv_grad = lax.dynamic_update_slice_in_dim(kv_grad, key_part, offset, 1)
        kv_grad = lax.dynamic_update_slice_in_dim(kv_grad, value_part, local_width + offset, 1)
        return (query_grad, kv_grad)

    start = (
        jnp.zeros((tok_rows, local_width), jnp.float32),
        jnp.zeros((key_rows, 2 * local_width), jnp.float32),
    )
    return lax.fori_loop(0, head_count, one_head, start)


def on_device(
    hidden_in,
    out_grad,
    parents,
    routes,
    attn_gain,
    w_query,
    w_key,
    w_value,
    b_query,
    b_key,
    b_value,
    w_out,
    ffn_gain,
    w_router,
    shared_gate,
    shared_w_gate,
    shared_w_up,
    shared_w_down,
    expert_w_gate,
    expert_w_up,
    expert_w_down,
):
    tok_rows, model_width = hidden_in.shape
    devices = lax.axis_size("dp")
    all_rows = tok_rows * devices
    local_width = w_query.shape[1]
    experts = w_router.shape[1]
    top_count = routes.shape[1]
    route_cap = max(2, 2 * tok_rows * top_count // experts)
    capacity = 5 * tok_rows * top_count // 4
    score_scale = HEAD_DIM ** (-0.5)
    reach = ancestry(parents)
    global_rows = lax.axis_index("dp") * tok_rows + jnp.arange(tok_rows, dtype=jnp.int32)
    segments = global_rows // SEG
    seg_onehot = (
        segments[:, None] == jnp.arange(parents.shape[0], dtype=jnp.int32)[None, :]
    ).astype(jnp.float32)
    ancestors = jnp.dot(seg_onehot, reach, precision=highest)
    positions = (jnp.sum(ancestors, 1) - 1.0) * SEG + (global_rows % SEG).astype(jnp.float32)
    cosine, sine = rope_tables(positions)
    hidden_f = hidden_in.astype(jnp.float32)
    attn_scale, attn_unit = norm_parts(hidden_f)
    attn_normed = (attn_unit * attn_gain).astype(jnp.bfloat16)
    query_rot = turn_heads(
        product(attn_normed, w_query) + b_query.reshape(-1), cosine, sine, 1.0
    ).astype(jnp.bfloat16)
    key_rot = turn_heads(product(attn_normed, w_key) + b_key.reshape(-1), cosine, sine, 1.0).astype(
        jnp.bfloat16
    )
    value_rows = (product(attn_normed, w_value) + b_value.reshape(-1)).astype(jnp.bfloat16)
    key_value = jnp.concatenate([key_rot, value_rows], 1)
    gathered = fetch_keys(key_value)
    allowed = jnp.repeat(ancestors > 0.5, SEG, axis=1) & (
        jnp.arange(all_rows, dtype=jnp.int32)[None, :] <= global_rows[:, None]
    )
    attended, lse_rows = attend_forward(query_rot, gathered, allowed, score_scale)
    attended_low = attended.astype(jnp.bfloat16)
    attn_full = lax.psum(product_nt(attended_low, w_out), "tensor")
    residual = hidden_f + attn_full
    ffn_scale, ffn_unit = norm_parts(residual)
    ffn_normed = (ffn_unit * ffn_gain).astype(jnp.bfloat16)
    probs = jax.nn.softmax(product(ffn_normed, w_router), 1)
    pair_onehot = routes[:, :, None] == jnp.arange(experts, dtype=jnp.int32)[None, None, :]
    pair_gate = jnp.sum(jnp.where(pair_onehot, probs[:, None, :], 0.0), 2)
    shared_weight = jax.nn.sigmoid(product(ffn_normed, shared_gate))
    token_hits = jnp.sum(pair_onehot.astype(jnp.int32), 1)
    offsets = prefix(jnp.sum(token_hits, 0), "dp", add_counts, jnp.zeros((experts,), jnp.int32))
    earlier = jnp.cumsum(token_hits, 0) - token_hits
    local_rank = jnp.sum(jnp.where(pair_onehot, earlier[:, None, :], 0), 2)
    global_slot = local_rank + jnp.sum(jnp.where(pair_onehot, offsets[None, None, :], 0), 2)
    keep = global_slot < capacity
    gate_kept = jnp.where(keep, pair_gate, 0.0)
    buffer_pos = (routes * route_cap + local_rank).reshape(-1)
    pair_count = tok_rows * top_count
    pair_ids = jnp.arange(pair_count, dtype=jnp.int32).reshape(tok_rows, top_count)
    slot_pair = (
        jnp.full((experts * route_cap,), pair_count, jnp.int32)
        .at[buffer_pos]
        .set(jnp.where(keep, pair_ids, pair_count).reshape(-1))
    )
    slot_token = slot_pair // top_count
    padded_normed = jnp.concatenate([ffn_normed, jnp.zeros((1, model_width), jnp.bfloat16)], 0)
    send_rows = jnp.take(padded_normed, slot_token, axis=0).reshape(experts, route_cap, model_width)
    expert_in = lax.all_to_all(send_rows, "dp", split_axis=0, concat_axis=0, tiled=True).reshape(
        experts * route_cap, model_width
    )
    expert_pre_gate = product(expert_in, expert_w_gate[0])
    expert_pre_up = product(expert_in, expert_w_up[0])
    expert_hidden = swiglu(expert_pre_gate, expert_pre_up)
    expert_result = product_nt(expert_hidden, expert_w_down[0]).reshape(
        experts, route_cap, model_width
    )
    returned = lax.all_to_all(expert_result, "dp", split_axis=0, concat_axis=0, tiled=True).reshape(
        experts * route_cap, model_width
    )
    pair_out = jnp.take(returned, buffer_pos, axis=0).reshape(tok_rows, top_count, model_width)
    moe_part = jnp.sum(gate_kept[:, :, None] * pair_out, 1)
    shared_pre_gate = product(ffn_normed, shared_w_gate)
    shared_pre_up = product(ffn_normed, shared_w_up)
    shared_hidden = swiglu(shared_pre_gate, shared_pre_up)
    shared_result = product_nt(shared_hidden, shared_w_down)
    ffn_full = lax.psum(
        (moe_part + shared_weight[:, None] * shared_result).astype(jnp.bfloat16), "tensor"
    ).astype(jnp.float32)
    hidden_out = (residual + ffn_full).astype(jnp.bfloat16)
    out_f = out_grad.astype(jnp.float32)
    shared_out_grad = (shared_weight[:, None] * out_f).astype(jnp.bfloat16)
    grad_shared_down = product_tn(shared_out_grad, shared_hidden)
    shared_gate_rows, shared_up_rows = swiglu_back(
        product(shared_out_grad, shared_w_down), shared_pre_gate, shared_pre_up
    )
    grad_shared_gate_w = product_tn(ffn_normed, shared_gate_rows)
    grad_shared_up = product_tn(ffn_normed, shared_up_rows)
    normed_part = product_nt(shared_gate_rows, shared_w_gate) + product_nt(
        shared_up_rows, shared_w_up
    )
    weight_part = jnp.sum(out_f * shared_result, 1)
    pair_grad = (
        (gate_kept[:, :, None] * out_f[:, None, :])
        .astype(jnp.bfloat16)
        .reshape(pair_count, model_width)
    )
    padded_grad = jnp.concatenate([pair_grad, jnp.zeros((1, model_width), jnp.bfloat16)], 0)
    send_grads = jnp.take(padded_grad, slot_pair, axis=0).reshape(experts, route_cap, model_width)
    expert_grad_in = lax.all_to_all(
        send_grads, "dp", split_axis=0, concat_axis=0, tiled=True
    ).reshape(experts * route_cap, model_width)
    grad_expert_down = product_tn(expert_grad_in, expert_hidden)[None]
    expert_gate_rows, expert_up_rows = swiglu_back(
        product(expert_grad_in, expert_w_down[0]), expert_pre_gate, expert_pre_up
    )
    grad_expert_gate = product_tn(expert_in, expert_gate_rows)[None]
    grad_expert_up = product_tn(expert_in, expert_up_rows)[None]
    expert_in_grad = product_nt(expert_gate_rows, expert_w_gate[0]) + product_nt(
        expert_up_rows, expert_w_up[0]
    )
    back_rows = lax.all_to_all(
        expert_in_grad.reshape(experts, route_cap, model_width),
        "dp",
        split_axis=0,
        concat_axis=0,
        tiled=True,
    ).reshape(experts * route_cap, model_width)
    pair_back = jnp.take(back_rows, buffer_pos, axis=0).reshape(tok_rows, top_count, model_width)
    normed_part = normed_part + jnp.sum(jnp.where(keep[:, :, None], pair_back, 0.0), 1)
    gate_part = jnp.where(keep, jnp.sum(out_f[:, None, :] * pair_out, 2), 0.0)
    normed_grad, gate_grad, weight_grad = lax.psum((normed_part, gate_part, weight_part), "tensor")
    prob_grad = jnp.sum(jnp.where(pair_onehot, gate_grad[:, :, None], 0.0), 1)
    logit_grad = (probs * (prob_grad - jnp.sum(probs * prob_grad, 1, keepdims=True))).astype(
        jnp.bfloat16
    )
    grad_router = product_tn(ffn_normed, logit_grad)
    weight_logit_grad = (weight_grad * shared_weight * (1.0 - shared_weight)).astype(jnp.bfloat16)
    grad_shared_weight = product_tn(ffn_normed, weight_logit_grad)
    normed_grad = (
        normed_grad
        + product_nt(logit_grad, w_router)
        + weight_logit_grad.astype(jnp.float32)[:, None] * shared_gate.astype(jnp.float32)[None, :]
    )
    grad_ffn_gain = jnp.sum(normed_grad * ffn_unit, 0)
    residual_grad = out_f + norm_back(normed_grad, ffn_unit, ffn_scale, ffn_gain)
    residual_low = residual_grad.astype(jnp.bfloat16)
    grad_out_proj = product_tn(residual_low, attended_low)
    attended_grad = product(residual_low, w_out).astype(jnp.bfloat16)
    gathered_back = fetch_keys(key_value)
    query_grad, kv_grad_all = attend_backward(
        query_rot, gathered_back, allowed, lse_rows, attended_grad, score_scale
    )
    kv_grad = lax.psum_scatter(kv_grad_all, "dp", scatter_dimension=0, tiled=True)
    query_pre_grad = turn_heads(query_grad, cosine, sine, -1.0).astype(jnp.bfloat16)
    key_pre_grad = turn_heads(kv_grad[:, :local_width], cosine, sine, -1.0).astype(jnp.bfloat16)
    value_pre_grad = kv_grad[:, local_width:].astype(jnp.bfloat16)
    grad_query = product_tn(attn_normed, query_pre_grad)
    grad_key = product_tn(attn_normed, key_pre_grad)
    grad_value = product_tn(attn_normed, value_pre_grad)
    bias_shape = b_query.shape
    grad_bias_query = jnp.sum(query_pre_grad.astype(jnp.float32), 0).reshape(bias_shape)
    grad_bias_key = jnp.sum(key_pre_grad.astype(jnp.float32), 0).reshape(bias_shape)
    grad_bias_value = jnp.sum(value_pre_grad.astype(jnp.float32), 0).reshape(bias_shape)
    attn_part = (
        product_nt(query_pre_grad, w_query)
        + product_nt(key_pre_grad, w_key)
        + product_nt(value_pre_grad, w_value)
    )
    attn_normed_grad = lax.psum(attn_part, "tensor")
    grad_attn_gain = jnp.sum(attn_normed_grad * attn_unit, 0)
    hidden_in_grad = (
        residual_grad + norm_back(attn_normed_grad, attn_unit, attn_scale, attn_gain)
    ).astype(jnp.bfloat16)
    (
        sum_query,
        sum_key,
        sum_value,
        sum_out,
        sum_attn_gain,
        sum_bias_query,
        sum_bias_key,
        sum_bias_value,
        sum_shared_gate_w,
        sum_shared_up,
        sum_shared_down,
        sum_router,
        sum_ffn_gain,
        sum_shared_weight,
    ) = (
        lax.psum_scatter(grad_query, "dp", scatter_dimension=0, tiled=True),
        lax.psum_scatter(grad_key, "dp", scatter_dimension=0, tiled=True),
        lax.psum_scatter(grad_value, "dp", scatter_dimension=0, tiled=True),
        lax.psum_scatter(grad_out_proj, "dp", scatter_dimension=0, tiled=True),
        lax.psum_scatter(grad_attn_gain, "dp", scatter_dimension=0, tiled=True),
        lax.psum_scatter(grad_bias_query, "dp", scatter_dimension=1, tiled=True),
        lax.psum_scatter(grad_bias_key, "dp", scatter_dimension=1, tiled=True),
        lax.psum_scatter(grad_bias_value, "dp", scatter_dimension=1, tiled=True),
        lax.psum_scatter(grad_shared_gate_w, "dp", scatter_dimension=0, tiled=True),
        lax.psum_scatter(grad_shared_up, "dp", scatter_dimension=0, tiled=True),
        lax.psum_scatter(grad_shared_down, "dp", scatter_dimension=0, tiled=True),
        lax.psum_scatter(grad_router, "dp", scatter_dimension=0, tiled=True),
        lax.psum_scatter(grad_ffn_gain, "dp", scatter_dimension=0, tiled=True),
        lax.psum_scatter(grad_shared_weight, "dp", scatter_dimension=0, tiled=True),
    )
    return (
        hidden_out,
        hidden_in_grad,
        sum_attn_gain,
        sum_query,
        sum_key,
        sum_value,
        sum_bias_query,
        sum_bias_key,
        sum_bias_value,
        sum_out,
        sum_ffn_gain,
        sum_router,
        sum_shared_weight,
        sum_shared_gate_w,
        sum_shared_up,
        sum_shared_down,
        grad_expert_gate,
        grad_expert_up,
        grad_expert_down,
    )


def solution(mesh):
    return jax.shard_map(
        on_device,
        mesh=mesh,
        in_specs=(
            P("dp", None),
            P("dp", None),
            P(),
            P("dp", None),
            P(),
            P(None, "tensor"),
            P(None, "tensor"),
            P(None, "tensor"),
            P("tensor", None),
            P("tensor", None),
            P("tensor", None),
            P(None, "tensor"),
            P(),
            P(),
            P(),
            P(None, "tensor"),
            P(None, "tensor"),
            P(None, "tensor"),
            P("dp", None, "tensor"),
            P("dp", None, "tensor"),
            P("dp", None, "tensor"),
        ),
        out_specs=(
            P("dp", None),
            P("dp", None),
            P("dp"),
            P("dp", "tensor"),
            P("dp", "tensor"),
            P("dp", "tensor"),
            P("tensor", "dp"),
            P("tensor", "dp"),
            P("tensor", "dp"),
            P("dp", "tensor"),
            P("dp"),
            P("dp", None),
            P("dp"),
            P("dp", "tensor"),
            P("dp", "tensor"),
            P("dp", "tensor"),
            P("dp", None, "tensor"),
            P("dp", None, "tensor"),
            P("dp", None, "tensor"),
        ),
        check_vma=False,
    )
```

profile of v0, /device:TPU:0, one launch (start us, length us, event | category | flops | bytes accessed | tf_op | source)
XLA Modules:
  0.0 1969.1 jit_solution(7226027015162608349)
XLA Ops:
  36.7 9.4 all-reduce.2
  46.2 27.2 %all-gather.3.cloned.1.call-done = bf16[2048,1024]{1,0:T(8,128)(2,1)} async-done(((bf16[256,1024]{1,0:T(8,128)(2,1)}), bf16[2048,1024]{1,0:T(8,128)(2,1)}) %all-gather.3.cloned.1.call-update) | async-done | bytes 4194320 | tf_op jit(solution)/shard_map/all_gather | solution.py:94
  73.4 31.8 %while.65 = (s32[]{:T(128)}, bf16[256,512]{1,0:T(8,128)(2,1)S(1)}, f32[256,4]{0,1:T(4,128)}, bf16[256,512]{1,0:T(8,128)(2,1)}, bf16[2048,1024]{1,0:T(8,128)(2,1)}, /*index=5*/pred[256,8]{1,0:T(8,128)(4,1)S(1)}, s32[256]{0:T(256)S(1)}) while((s32[]{:T(128)}, bf16[256,512]{1,0:T(8,128)(2,1)S(1)}, f32[256,4]{0,1:T(4,128)}, ...), condition=%wide.region_7.8_spmd.clone.clone, body=%wide.region_4.7_spmd.clone.sunk.clone | while | flops 273153792 | bytes 18034916 | solution.py:123
  113.7 80.4 %all-reduce.13.cloned.1.call-done = f32[256,2048]{1,0:T(8,128)} async-done(((f32[256,2048]{1,0:T(8,128)}), f32[256,2048]{1,0:T(8,128)}) %all-reduce.13.cloned.1.call-update) | async-done | bytes 2097168 | tf_op jit(solution)/shard_map/psum | solution.py:217
  197.7 11.0 gather_fusion.1
  208.7 7.4 broadcast_select_fusion.1
  216.1 97.9 %all_to_all.20 = bf16[8,256,2048]{2,1,0:T(8,128)(2,1)S(1)} all-to-all(bf16[8,256,2048]{2,1,0:T(8,128)(2,1)} %broadcast_select_fusion.1), channel_id=1, replica_groups=mesh['dp'=8,'tensor'=4] {'dp'}, dimensions={0} | all-to-all | bytes 16777216 | tf_op jit(solution)/shard_map/all_to_all | solution.py:243
  323.5 8.2 fusion.48
  331.7 6.0 all-to-all-start.1
  343.3 10.1 mul.466
  359.1 6.2 multiply_convert_fusion.9
  369.3 152.4 %all-to-all-done.1 = f32[8,256,2048]{2,1,0:T(8,128)} async-done(((f32[8,256,2048]{2,1,0:T(8,128)}), f32[8,256,2048]{2,1,0:T(8,128)}, u32[]{:S(2)}, u32[]{:S(2)}) %all-to-all-start.1) | async-done | bytes 16777248 | tf_op jit(solution)/shard_map/all_to_all | solution.py:252
  521.7 14.7 gather_fusion.3
  536.4 10.0 multiply_reduce_fusion.1
  546.6 9.9 all-reduce.7
  563.1 19.1 gather_fusion.2
  582.2 7.6 broadcast_select_fusion
  589.7 98.6 %all_to_all.21 = bf16[8,256,2048]{2,1,0:T(8,128)(2,1)S(1)} all-to-all(bf16[8,256,2048]{2,1,0:T(8,128)(2,1)} %broadcast_select_fusion), channel_id=1, replica_groups=mesh['dp'=8,'tensor'=4] {'dp'}, dimensions={0} | all-to-all | bytes 16777216 | tf_op jit(solution)/shard_map/all_to_all | solution.py:284
  693.6 6.5 fusion.57
  700.1 12.6 convolution_add_fusion
  719.4 6.7 multiply_convert_fusion.7
  732.8 169.8 %all-to-all-done.3 = f32[8,256,2048]{2,1,0:T(8,128)} async-done(((f32[8,256,2048]{2,1,0:T(8,128)}), f32[8,256,2048]{2,1,0:T(8,128)}, u32[]{:S(2)}, u32[]{:S(2)}) %all-to-all-start.3) | async-done | bytes 16777248 | tf_op jit(solution)/shard_map/all_to_all | solution.py:296
  902.5 14.8 gather_fusion.4
  917.3 7.3 broadcast_select_fusion.2
  924.6 9.8 reshape.407
  934.4 11.5 select_reduce_fusion
  945.8 7.2 fusion.39
  953.2 10.1 reshape.403
  963.2 11.4 multiply_reduce_fusion.2
  978.3 57.9 %all-reduce.17.cloned.1.call-done = f32[256,2048]{1,0:T(8,128)} async-done(((f32[256,2048]{1,0:T(8,128)}), f32[256,2048]{1,0:T(8,128)}) %all-reduce.17.cloned.1.call-update) | async-done | bytes 2097168 | tf_op jit(solution)/shard_map/psum | solution.py:306
  1040.6 49.2 %all-reduce.15.cloned.1.call-done = bf16[256,2048]{1,0:T(8,128)(2,1)} async-done(((bf16[256,2048]{1,0:T(8,128)(2,1)}), bf16[256,2048]{1,0:T(8,128)(2,1)}) %all-reduce.15.cloned.1.call-update) | async-done | bytes 1048592 | tf_op jit(solution)/shard_map/psum | solution.py:261
  1100.8 55.1 %while.66 = (s32[]{:T(128)}, f32[256,512]{1,0:T(8,128)}, f32[2048,1024]{1,0:T(8,128)}, bf16[256,512]{1,0:T(8,128)(2,1)}, bf16[2048,1024]{1,0:T(8,128)(2,1)}, /*i...) while((s32[]{:T(128)}, f32[256,512]{1,0:T(8,128)}, ...), condition=%wide.region_35.37_spmd.clone.clone, body=%wide.region_33.36_spmd.clone.sunk.clone | while | flops 677150464 | bytes 30286092 | solution.py:156
  1160.5 66.2 %reduce-scatter.19.cloned.1.call-done = f32[256,1024]{1,0:T(8,128)} async-done(((f32[2048,1024]{1,0:T(8,128)}), f32[256,1024]{1,0:T(8,128)}) %reduce-scatter.19.cloned.1.call-update) | async-done | bytes 1048592 | tf_op jit(solution)/shard_map/reduce_scatter | solution.py:328
  1251.8 7.3 fusion.112
  1259.1 7.2 fusion.113
  1267.5 7.3 fusion.69
  1294.2 8.7 convolution_bitcast_fusion
  1302.9 8.3 convolution_bitcast_fusion.1
  1318.7 24.1 %reduce-scatter.41.cloned.1.call-done = f32[16,4]{1,0:T(8,128)} async-done(((f32[128,4]{1,0:T(8,128)}), f32[16,4]{1,0:T(8,128)}) %reduce-scatter.41.cloned.1.call-update) | async-done | bytes 272
  1344.1 87.7 %all-reduce.19.cloned.1.call-done = f32[256,2048]{1,0:T(8,128)} async-done(((f32[256,2048]{1,0:T(8,128)}), f32[256,2048]{1,0:T(8,128)}) %all-reduce.19.cloned.1.call-update) | async-done | bytes 2097168 | tf_op jit(solution)/shard_map/psum | solution.py:344
  1434.1 24.1 %all-reduce.6 = (f32[2048]{0:T(1024)S(1)}, f32[2048]{0:T(1024)S(1)}, f32[2048]{0:T(1024)S(1)}) all-reduce(f32[2048]{0:T(1024)S(1)} %get-tuple-element.546, f32[2048]{0:T(1024)S(1)} %get-tuple-element.544, f32[2048]{0:T(1024)S(1)} %bitcast.215), channel_id=4, replica_groups=mesh['dp'=8,'tensor'=4] {'dp'}, use_global_device_ids=true, to_apply=%region_40.42.clone | all-reduce | flops 6144 | bytes 49152
  1467.4 91.3 %reduce-scatter.31.cloned.1.call-done = f32[256,1408]{1,0:T(8,128)} async-done(((f32[2048,1408]{1,0:T(8,128)}), f32[256,1408]{1,0:T(8,128)}) %reduce-scatter.31.cloned.1.call-update) | async-done | bytes 1441808 | tf_op jit(solution)/shard_map/reduce_scatter | solution.py:373
  1558.7 91.1 %reduce-scatter.33.cloned.1.call-done = f32[256,1408]{1,0:T(8,128)} async-done(((f32[2048,1408]{1,0:T(8,128)}), f32[256,1408]{1,0:T(8,128)}) %reduce-scatter.33.cloned.1.call-update) | async-done | bytes 1441808 | tf_op jit(solution)/shard_map/reduce_scatter | solution.py:374
  1649.8 91.3 %reduce-scatter.35.cloned.1.call-done = f32[256,1408]{1,0:T(8,128)} async-done(((f32[2048,1408]{1,0:T(8,128)}), f32[256,1408]{1,0:T(8,128)}) %reduce-scatter.35.cloned.1.call-update) | async-done | bytes 1441808 | tf_op jit(solution)/shard_map/reduce_scatter | solution.py:375
  1741.1 55.5 %reduce-scatter.27.cloned.1.call-done = f32[256,512]{1,0:T(8,128)} async-done(((f32[2048,512]{1,0:T(8,128)}), f32[256,512]{1,0:T(8,128)}) %reduce-scatter.27.cloned.1.call-update) | async-done | bytes 524304 | tf_op jit(solution)/shard_map/reduce_scatter | solution.py:368
  1796.6 55.1 %reduce-scatter.21.cloned.1.call-done = f32[256,512]{1,0:T(8,128)} async-done(((f32[2048,512]{1,0:T(8,128)}), f32[256,512]{1,0:T(8,128)}) %reduce-scatter.21.cloned.1.call-update) | async-done | bytes 524304 | tf_op jit(solution)/shard_map/reduce_scatter | solution.py:365
  1851.7 55.5 %reduce-scatter.23.cloned.1.call-done = f32[256,512]{1,0:T(8,128)} async-done(((f32[2048,512]{1,0:T(8,128)}), f32[256,512]{1,0:T(8,128)}) %reduce-scatter.23.cloned.1.call-update) | async-done | bytes 524304 | tf_op jit(solution)/shard_map/reduce_scatter | solution.py:366
  1907.3 55.1 %reduce-scatter.25.cloned.1.call-done = f32[256,512]{1,0:T(8,128)} async-done(((f32[2048,512]{1,0:T(8,128)}), f32[256,512]{1,0:T(8,128)}) %reduce-scatter.25.cloned.1.call-update) | async-done | bytes 524304 | tf_op jit(solution)/shard_map/reduce_scatter | solution.py:367
  (420 shorter events, 271.7 us)
Async XLA Ops:
  7.2 98.1 %copy-start = (bf16[2048,512]{1,0:T(8,128)(2,1)S(1)}, bf16[2048,512]{1,0:T(8,128)(2,1)}, u32[]{:S(2)}) copy-start(bf16[2048,512]{1,0:T(8,128)(2,1)} %param.42) | copy-start | bytes 6291460
  7.2 66.2 %all-gather.3.cloned.1.call-start = ((), (), s32[]{:S(2)}) async-start(), calls=%async_computation.16 | async-start | bytes 4718592 | tf_op jit(solution)/shard_map/all_gather | solution.py:94
  8.9 20.7 %copy-start.45 = (f32[256]{0:T(256)}, f32[256]{0:T(256)S(1)}, u32[]{:S(2)}) copy-start(f32[256]{0:T(256)S(1)} %add_rsqrt_fusion.1) | copy-start | bytes 3076
  8.9 5.6 copy-start.4
  9.0 5.6 copy-start.36
  33.9 160.2 %all-reduce.13.cloned.1.call-start = ((), (), s32[]{:S(2)}) async-start(), calls=%async_computation.17 | async-start | bytes 4194304 | tf_op jit(solution)/shard_map/psum | solution.py:217
  35.1 38.3 %copy-start.57 = (s32[8,3]{0,1:T(4,128)}, s32[8,3]{0,1:T(4,128)S(1)}, u32[]{:S(2)}) copy-start(s32[8,3]{0,1:T(4,128)S(1)} %reduce-window.9) | copy-start | bytes 292
  113.7 82.4 %copy-start.47 = (f32[2048]{0:T(1024)S(1)}, f32[2048]{0:T(1024)}, u32[]{:S(2)}) copy-start(f32[2048]{0:T(1024)} %param.43) | copy-start | bytes 24580
  216.1 97.9 %copy-start.35 = (bf16[1,2048,352]{1,2,0:T(8,128)(2,1)S(1)}, bf16[1,2048,352]{1,2,0:T(8,128)(2,1)}, u32[]{:S(2)}) copy-start(bf16[1,2048,352]{1,2,0:T(8,128)(2,1)} %param.49) | copy-start | bytes 4325380
  317.3 6.2 copy-start.32
  331.7 6.2 copy-start.11
  331.7 190.0 %all-to-all-start.1 = ((f32[8,256,2048]{2,1,0:T(8,128)}), f32[8,256,2048]{2,1,0:T(8,128)}, u32[]{:S(2)}, u32[]{:S(2)}) async-start(f32[8,256,2048]{2,1,0:T(8,128)} %fusion.48), calls=%async_computation.1 | async-start | bytes 33554432 | tf_op jit(solution)/shard_map/all_to_all | solution.py:252
  343.3 10.1 copy-start.7
  343.3 10.1 copy-start.43
  354.4 11.7 slice-start.3
  359.0 6.2 copy-start.63
  359.0 7.1 copy-start.12
  359.1 7.1 slice-start.4
  589.7 98.6 %copy-start.33 = (bf16[1,2048,352]{1,2,0:T(8,128)(2,1)S(1)}, bf16[1,2048,352]{1,2,0:T(8,128)(2,1)}, u32[]{:S(2)}) copy-start(bf16[1,2048,352]{1,2,0:T(8,128)(2,1)} %param.51) | copy-start | bytes 4325380
  589.7 98.6 %copy-start.65 = (f32[2048,352]{0,1:T(8,128)S(1)}, f32[2048,352]{0,1:T(8,128)}, u32[]{:S(2)}) copy-start(f32[2048,352]{0,1:T(8,128)} %copy-done.64) | copy-start | bytes 8650756
  589.7 98.6 %copy-start.66 = (f32[2048,352]{0,1:T(8,128)S(1)}, f32[2048,352]{0,1:T(8,128)}, u32[]{:S(2)}) copy-start(f32[2048,352]{0,1:T(8,128)} %get-tuple-element.660) | copy-start | bytes 8650756
  693.6 6.5 copy-start.23
  712.7 6.3 copy-start.52
  712.7 6.3 copy-start.8
  712.7 189.8 %all-to-all-start.3 = ((f32[8,256,2048]{2,1,0:T(8,128)}), f32[8,256,2048]{2,1,0:T(8,128)}, u32[]{:S(2)}, u32[]{:S(2)}) async-start(f32[8,256,2048]{2,1,0:T(8,128)} %bitcast.188), calls=%async_computation.3 | async-start | bytes 33554432 | tf_op jit(solution)/shard_map/all_to_all | solution.py:296
  718.6 317.6 %all-reduce.17.cloned.1.call-start = ((), (), s32[]{:S(2)}) async-start(), calls=%async_computation.19 | async-start | bytes 4194304 | tf_op jit(solution)/shard_map/psum | solution.py:306
  953.1 136.7 %all-reduce.15.cloned.1.call-start = ((), (), s32[]{:S(2)}) async-start(), calls=%async_computation.18 | async-start | bytes 2097152 | tf_op jit(solution)/shard_map/psum | solution.py:261
  974.6 61.6 %copy-start.44 = (bf16[2048,8]{0,1:T(8,128)(2,1)S(1)}, bf16[2048,8]{0,1:T(8,128)(2,1)}, u32[]{:S(2)}) copy-start(bf16[2048,8]{0,1:T(8,128)(2,1)} %param.44) | copy-start | bytes 98308
  974.6 61.6 %copy-start.48 = (f32[2048]{0:T(1024)S(1)}, f32[2048]{0:T(1024)}, u32[]{:S(2)}) copy-start(f32[2048]{0:T(1024)} %param.43) | copy-start | bytes 24580
  974.6 61.6 %copy-start.56 = (f32[256]{0:T(256)S(1)}, f32[256]{0:T(256)}, u32[]{:S(2)}) copy-start(f32[256]{0:T(256)} %copy-done.55) | copy-start | bytes 3076
  978.2 248.6 %reduce-scatter.19.cloned.1.call-start = ((), (), s32[]{:S(2)}) async-start(), calls=%async_computation.20 | async-start | bytes 9437184 | tf_op jit(solution)/shard_map/reduce_scatter | solution.py:328
  1155.9 160.0 %reduce-scatter.37.cloned.1.call-start = ((), (), s32[]{:S(2)}) async-start(), calls=%async_computation.30 | async-start | bytes 73728
  1160.5 71.8 %copy-start.40 = (f32[256,128]{1,0:T(8,128)S(1)}, f32[256,128]{1,0:T(8,128)}, u32[]{:S(2)}) copy-start(f32[256,128]{1,0:T(8,128)} %get-tuple-element.645) | copy-start | bytes 393220
  1236.6 80.8 %reduce-scatter.39.cloned.1.call-start = ((), (), s32[]{:S(2)}) async-start(), calls=%async_computation.31 | async-start | bytes 73728
  1241.1 101.6 %reduce-scatter.41.cloned.1.call-start = ((), (), s32[]{:S(2)}) async-start(), calls=%async_computation.32 | async-start | bytes 73728
  1246.2 185.6 %all-reduce.19.cloned.1.call-start = ((), (), s32[]{:S(2)}) async-start(), calls=%async_computation.21 | async-start | bytes 4194304 | tf_op jit(solution)/shard_map/psum | solution.py:344
  1250.8 216.6 %reduce-scatter.29.cloned.1.call-start = ((), (), s32[]{:S(2)}) async-start(), calls=%async_computation.26 | async-start | bytes 73728 | tf_op jit(solution)/shard_map/reduce_scatter | solution.py:376
  1251.7 307.0 %reduce-scatter.31.cloned.1.call-start = ((), (), s32[]{:S(2)}) async-start(), calls=%async_computation.27 | async-start | bytes 12976128 | tf_op jit(solution)/shard_map/reduce_scatter | solution.py:373
  1259.1 390.8 %reduce-scatter.33.cloned.1.call-start = ((), (), s32[]{:S(2)}) async-start(), calls=%async_computation.28 | async-start | bytes 12976128 | tf_op jit(solution)/shard_map/reduce_scatter | solution.py:374
  1266.3 474.8 %reduce-scatter.35.cloned.1.call-start = ((), (), s32[]{:S(2)}) async-start(), calls=%async_computation.29 | async-start | bytes 12976128 | tf_op jit(solution)/shard_map/reduce_scatter | solution.py:375
  1274.8 521.8 %reduce-scatter.27.cloned.1.call-start = ((), (), s32[]{:S(2)}) async-start(), calls=%async_computation.25 | async-start | bytes 4718592 | tf_op jit(solution)/shard_map/reduce_scatter | solution.py:368
  1280.0 571.7 %reduce-scatter.21.cloned.1.call-start = ((), (), s32[]{:S(2)}) async-start(), calls=%async_computation.22 | async-start | bytes 4718592 | tf_op jit(solution)/shard_map/reduce_scatter | solution.py:365
  1285.1 622.2 %reduce-scatter.23.cloned.1.call-start = ((), (), s32[]{:S(2)}) async-start(), calls=%async_computation.23 | async-start | bytes 4718592 | tf_op jit(solution)/shard_map/reduce_scatter | solution.py:366
  1288.0 674.4 %reduce-scatter.25.cloned.1.call-start = ((), (), s32[]{:S(2)}) async-start(), calls=%async_computation.24 | async-start | bytes 4718592 | tf_op jit(solution)/shard_map/reduce_scatter | solution.py:367
  1294.2 8.7 copy-start.22
  1294.2 17.0 slice-start
  1302.9 8.3 slice-start.1
  1302.9 8.3 copy-start.24
  (49 other events, 118.4 us)
Sparse Core Ops, SparseCore 0:
  34.0 39.3 all-gather.2
  107.5 86.4 all-reduce.12
  953.2 82.9 all-reduce.16
  1039.0 50.7 all-reduce.14
  1156.1 70.6 reduce-scatter.18
  1236.7 33.2 reduce-scatter.36
  1273.2 33.2 reduce-scatter.38
  1309.5 33.2 reduce-scatter.40
  1345.3 86.5 all-reduce.18
  1435.2 32.1 reduce-scatter.28
  1471.9 86.7 reduce-scatter.30
  1563.1 86.7 reduce-scatter.32
  1654.3 86.7 reduce-scatter.34
  1745.3 51.2 reduce-scatter.26
  1800.4 51.3 reduce-scatter.20
  1855.9 51.3 reduce-scatter.22
  1911.0 51.3 reduce-scatter.24
where the time goes:
time: 1980 us; the launch traced here: 1970 us
  waiting for transfers between devices  1210 us (61%)
  blocking collectives  240 us (12%)
  matrix products  228 us (12%)
  local copies, waits for them, and re-layouts  163 us (8%)
  other arithmetic  94.5 us (5%)
    all_to_all x1, waiting for transfers between devices, on_device(): lax.all_to_all(expert_in_grad.reshape(experts, route_cap, model_width), '...  170 us
    all_to_all x1, waiting for transfers between devices, on_device(): lax.all_to_all(expert_result, 'dp', split_axis=0, concat_axis=0, tiled=True)  152 us
    all_to_all x1, blocking collectives, on_device(): lax.all_to_all(send_grads, 'dp', split_axis=0, concat_axis=0, tiled=True)  98.6 us
    all_to_all x1, blocking collectives, on_device(): lax.all_to_all(send_rows, 'dp', split_axis=0, concat_axis=0, tiled=True)  97.9 us
    dot_general x23, matrix products, product_nt(): lax.dot_general(left, right, (((1,), (1,)), ((), ())), preferred_element_...  93.5 us
    reduce_scatter x1, waiting for transfers between devices, on_device(): lax.psum_scatter(grad_shared_gate_w, 'dp', scatter_dimension=0, tiled=True)  91.3 us
    reduce_scatter x1, waiting for transfers between devices, on_device(): lax.psum_scatter(grad_shared_down, 'dp', scatter_dimension=0, tiled=True)  91.3 us
    reduce_scatter x1, waiting for transfers between devices, on_device(): lax.psum_scatter(grad_shared_up, 'dp', scatter_dimension=0, tiled=True)  91.1 us
  transfers between devices with their start and end apart: 19, of which 17 were waited for; matrix products, arithmetic and copies ran while one was open for 9% of the time, Pallas kernels for 0%

commit v1 on v0

v1 whole, which is shorter than its diff:
```python
import jax
import jax.numpy as jnp
from jax import lax
from jax.sharding import PartitionSpec as P

HEAD_DIM = 128
SEG = 256


epsilon = 1e-06
rope_base = 1000000.0
highest = lax.Precision.HIGHEST


def product(left, right):
    return jnp.dot(left, right, preferred_element_type=jnp.float32)


def product_tn(left, right):
    return lax.dot_general(
        left, right, (((0,), (0,)), ((), ())), preferred_element_type=jnp.float32
    )


def product_nt(left, right):
    return lax.dot_general(
        left, right, (((1,), (1,)), ((), ())), preferred_element_type=jnp.float32
    )


def ancestry(parents):
    seg_count = parents.shape[0]
    labels = jnp.arange(seg_count, dtype=jnp.int32)

    def climb(level, carry):
        current, reach = carry
        upward = jnp.where(current >= 0, parents[jnp.maximum(current, 0)], -1)
        reach = jnp.maximum(reach, (upward[:, None] == labels[None, :]).astype(jnp.float32))
        return (upward, reach)

    start = (labels, jnp.eye(seg_count, dtype=jnp.float32))
    return lax.fori_loop(0, seg_count, climb, start)[1]


def rope_tables(positions):
    freqs = rope_base ** (-jnp.arange(0, HEAD_DIM, 2, dtype=jnp.float32) / HEAD_DIM)
    angles = positions[:, None] * freqs[None, :]
    angles = jnp.concatenate([angles, angles], 1)
    return (jnp.cos(angles)[:, None, :], jnp.sin(angles)[:, None, :])


def turn_heads(matrix, cosine, sine, sign_value):
    shaped = matrix.reshape(matrix.shape[0], matrix.shape[1] // HEAD_DIM, HEAD_DIM)
    half = HEAD_DIM // 2
    turned = jnp.concatenate([-shaped[..., half:], shaped[..., :half]], -1)
    return (shaped * cosine + sign_value * turned * sine).reshape(matrix.shape)


def norm_parts(values):
    scale_rows = lax.rsqrt(jnp.mean(values * values, 1, keepdims=True) + epsilon)
    return (scale_rows, values * scale_rows)


def norm_back(grad_rows, unit_rows, scale_rows, gain):
    unit_grad = grad_rows * gain
    return scale_rows * (unit_grad - unit_rows * jnp.mean(unit_grad * unit_rows, 1, keepdims=True))


LEVELS = 4


def gather_dp(rows):
    return lax.all_gather(rows, "dp", axis=0, tiled=True)


def gather_tensor(rows):
    return lax.all_gather(rows, "tensor", axis=0, tiled=True)


def gather_all(rows):
    return gather_dp(gather_tensor(rows))


def scatter_dp(rows):
    return lax.psum_scatter(rows, "dp", scatter_dimension=0, tiled=True)


def scatter_tensor(rows):
    return lax.psum_scatter(rows, "tensor", scatter_dimension=0, tiled=True)


def scatter_all(rows):
    return scatter_tensor(scatter_dp(rows))


def path_of(parents, segment):
    path = [segment]
    for _ in range(LEVELS - 1):
        last = path[-1]
        path.append(jnp.where(last >= 0, parents[jnp.maximum(last, 0)], -1))
    return jnp.stack(path)


def heads_of(matrix):
    return matrix.reshape(matrix.shape[0], -1, HEAD_DIM)


def attend_forward(query_rot, key_path, value_path, allowed, score_scale):
    scores = (
        jnp.einsum(
            "qhd,khd->hqk",
            heads_of(query_rot),
            heads_of(key_path),
            preferred_element_type=jnp.float32,
        )
        * score_scale
    )
    scores = jnp.where(allowed[None], scores, -jnp.inf)
    peak = jnp.max(scores, 2, keepdims=True)
    log_total = peak + jnp.log(jnp.sum(jnp.exp(scores - peak), 2, keepdims=True))
    weights = jnp.exp(scores - log_total).astype(jnp.bfloat16)
    attended = jnp.einsum(
        "hqk,khd->qhd", weights, heads_of(value_path), preferred_element_type=jnp.float32
    )
    return attended.reshape(query_rot.shape), log_total


def attend_backward(
    query_rot, key_path, value_path, allowed, log_total, attended_grad, score_scale
):
    query, key, value = heads_of(query_rot), heads_of(key_path), heads_of(value_path)
    grad = heads_of(attended_grad)
    scores = jnp.einsum("qhd,khd->hqk", query, key, preferred_element_type=jnp.float32)
    weights = jnp.exp(jnp.where(allowed[None], scores * score_scale, -jnp.inf) - log_total)
    weight_grad = jnp.einsum("qhd,khd->hqk", grad, value, preferred_element_type=jnp.float32)
    center = jnp.sum(weights * weight_grad, 2, keepdims=True)
    score_grad = (weights * (weight_grad - center)).astype(jnp.bfloat16)
    query_grad = (
        jnp.einsum("hqk,khd->qhd", score_grad, key, preferred_element_type=jnp.float32)
        * score_scale
    )
    key_grad = (
        jnp.einsum("hqk,qhd->khd", score_grad, query, preferred_element_type=jnp.float32)
        * score_scale
    )
    value_grad = jnp.einsum(
        "hqk,qhd->khd",
        weights.astype(jnp.bfloat16),
        grad,
        preferred_element_type=jnp.float32,
    )
    return (
        query_grad.reshape(query_rot.shape),
        key_grad.reshape(key_path.shape),
        value_grad.reshape(value_path.shape),
    )


def on_device(
    hidden_in,
    out_grad,
    parents,
    routes,
    attn_gain,
    w_query,
    w_key,
    w_value,
    b_query,
    b_key,
    b_value,
    w_out,
    ffn_gain,
    w_router,
    shared_gate,
    shared_w_gate,
    shared_w_up,
    shared_w_down,
    expert_w_gate,
    expert_w_up,
    expert_w_down,
):
    tok_rows, model_width = hidden_in.shape
    devices = lax.axis_size("dp")
    columns = lax.axis_size("tensor")
    place, column = lax.axis_index("dp"), lax.axis_index("tensor")
    all_rows = tok_rows * devices
    part_rows = tok_rows // columns
    local_width = w_query.shape[1]
    experts = w_router.shape[1]
    top_count = routes.shape[1]
    capacity = 5 * tok_rows * top_count // 4
    score_scale = HEAD_DIM ** (-0.5)
    bf16, f32 = jnp.bfloat16, jnp.float32

    expert_units = expert_w_gate.shape[2]
    shared_units = shared_w_gate.shape[1] // devices
    units = expert_units + shared_units
    units_pad = -(-(units + experts + 1) // 128) * 128

    def own_units(matrix):
        return lax.dynamic_slice_in_dim(matrix, place * shared_units, shared_units, 1)

    def pad_to(parts):
        joined = jnp.concatenate(parts, 1)
        return jnp.pad(joined, ((0, 0), (0, units_pad - joined.shape[1])))

    w_pre = jnp.concatenate(
        [
            pad_to([expert_w_gate[0], own_units(shared_w_gate), w_router, shared_gate[:, None]]),
            pad_to([expert_w_up[0], own_units(shared_w_up)]),
        ],
        1,
    )
    w_down = pad_to([expert_w_down[0], own_units(shared_w_down)])

    out_all = gather_dp(out_grad)

    routes_all = lax.all_gather(routes, "dp", axis=0, tiled=True)
    pair_onehot = routes_all[:, :, None] == jnp.arange(experts, dtype=jnp.int32)[None, None, :]
    hits = jnp.any(pair_onehot, 1)
    hit_blocks = hits.astype(bf16).reshape(devices, tok_rows, experts)
    below = (
        jnp.arange(tok_rows)[None, :] < jnp.arange(tok_rows)[:, None]
    ).astype(bf16)
    within = jnp.einsum("ij,bje->bie", below, hit_blocks, preferred_element_type=f32)
    block_sums = jnp.sum(hit_blocks.astype(f32), 1)
    before = jnp.cumsum(block_sums, 0) - block_sums
    slots = (within + before[:, None, :]).reshape(all_rows, experts)
    kept = (hits & (slots < capacity)).astype(f32)

    path = path_of(parents, place * tok_rows // SEG)
    reachable = path >= 0
    path_rows = jnp.maximum(path, 0)
    row_ids = jnp.arange(tok_rows, dtype=jnp.int32)
    depth = jnp.sum(reachable.astype(f32)) - 1.0
    cosine, sine = rope_tables(depth * SEG + row_ids.astype(f32))
    allowed = jnp.concatenate(
        [
            row_ids[:, None] >= row_ids[None, :],
            jnp.broadcast_to(
                jnp.repeat(reachable[1:], tok_rows)[None, :], (tok_rows, (LEVELS - 1) * tok_rows)
            ),
        ],
        1,
    )
    hidden_f = hidden_in.astype(f32)
    attn_scale, attn_unit = norm_parts(hidden_f)
    attn_normed = (attn_unit * attn_gain).astype(bf16)
    query_rot = turn_heads(
        product(attn_normed, w_query) + b_query.reshape(-1), cosine, sine, 1.0
    ).astype(bf16)
    key_rot = turn_heads(
        product(attn_normed, w_key) + b_key.reshape(-1), cosine, sine, 1.0
    ).astype(bf16)
    value_rows = (product(attn_normed, w_value) + b_value.reshape(-1)).astype(bf16)
    gathered = gather_dp(jnp.concatenate([key_rot, value_rows], 1))
    kv_blocks = gathered.reshape(devices, tok_rows, 2 * local_width)
    kv_path = jnp.take(kv_blocks, path_rows, axis=0).reshape(LEVELS * tok_rows, 2 * local_width)
    key_path, value_path = kv_path[:, :local_width], kv_path[:, local_width:]
    attended, log_total = attend_forward(query_rot, key_path, value_path, allowed, score_scale)
    attended_low = attended.astype(bf16)
    attn_part = scatter_tensor(product_nt(attended_low, w_out).astype(bf16))

    hidden_own = lax.dynamic_slice_in_dim(hidden_f, column * part_rows, part_rows, 0)
    out_own = lax.dynamic_slice_in_dim(out_grad, column * part_rows, part_rows, 0).astype(f32)
    residual = hidden_own + attn_part.astype(f32)
    ffn_scale, ffn_unit = norm_parts(residual)
    ffn_normed = (ffn_unit * ffn_gain).astype(bf16)
    normed_all = gather_all(ffn_normed)

    pre = product(normed_all, w_pre)
    pre_gate, pre_up = pre[:, :units_pad], pre[:, units_pad:]
    logits = pre[:, units : units + experts]
    probs = jax.nn.softmax(logits, 1)
    shared_weight = jax.nn.sigmoid(pre[:, units + experts])
    own_expert = jnp.arange(experts, dtype=jnp.int32)[None, :] == place
    gate_own = jnp.sum(jnp.where(own_expert, probs * kept, 0.0), 1)
    lane = jnp.arange(units_pad)[None, :]
    weight = jnp.where(
        lane < expert_units,
        gate_own[:, None],
        jnp.where(lane < units, shared_weight[:, None], 0.0),
    )
    down_back = product(out_all, w_down)
    sigmoid_gate = jax.nn.sigmoid(pre_gate)
    hidden = (pre_gate * sigmoid_gate * pre_up).astype(bf16).astype(f32)
    hidden_scaled = (hidden * weight).astype(bf16)
    hidden_grad = down_back * weight
    up_rows = (hidden_grad * pre_gate * sigmoid_gate).astype(bf16)
    gate_rows = (
        hidden_grad * pre_up * sigmoid_gate * (1.0 + pre_gate * (1.0 - sigmoid_gate))
    ).astype(bf16)
    both_rows = jnp.concatenate([gate_rows, up_rows], 1)
    dots = hidden * down_back
    gate_dot = jnp.sum(jnp.where(lane < expert_units, dots, 0.0), 1)
    shared_dot = jnp.sum(jnp.where((lane >= expert_units) & (lane < units), dots, 0.0), 1)
    dot_parts = jnp.concatenate(
        [jnp.where(own_expert, gate_dot[:, None] * kept, 0.0), shared_dot[:, None]], 1
    )
    ffn_part = product_nt(hidden_scaled, w_down).astype(bf16)
    normed_part = product_nt(both_rows, w_pre).astype(bf16)
    grad_pre = product_tn(normed_all, both_rows)
    grad_down = product_tn(out_all, hidden_scaled)

    dot_own = scatter_all(dot_parts)
    ffn_own = scatter_all(ffn_part).astype(f32)
    normed_own = scatter_all(normed_part).astype(f32)
    hidden_out = gather_tensor((residual + ffn_own).astype(bf16))

    first = (place * tok_rows) + column * part_rows
    own = lambda array: lax.dynamic_slice_in_dim(array, first, part_rows, 0)
    probs_own, shared_own = own(probs), own(shared_weight)
    prob_grad = dot_own[:, :experts]
    logit_grad = (
        probs_own * (prob_grad - jnp.sum(probs_own * prob_grad, 1, keepdims=True))
    ).astype(bf16)
    weight_logit_grad = (dot_own[:, experts] * shared_own * (1.0 - shared_own)).astype(bf16)
    side_grad = jnp.concatenate([logit_grad, weight_logit_grad[:, None]], 1)
    side_w = jnp.concatenate([w_router, shared_gate[:, None]], 1)
    normed_grad = normed_own + product_nt(side_grad, side_w)
    grad_side = product_tn(ffn_normed, side_grad)
    grad_ffn_gain = jnp.sum(normed_grad * ffn_unit, 0)
    residual_grad = out_own + norm_back(normed_grad, ffn_unit, ffn_scale, ffn_gain)
    residual_low = gather_tensor(residual_grad.astype(bf16))
    grad_out_proj = product_tn(residual_low, attended_low)
    attended_grad = product(residual_low, w_out).astype(bf16)

    query_grad, key_grad, value_grad = attend_backward(
        query_rot, key_path, value_path, allowed, log_total, attended_grad, score_scale
    )
    kv_grad = jnp.concatenate([key_grad, value_grad], 1).reshape(
        LEVELS, tok_rows, 2 * local_width
    )
    kv_all = jnp.zeros((devices, tok_rows, 2 * local_width), f32)
    for level in range(LEVELS):
        kv_all = kv_all.at[path_rows[level]].add(kv_grad[level])
    kv_own = scatter_dp(
        kv_all.reshape(all_rows, 2 * local_width).astype(bf16)
    ).astype(f32)
    query_pre_grad = turn_heads(query_grad, cosine, sine, -1.0).astype(bf16)
    key_pre_grad = turn_heads(kv_own[:, :local_width], cosine, sine, -1.0).astype(bf16)
    value_pre_grad = kv_own[:, local_width:].astype(bf16)
    qkv_pre_grad = jnp.concatenate([query_pre_grad, key_pre_grad, value_pre_grad], 1)
    grad_qkv = product_tn(attn_normed, qkv_pre_grad)
    bias_grads = jnp.sum(qkv_pre_grad.astype(f32), 0).reshape(3, -1, HEAD_DIM)
    attn_part_grad = (
        product_nt(query_pre_grad, w_query)
        + product_nt(key_pre_grad, w_key)
        + product_nt(value_pre_grad, w_value)
    )
    grad_attn_gain = jnp.sum(attn_part_grad * attn_unit, 0)
    attn_own_grad = scatter_tensor(attn_part_grad.astype(bf16)).astype(f32)
    own_rows = lambda array: lax.dynamic_slice_in_dim(
        array, column * part_rows, part_rows, 0
    )
    hidden_in_grad = gather_tensor(
        (
            residual_grad
            + norm_back(attn_own_grad, own_rows(attn_unit), own_rows(attn_scale), attn_gain)
        ).astype(bf16)
    )

    small = jnp.concatenate(
        [grad_side, grad_ffn_gain[:, None], grad_attn_gain[:, None]], 1
    )
    small = scatter_dp(lax.psum(small, "tensor"))
    bias_sums = lax.psum_scatter(bias_grads, "dp", scatter_dimension=2, tiled=True)
    grad_attn = scatter_dp(jnp.concatenate([grad_qkv, grad_out_proj], 1).astype(bf16)).astype(f32)
    shared_grads = jnp.stack(
        [
            grad_pre[:, expert_units:units],
            grad_pre[:, units_pad + expert_units : units_pad + units],
            grad_down[:, expert_units:units],
        ]
    ).astype(bf16)
    shared_grads = lax.all_to_all(
        shared_grads, "dp", split_axis=1, concat_axis=2, tiled=True
    ).astype(f32)
    return (
        hidden_out,
        hidden_in_grad,
        small[:, experts + 2],
        grad_attn[:, :local_width],
        grad_attn[:, local_width : 2 * local_width],
        grad_attn[:, 2 * local_width : 3 * local_width],
        bias_sums[0],
        bias_sums[1],
        bias_sums[2],
        grad_attn[:, 3 * local_width :],
        small[:, experts + 1],
        small[:, :experts],
        small[:, experts],
        shared_grads[0],
        shared_grads[1],
        shared_grads[2],
        grad_pre[None, :, :expert_units],
        grad_pre[None, :, units_pad : units_pad + expert_units],
        grad_down[None, :, :expert_units],
    )


def solution(mesh):
    return jax.shard_map(
        on_device,
        mesh=mesh,
        in_specs=(
            P("dp", None),
            P("dp", None),
            P(),
            P("dp", None),
            P(),
            P(None, "tensor"),
            P(None, "tensor"),
            P(None, "tensor"),
            P("tensor", None),
            P("tensor", None),
            P("tensor", None),
            P(None, "tensor"),
            P(),
            P(),
            P(),
            P(None, "tensor"),
            P(None, "tensor"),
            P(None, "tensor"),
            P("dp", None, "tensor"),
            P("dp", None, "tensor"),
            P("dp", None, "tensor"),
        ),
        out_specs=(
            P("dp", None),
            P("dp", None),
            P("dp"),
            P("dp", "tensor"),
            P("dp", "tensor"),
            P("dp", "tensor"),
            P("tensor", "dp"),
            P("tensor", "dp"),
            P("tensor", "dp"),
            P("dp", "tensor"),
            P("dp"),
            P("dp", None),
            P("dp"),
            P("dp", "tensor"),
            P("dp", "tensor"),
            P("dp", "tensor"),
            P("dp", None, "tensor"),
            P("dp", None, "tensor"),
            P("dp", None, "tensor"),
        ),
        check_vma=False,
    )
```

time: 1980 us -> 932 us (0.47)
  waiting for transfers between devices: 1210 us -> 519 us
  blocking collectives: 240 us -> 26.7 us
  matrix products: 228 us -> 137 us
  local copies, waits for them, and re-layouts: 163 us -> 132 us
  other arithmetic: 94.5 us -> 73.7 us
    all_to_all x2 -> x1, waiting for transfers between devices: 322 us -> 39.6 us  [on_device(): lax.all_to_all(shared_grads, 'dp', split_axis=1, concat_axis=2, tiled=True)]
    psum x4 -> x0, waiting for transfers between devices: 275 us -> none  [the longest x1 87.7 us: on_device(): attn_normed_grad = lax.psum(attn_part, 'tensor')]
    reduce_scatter x9 -> x10, waiting for transfers between devices: 565 us -> 319 us  [the longest x6 227 us: scatter_dp(): return lax.psum_scatter(rows, 'dp', scatter_dimension=0, tiled=True)]
    all_to_all x2 -> x0, blocking collectives: 197 us -> none  [the longest x1 98.6 us: on_device(): lax.all_to_all(send_grads, 'dp', split_axis=0, concat_axis=0, tiled=True)]
    all_gather x1 -> x7, waiting for transfers between devices: 27.2 us -> 137 us  [the longest x3 94.3 us: gather_dp(): return lax.all_gather(rows, 'dp', axis=0, tiled=True)]
    gather x12 -> x2, local copies, waits for them, and re-layouts: 64.7 us -> 8.12 us  [on_device(): jnp.take(kv_blocks, path_rows, axis=0)]
    dot_general x23 -> x7, matrix products: 93.5 us -> 39.5 us  [product_nt(): lax.dot_general(left, right, (((1,), (1,)), ((), ())), preferred_element_...]
    dot_general x20 -> x5, matrix products: 76.5 us -> 35.6 us  [product_tn(): lax.dot_general(left, right, (((0,), (0,)), ((), ())), preferred_element_...]
  transfers between devices with their start and end apart: 19 -> 20, of which waited for: 17 -> 16; matrix products, arithmetic and copies ran while one was open for 9% -> 24% of each run, Pallas kernels for 0% -> 0%
where the time goes in v1:
time: 932 us; the launch traced here: 920 us
  waiting for transfers between devices  519 us (56%)
  matrix products  137 us (15%)
  local copies, waits for them, and re-layouts  132 us (14%)
  other arithmetic  73.7 us (8%)
  blocking collectives  26.7 us (3%)
  between operations  25.3 us (3%)
    reduce_scatter x6, waiting for transfers between devices, scatter_dp(): return lax.psum_scatter(rows, 'dp', scatter_dimension=0, tiled=True)  227 us
    all_gather x3, waiting for transfers between devices, gather_dp(): return lax.all_gather(rows, 'dp', axis=0, tiled=True)  94.3 us
    reduce_scatter x4, waiting for transfers between devices, scatter_tensor(): return lax.psum_scatter(rows, 'tensor', scatter_dimension=0, tiled=True)  91 us
    unnamed x130, local copies, waits for them, and re-layouts  50.3 us
    dot_general x6, matrix products, product(): return jnp.dot(left, right, preferred_element_type=jnp.float32)  44.4 us
    all_gather x4, waiting for transfers between devices, gather_tensor(): return lax.all_gather(rows, 'tensor', axis=0, tiled=True)  42.7 us
    all_to_all x1, waiting for transfers between devices, on_device(): lax.all_to_all(shared_grads, 'dp', split_axis=1, concat_axis=2, tiled=True)  39.6 us
    dot_general x7, matrix products, product_nt(): lax.dot_general(left, right, (((1,), (1,)), ((), ())), preferred_element_...  39.5 us
  transfers between devices with their start and end apart: 20, of which 16 were waited for; matrix products, arithmetic and copies ran while one was open for 24% of the time, Pallas kernels for 0%

profile of v1, /device:TPU:0, one launch (start us, length us, event | category | flops | bytes accessed | tf_op | source)
XLA Modules:
  0.0 920.0 jit_solution(11083305014770489819)
XLA Ops:
  17.9 3.5 convolution_add_fusion.5
  23.4 3.1 convolution_add_fusion.3
  37.6 38.2 %all-gather.8.cloned.1.call-done = bf16[2048,1024]{1,0:T(8,128)(2,1)} async-done(((bf16[256,1024]{1,0:T(8,128)(2,1)}), bf16[2048,1024]{1,0:T(8,128)(2,1)}) %all-gather.8.cloned.1.call-update) | async-done | bytes 4194320 | tf_op jit(solution)/shard_map/all_gather | solution.py:73
  75.8 4.2 gather_fusion
  80.0 3.9 copy.213
  94.6 25.7 %reduce-scatter.17.cloned.1.call-done = bf16[64,2048]{1,0:T(8,128)(2,1)} async-done(((bf16[256,2048]{1,0:T(8,128)(2,1)}), bf16[64,2048]{1,0:T(8,128)(2,1)}) %reduce-scatter.17.cloned.1.call-update) | async-done | bytes 262160 | tf_op jit(solution)/shard_map/reduce_scatter | solution.py:89
  123.2 26.7 %all-gather.10.cloned.1.call-done = bf16[256,2048]{1,0:T(8,128)(2,1)} async-done(((bf16[64,2048]{1,0:T(8,128)(2,1)}), bf16[256,2048]{1,0:T(8,128)(2,1)}) %all-gather.10.cloned.1.call-update) | async-done | bytes 1048592 | tf_op jit(solution)/shard_map/all_gather | solution.py:77
  150.6 4.3 constant_dynamic-slice_fusion.3
  159.9 9.6 %all_gather.27 = s32[2048,4]{0,1:T(4,128)S(1)} all-gather(s32[256,4]{0,1:T(4,128)S(1)} %copy-done.44), channel_id=1, replica_groups=mesh['dp'=8,'tensor'=4] {'dp'}, dimensions={0}, use_global_device_ids=true | all-gather | bytes 36864 | tf_op jit(solution)/shard_map/all_gather | solution.py:218
  181.0 3.5 fusion.15
  186.1 19.7 %all-gather.12.cloned.1.call-done = bf16[2048,2048]{1,0:T(8,128)(2,1)} async-done(((bf16[256,2048]{1,0:T(8,128)(2,1)}), bf16[2048,2048]{1,0:T(8,128)(2,1)}) %all-gather.12.cloned.1.call-update) | async-done | bytes 8388624 | tf_op jit(solution)/shard_map/all_gather | solution.py:73
  205.8 15.2 %fusion.10 = f32[2048,1280]{0,1:T(8,128)S(1)} fusion(bf16[2048,2048]{1,0:T(8,128)(2,1)} %all-gather.12.cloned.1.call-done, bf16[2048,640]{0,1:T(8,128)(2,1)} %fusion.15, bf16[2048,640]{0,1:T(8,128)(2,1)} %fusion.14), kind=kOutput, calls=%fused_computation.41 | convolution fusion | flops 10747904000 | bytes 24117248 | tf_op jit(solution)/shard_map/dot_general | solution.py:16
  225.7 36.4 %all-gather.16.cloned.1.call-done = bf16[2048,2048]{1,0:T(8,128)(2,1)} async-done(((bf16[256,2048]{1,0:T(8,128)(2,1)}), bf16[2048,2048]{1,0:T(8,128)(2,1)}) %all-gather.16.cloned.1.call-update) | async-done | bytes 8388624 | tf_op jit(solution)/shard_map/all_gather | solution.py:73
  262.1 17.6 %multiply_convert_fusion.1 = (bf16[2048,640]{0,1:T(8,128)(2,1)}, bf16[2048,640]{0,1:T(8,128)(2,1)}, f32[2048]{0:T(1024)}, f32[2048]{0:T(1024)}, bf16[2048,640]{0,1:T(8,128)(2,1)}) fusion(f32[2048,1280]{0,1:T(8,128)} %copy-done.45, f32[2048]{0:T(1024)} %bitcast.213, f32[2048]{0:T(1024)} %get-tuple-element.192, pred[640]{0:T(1024)(128)(4,1)} %get-tuple-element.267, ...), kind=kOutput, calls=%fused_computation.30 | convolution fusion | flops 5410648064 | bytes 28936064 | tf_op jit(solution)/shard_map/dot_general | solution.py:16
  282.2 16.9 %convolution_convert_fusion.1 = bf16[2048,2048]{1,0:T(8,128)(2,1)} fusion(bf16[2048,640]{0,1:T(8,128)(2,1)} %get-tuple-element.197, bf16[2048,640]{0,1:T(8,128)(2,1)} %get-tuple-element.196, bf16[2048,640]{0,1:T(8,128)(2,1)} %fusion.15, bf16[2048,640]{0,1:T(8,128)(2,1)} %fusion.14), kind=kOutput, calls=%fused_computation.3 | convolution fusion | flops 10762584064 | bytes 18874368 | tf_op jit(solution)/shard_map/dot_general | solution.py:26
  299.2 16.3 %reduce-scatter.27.cloned.1.call-done = f32[256,9]{0,1:T(8,128)} async-done(((f32[2048,9]{0,1:T(8,128)}), f32[256,9]{0,1:T(8,128)}) %reduce-scatter.27.cloned.1.call-update) | async-done | bytes 9232 | tf_op jit(solution)/shard_map/reduce_scatter | solution.py:85
  317.0 73.2 %reduce-scatter.23.cloned.1.call-done = bf16[256,2048]{1,0:T(8,128)(2,1)} async-done(((bf16[2048,2048]{1,0:T(8,128)(2,1)}), bf16[256,2048]{1,0:T(8,128)(2,1)}) %reduce-scatter.23.cloned.1.call-update) | async-done | bytes 1048592 | tf_op jit(solution)/shard_map/reduce_scatter | solution.py:85
  390.3 22.0 %reduce-scatter.37.cloned.1.call-done = f32[64,9]{1,0:T(8,128)} async-done(((f32[256,9]{1,0:T(8,128)}), f32[64,9]{1,0:T(8,128)}) %reduce-scatter.37.cloned.1.call-update) | async-done | bytes 2320
  420.0 20.0 %reduce-scatter.25.cloned.1.call-done = bf16[64,2048]{1,0:T(8,128)(2,1)} async-done(((bf16[256,2048]{1,0:T(8,128)(2,1)}), bf16[64,2048]{1,0:T(8,128)(2,1)}) %reduce-scatter.25.cloned.1.call-update) | async-done | bytes 262160 | tf_op jit(solution)/shard_map/reduce_scatter | solution.py:89
  455.7 16.0 %all-gather.18.cloned.1.call-done = bf16[256,2048]{1,0:T(8,128)(2,1)} async-done(((bf16[64,2048]{1,0:T(8,128)(2,1)}), bf16[256,2048]{1,0:T(8,128)(2,1)}) %all-gather.18.cloned.1.call-update) | async-done | bytes 1048592 | tf_op jit(solution)/shard_map/all_gather | solution.py:77
  471.7 3.3 convolution_convert_fusion.5
  476.8 5.0 fusion.71
  481.9 3.6 multiply_reduce_fusion
  485.5 2.9 copy.195
  488.4 4.1 multiply_convert_fusion.3
  507.6 12.0 %convolution_convert_fusion.2 = bf16[2048,2048]{1,0:T(8,128)(2,1)} fusion(bf16[2048,176]{0,1:T(8,128)(2,1)} %copy.223, bf16[2048,352]{0,1:T(8,128)(2,1)} %bitcast.224, bf16[2048,640]{0,1:T(8,128)(2,1)} %get-tuple-element.200, f32[2048]{0:T(1024)S(1)} %bitcast.214, f32[2048]{0:T(1024)S(1)} %copy-done.40, pred[640]{0:T(1024)(128)(4,1)S(1)} %copy-done.48, ...), kind=kOutput, calls=%fused_computation.4 | convolution fusion | flops 5388632064 | bytes 13190400 | tf_op jit(solution)/shard_map/dot_general | solution.py:26
  520.0 3.6 broadcast_multiply_fusion.1
  524.4 33.5 %reduce-scatter.29.cloned.1.call-done = bf16[256,1024]{1,0:T(8,128)(2,1)} async-done(((bf16[2048,1024]{1,0:T(8,128)(2,1)}), bf16[256,1024]{1,0:T(8,128)(2,1)}) %reduce-scatter.29.cloned.1.call-update) | async-done | bytes 524304 | tf_op jit(solution)/shard_map/reduce_scatter | solution.py:85
  568.7 3.0 fusion.86
  572.9 3.1 multiply_reduce_fusion.1
  576.0 56.5 %reduce-scatter.19.cloned.1.call-done = bf16[256,2048]{1,0:T(8,128)(2,1)} async-done(((bf16[2048,2048]{1,0:T(8,128)(2,1)}), bf16[256,2048]{1,0:T(8,128)(2,1)}) %reduce-scatter.19.cloned.1.call-update) | async-done | bytes 1048592 | tf_op jit(solution)/shard_map/reduce_scatter | solution.py:85
  644.0 18.7 %reduce-scatter.31.cloned.1.call-done = bf16[64,2048]{1,0:T(8,128)(2,1)} async-done(((bf16[256,2048]{1,0:T(8,128)(2,1)}), bf16[64,2048]{1,0:T(8,128)(2,1)}) %reduce-scatter.31.cloned.1.call-update) | async-done | bytes 262160 | tf_op jit(solution)/shard_map/reduce_scatter | solution.py:89
  663.9 26.7 %reduce-scatter.21.cloned.1.call-done = bf16[64,2048]{1,0:T(8,128)(2,1)} async-done(((bf16[256,2048]{1,0:T(8,128)(2,1)}), bf16[64,2048]{1,0:T(8,128)(2,1)}) %reduce-scatter.21.cloned.1.call-update) | async-done | bytes 262160 | tf_op jit(solution)/shard_map/reduce_scatter | solution.py:89
  693.9 3.3 convolution_convert_fusion.3
  697.3 5.6 convolution_convert_fusion
  702.9 8.4 pad_maximum_fusion
  711.3 17.4 %fusion.85 = (bf16[2048,1280]{0,1:T(8,128)(2,1)S(1)}, f32[2048,1280]{0,1:T(8,128)}) fusion(bf16[2048,2048]{1,0:T(8,128)(2,1)} %all-gather.12.cloned.1.call-done, bf16[2048,640]{0,1:T(8,128)(2,1)} %get-tuple-element.197, bf16[2048,640]{0,1:T(8,128)(2,1)} %get-tuple-element.196), kind=kOutput, calls=%fused_computation.220 | convolution fusion | flops 10750525440 | bytes 29360128 | tf_op jit(solution)/shard_map/dot_general | solution.py:20
  728.9 8.2 convolution_bitcast_fusion
  741.0 6.9 copy.199
  747.9 4.7 all-to-all-start
  752.6 3.7 slice_bitcast_fusion
  756.4 6.0 slice_bitcast_fusion.1
  762.3 39.6 %all-to-all-done = bf16[3,2048,176]{2,0,1:T(4,128)(2,1)} async-done(((bf16[3,2048,176]{2,0,1:T(4,128)(2,1)}), bf16[3,2048,176]{2,0,1:T(4,128)(2,1)}, u32[]{:S(2)}, u32[]{:S(2)}) %all-to-all-start) | async-done | bytes 2162720 | tf_op jit(solution)/shard_map/all_to_all | solution.py:376
  802.0 7.0 copy.200
  819.6 3.0 copy.202
  825.4 3.0 copy.203
  834.1 17.1 %psum.8 = f32[256,11]{0,1:T(8,128)S(1)} all-reduce(f32[256,11]{0,1:T(8,128)} %reduce-scatter.35.cloned.1.call-done), channel_id=1, replica_groups=mesh['dp'=8,'tensor'=4] {'tensor'}, use_global_device_ids=true, to_apply=%region_32.33 | all-reduce | flops 2816 | bytes 22528 | tf_op jit(solution)/shard_map/psum | solution.py:366
  852.3 48.0 %reduce-scatter.33.cloned.1.call-done = bf16[256,2048]{0,1:T(8,128)(2,1)} async-done(((bf16[2048,2048]{0,1:T(8,128)(2,1)}), bf16[256,2048]{0,1:T(8,128)(2,1)}) %reduce-scatter.33.cloned.1.call-update) | async-done | bytes 1048592 | tf_op jit(solution)/shard_map/reduce_scatter | solution.py:85
  (278 shorter events, 160.8 us)
Async XLA Ops:
  7.2 24.7 %copy-start = (bf16[2048,512]{1,0:T(8,128)(2,1)S(1)}, bf16[2048,512]{1,0:T(8,128)(2,1)}, u32[]{:S(2)}) copy-start(bf16[2048,512]{1,0:T(8,128)(2,1)} %param.36) | copy-start | bytes 6291460
  7.2 16.2 %copy-start.5 = (bf16[256,2048]{1,0:T(8,128)(2,1)S(1)}, bf16[256,2048]{1,0:T(8,128)(2,1)}, u32[]{:S(2)}) copy-start(bf16[256,2048]{1,0:T(8,128)(2,1)} %param.29) | copy-start | bytes 3145732
  7.2 16.2 %copy-start.25 = (f32[2048]{0:T(1024)S(1)}, f32[2048]{0:T(1024)}, u32[]{:S(2)}) copy-start(f32[2048]{0:T(1024)} %param.33) | copy-start | bytes 24580
  7.2 68.6 %all-gather.8.cloned.1.call-start = ((), (), s32[]{:S(2)}) async-start(), calls=%async_computation.13 | async-start | bytes 4718592 | tf_op jit(solution)/shard_map/all_gather | solution.py:73
  16.3 7.1 copy-start.52
  17.9 14.0 %copy-start.35 = (f32[256]{0:T(256)}, f32[256]{0:T(256)S(1)}, u32[]{:S(2)}) copy-start(f32[256]{0:T(256)S(1)} %add_rsqrt_fusion) | copy-start | bytes 3076
  36.2 84.0 %reduce-scatter.17.cloned.1.call-start = ((), (), s32[]{:S(2)}) async-start(), calls=%async_computation.14 | async-start | bytes 1310720 | tf_op jit(solution)/shard_map/reduce_scatter | solution.py:89
  91.2 31.2 %copy-start.27 = (f32[2048]{0:T(1024)S(1)}, f32[2048]{0:T(1024)}, u32[]{:S(2)}) copy-start(f32[2048]{0:T(1024)} %param.41) | copy-start | bytes 24580
  92.9 57.0 %all-gather.10.cloned.1.call-start = ((), (), s32[]{:S(2)}) async-start(), calls=%async_computation.15 | async-start | bytes 1310720 | tf_op jit(solution)/shard_map/all_gather | solution.py:77
  123.2 33.9 %copy-start.43 = (bf16[2048]{0:T(1024)(128)(2,1)S(1)}, bf16[2048]{0:T(1024)(128)(2,1)}, u32[]{:S(2)}) copy-start(bf16[2048]{0:T(1024)(128)(2,1)} %param.43) | copy-start | bytes 12292
  123.2 82.6 %all-gather.12.cloned.1.call-start = ((), (), s32[]{:S(2)}) async-start(), calls=%async_computation.16 | async-start | bytes 9437184 | tf_op jit(solution)/shard_map/all_gather | solution.py:73
  149.9 9.9 %copy-start.44 = (s32[256,4]{0,1:T(4,128)S(1)}, s32[256,4]{0,1:T(4,128)}, u32[]{:S(2)}) copy-start(s32[256,4]{0,1:T(4,128)} %param.32) | copy-start | bytes 12292
  150.0 112.2 %all-gather.16.cloned.1.call-start = ((), (), s32[]{:S(2)}) async-start(), calls=%async_computation.20 | async-start | bytes 9437184 | tf_op jit(solution)/shard_map/all_gather | solution.py:73
  150.5 164.9 %reduce-scatter.27.cloned.1.call-start = ((), (), s32[]{:S(2)}) async-start(), calls=%async_computation.23 | async-start | bytes 147456 | tf_op jit(solution)/shard_map/reduce_scatter | solution.py:85
  177.8 6.7 copy-start.13
  177.8 6.7 copy-start.23
  177.8 6.7 copy-start.29
  177.8 6.7 copy-start.30
  205.8 15.3 %copy-start.34 = (pred[8,8,256]{2,1,0:T(8,128)(4,1)S(1)}, pred[8,8,256]{2,1,0:T(8,128)(4,1)}, u32[]{:S(2)}) copy-start(pred[8,8,256]{2,1,0:T(8,128)(4,1)} %fusion.19) | copy-start | bytes 49156
  205.8 15.3 %copy-start.46 = (pred[8]{0:T(512)(128)(4,1)S(1)}, pred[8]{0:T(512)(128)(4,1)}, u32[]{:S(2)}) copy-start(pred[8]{0:T(512)(128)(4,1)} %iota_compare_fusion.8) | copy-start | bytes 28
  282.0 108.3 %reduce-scatter.23.cloned.1.call-start = ((), (), s32[]{:S(2)}) async-start(), calls=%async_computation.21 | async-start | bytes 9437184 | tf_op jit(solution)/shard_map/reduce_scatter | solution.py:85
  299.1 141.0 %copy-start.28 = (f32[2048]{0:T(1024)S(1)}, f32[2048]{0:T(1024)}, u32[]{:S(2)}) copy-start(f32[2048]{0:T(1024)} %param.41) | copy-start | bytes 24580
  299.1 141.0 %copy-start.31 = (bf16[2048,1]{0,1:T(2,128)(2,1)S(1)}, bf16[2048,1]{0,1:T(2,128)(2,1)}, u32[]{:S(2)}) copy-start(bf16[2048,1]{0,1:T(2,128)(2,1)} %broadcast_in_dim.181) | copy-start | bytes 12292
  299.1 113.3 %reduce-scatter.37.cloned.1.call-start = ((), (), s32[]{:S(2)}) async-start(), calls=%async_computation.30 | async-start | bytes 163840
  317.0 123.1 %reduce-scatter.25.cloned.1.call-start = ((), (), s32[]{:S(2)}) async-start(), calls=%async_computation.22 | async-start | bytes 1310720 | tf_op jit(solution)/shard_map/reduce_scatter | solution.py:89
  390.3 81.4 %all-gather.18.cloned.1.call-start = ((), (), s32[]{:S(2)}) async-start(), calls=%async_computation.24 | async-start | bytes 1310720 | tf_op jit(solution)/shard_map/all_gather | solution.py:77
  442.1 34.7 %copy-start.33 = (f32[4,256]{1,0:T(4,128)S(1)}, f32[4,256]{1,0:T(4,128)}, u32[]{:S(2)}) copy-start(f32[4,256]{1,0:T(4,128)} %copy-done.32) | copy-start | bytes 12292
  442.1 34.7 %copy-start.47 = (f32[64]{0:T(128)}, f32[64]{0:T(128)S(1)}, u32[]{:S(2)}) copy-start(f32[64]{0:T(128)S(1)} %broadcast_multiply_fusion.6) | copy-start | bytes 772
  445.0 112.9 %reduce-scatter.29.cloned.1.call-start = ((), (), s32[]{:S(2)}) async-start(), calls=%async_computation.25 | async-start | bytes 4718592 | tf_op jit(solution)/shard_map/reduce_scatter | solution.py:85
  476.8 5.0 copy-start.12
  476.8 5.0 copy-start.17
  488.4 5.5 copy-start.16
  506.9 125.6 %reduce-scatter.19.cloned.1.call-start = ((), (), s32[]{:S(2)}) async-start(), calls=%async_computation.17 | async-start | bytes 9437184 | tf_op jit(solution)/shard_map/reduce_scatter | solution.py:85
  519.5 143.1 %reduce-scatter.31.cloned.1.call-start = ((), (), s32[]{:S(2)}) async-start(), calls=%async_computation.26 | async-start | bytes 1310720 | tf_op jit(solution)/shard_map/reduce_scatter | solution.py:89
  576.0 86.7 %copy-start.26 = (f32[2048]{0:T(1024)S(1)}, f32[2048]{0:T(1024)}, u32[]{:S(2)}) copy-start(f32[2048]{0:T(1024)} %param.33) | copy-start | bytes 24580
  576.0 114.6 %reduce-scatter.21.cloned.1.call-start = ((), (), s32[]{:S(2)}) async-start(), calls=%async_computation.18 | async-start | bytes 1310720 | tf_op jit(solution)/shard_map/reduce_scatter | solution.py:89
  632.5 198.8 %reduce-scatter.39.cloned.1.call-start = ((), (), s32[]{:S(2)}) async-start(), calls=%async_computation.31 | async-start | bytes 73728
  642.5 191.6 %reduce-scatter.35.cloned.1.call-start = ((), (), s32[]{:S(2)}) async-start(), calls=%async_computation.29 | async-start | bytes 147456 | tf_op jit(solution)/shard_map/reduce_scatter | solution.py:85
  643.9 53.4 %copy-start.37 = (f32[256]{0:T(256)S(1)}, f32[256]{0:T(256)}, u32[]{:S(2)}) copy-start(f32[256]{0:T(256)} %copy-done.35) | copy-start | bytes 3076
  643.9 208.4 %all-gather.14.cloned.1.call-start = ((), (), s32[]{:S(2)}) async-start(), calls=%async_computation.19 | async-start | bytes 1310720 | tf_op jit(solution)/shard_map/all_gather | solution.py:77
  693.3 159.0 %all-gather.20.cloned.1.call-start = ((), (), s32[]{:S(2)}) async-start(), calls=%async_computation.27 | async-start | bytes 1310720 | tf_op jit(solution)/shard_map/all_gather | solution.py:77
  693.9 206.4 %reduce-scatter.33.cloned.1.call-start = ((), (), s32[]{:S(2)}) async-start(), calls=%async_computation.28 | async-start | bytes 9437184 | tf_op jit(solution)/shard_map/reduce_scatter | solution.py:85
  711.3 17.6 %copy-start.39 = (f32[2048,1]{0,1:T(1,128)S(1)}, f32[2048,1]{0,1:T(1,128)}, u32[]{:S(2)}) copy-start(f32[2048,1]{0,1:T(1,128)} %fusion.54) | copy-start | bytes 24580
  711.3 17.6 %copy-start.41 = (f32[2048]{0:T(1024)S(1)}, f32[2048]{0:T(1024)}, u32[]{:S(2)}) copy-start(f32[2048]{0:T(1024)} %get-tuple-element.192) | copy-start | bytes 24580
  711.3 17.6 %copy-start.49 = (pred[640]{0:T(1024)(128)(4,1)S(1)}, pred[640]{0:T(1024)(128)(4,1)}, u32[]{:S(2)}) copy-start(pred[640]{0:T(1024)(128)(4,1)} %get-tuple-element.267) | copy-start | bytes 1924
  711.3 17.6 %copy-start.51 = (pred[640]{0:T(1024)(128)(4,1)S(1)}, pred[640]{0:T(1024)(128)(4,1)}, u32[]{:S(2)}) copy-start(pred[640]{0:T(1024)(128)(4,1)} %get-tuple-element.268) | copy-start | bytes 1924
  711.3 17.6 %copy-start.53 = (bf16[2048,640]{0,1:T(8,128)(2,1)S(1)}, bf16[2048,640]{0,1:T(8,128)(2,1)}, u32[]{:S(2)}) copy-start(bf16[2048,640]{0,1:T(8,128)(2,1)} %get-tuple-element.200) | copy-start | bytes 7864324
  747.9 54.0 %all-to-all-start = ((bf16[3,2048,176]{2,0,1:T(4,128)(2,1)}), bf16[3,2048,176]{2,0,1:T(4,128)(2,1)}, u32[]{:S(2)}, u32[]{:S(2)}) async-start(bf16[3,2048,176]{2,0,1:T(4,128)(2,1)} %copy.199), calls=%async_computation.9 | async-start | bytes 8388608 | tf_op jit(solution)/shard_map/all_to_all | solution.py:376
  (26 other events, 49.3 us)
Sparse Core Ops, SparseCore 0:
  36.3 39.4 all-gather.7
  93.1 27.1 reduce-scatter.16
  123.3 26.5 all-gather.9
  151.8 53.9 all-gather.11
  207.7 54.3 all-gather.15
  282.1 33.3 reduce-scatter.26
  318.9 71.2 reduce-scatter.22
  393.2 19.1 reduce-scatter.36
  414.7 25.3 reduce-scatter.24
  445.1 26.5 all-gather.17
  507.0 50.8 reduce-scatter.28
  561.2 71.2 reduce-scatter.18
  635.5 27.0 reduce-scatter.30
  664.8 25.7 reduce-scatter.20
  693.7 31.8 reduce-scatter.38
  728.5 33.5 reduce-scatter.34
  764.1 31.9 all-gather.13
  798.2 27.4 all-gather.19
  829.5 70.7 reduce-scatter.32

commit v2 on v1

--- a/solution.py
+++ b/solution.py
@@ -1,10 +1,15 @@
+import functools
+
 import jax
 import jax.numpy as jnp
 from jax import lax
+from jax.experimental import pallas as pl
+from jax.experimental.pallas import tpu as pltpu
 from jax.sharding import PartitionSpec as P
 
 HEAD_DIM = 128
 SEG = 256
+MESH = pl.DeviceIdType.MESH
 
 
 epsilon = 1e-06
@@ -154,6 +159,633 @@
         key_grad.reshape(key_path.shape),
         value_grad.reshape(value_path.shape),
     )
+
+
+def ffn_plain(attn_part, hidden_own, grad_own, ffn_gain, kept, out_all, w_pre, w_down, layout):
+    shared_pad, expert_units, experts, units_pad = layout
+    units = shared_pad + expert_units
+    bf16, f32 = jnp.bfloat16, jnp.float32
+    place, column = lax.axis_index("dp"), lax.axis_index("tensor")
+    columns, part_rows = lax.axis_size("tensor"), hidden_own.shape[0]
+    out_own = grad_own.astype(f32)
+    residual = hidden_own.astype(f32) + scatter_tensor(attn_part).astype(f32)
+    ffn_scale, ffn_unit = norm_parts(residual)
+    ffn_normed = (ffn_unit * ffn_gain).astype(bf16)
+    normed_all = gather_all(ffn_normed)
+
+    pre = product(normed_all, w_pre)
+    pre_gate, pre_up = pre[:, :units_pad], pre[:, units_pad:]
+    logits = pre[:, units : units + experts]
+    probs = jax.nn.softmax(logits, 1)
+    shared_weight = jax.nn.sigmoid(pre[:, units + experts])
+    own_expert = jnp.arange(experts, dtype=jnp.int32)[None, :] == place
+    gate_own = jnp.sum(jnp.where(own_expert, probs * kept, 0.0), 1)
+    lane = jnp.arange(units_pad)[None, :]
+    weight = jnp.where(
+        lane < shared_pad,
+        shared_weight[:, None],
+        jnp.where(lane < units, gate_own[:, None], 0.0),
+    )
+    down_back = product(out_all, w_down)
+    sigmoid_gate = jax.nn.sigmoid(pre_gate)
+    hidden = (pre_gate * sigmoid_gate * pre_up).astype(bf16).astype(f32)
+    hidden_scaled = (hidden * weight).astype(bf16)
+    hidden_grad = down_back * weight
+    up_rows = (hidden_grad * pre_gate * sigmoid_gate).astype(bf16)
+    gate_rows = (
+        hidden_grad * pre_up * sigmoid_gate * (1.0 + pre_gate * (1.0 - sigmoid_gate))
+    ).astype(bf16)
+    both_rows = jnp.concatenate([gate_rows, up_rows], 1)
+    dots = hidden * down_back
+    gate_dot = jnp.sum(jnp.where((lane >= shared_pad) & (lane < units), dots, 0.0), 1)
+    shared_dot = jnp.sum(jnp.where(lane < shared_pad, dots, 0.0), 1)
+    dot_parts = jnp.concatenate(
+        [jnp.where(own_expert, gate_dot[:, None] * kept, 0.0), shared_dot[:, None]], 1
+    )
+    ffn_part = product_nt(hidden_scaled, w_down).astype(bf16)
+    normed_part = product_nt(both_rows, w_pre).astype(bf16)
+    grad_pre = product_tn(normed_all, both_rows)
+    grad_down = product_tn(out_all, hidden_scaled)
+
+    dot_own = scatter_all(dot_parts)
+    normed_own = scatter_all(normed_part).astype(f32)
+
+    first = (place * columns + column) * part_rows
+    own = lambda array: lax.dynamic_slice_in_dim(array, first, part_rows, 0)
+    probs_own, shared_own = own(probs), own(shared_weight)
+    prob_grad = dot_own[:, :experts]
+    logit_grad = (
+        probs_own * (prob_grad - jnp.sum(probs_own * prob_grad, 1, keepdims=True))
+    ).astype(bf16)
+    weight_logit_grad = (dot_own[:, experts] * shared_own * (1.0 - shared_own)).astype(bf16)
+    side_grad = jnp.concatenate([logit_grad, weight_logit_grad[:, None]], 1)
+    side_w = w_pre[:, units : units + experts + 1]
+    normed_grad = normed_own + product_nt(side_grad, side_w)
+    grad_side = product_tn(ffn_normed, side_grad)
+    grad_ffn_gain = jnp.sum(normed_grad * ffn_unit, 0)
+    residual_grad = out_own + norm_back(normed_grad, ffn_unit, ffn_scale, ffn_gain)
+    expert = slice(shared_pad, units)
+    expert_up = slice(units_pad + shared_pad, units_pad + units)
+    grad_shared = jnp.stack(
+        [
+            grad_pre[:, : shared_pad],
+            grad_pre[:, units_pad : units_pad + shared_pad],
+            grad_down[:, : shared_pad],
+        ]
+    ).astype(bf16)
+    return (
+        residual,
+        residual_grad,
+        residual_grad.astype(bf16),
+        ffn_part,
+        grad_pre[:, expert],
+        grad_pre[:, expert_up],
+        grad_down[:, expert],
+        grad_shared,
+        grad_side,
+        grad_ffn_gain,
+    )
+
+
+def flip(bit):
+    return 1 - bit
+
+
+def other(index, step):
+    result, place = index, 1
+    while place <= step:
+        if step & place:
+            result = result + place - 2 * place * ((index // place) % 2)
+        place *= 2
+    return result
+
+
+def ffn_kernel(
+    units,
+    part_ref,
+    hidden_ref,
+    grad_ref,
+    gain_ref,
+    kept_ref,
+    grad_all_ref,
+    w_pre_ref,
+    w_down_ref,
+    residual_ref,
+    res_grad_ref,
+    res_low_ref,
+    ffn_part_ref,
+    e_gate_ref,
+    e_up_ref,
+    e_down_ref,
+    shared_ref,
+    side_ref,
+    gain_grad_ref,
+    rows_all,
+    dy_all,
+    w_pre,
+    w_down,
+    both_all,
+    scaled_all,
+    sums,
+    got_core,
+    got_x1,
+    got_y1,
+    got_y2,
+    got_x2,
+    got_z,
+    attn_z,
+    ffn_chunk,
+    tile_gate,
+    tile_up,
+    tile_down,
+    tile_shared,
+    load_sems,
+    store_sems,
+    tile_sems,
+    attn_sems,
+    zs,
+    links,
+    cores,
+    rs_core,
+    rs_links,
+    rs_z,
+):
+    shared_pad, expert_units, experts, unit_pad, half, wide = units
+    bf16, f32 = jnp.bfloat16, jnp.float32
+    place, column = lax.axis_index("dp"), lax.axis_index("tensor")
+    core, east, north = place % 2, (place // 2) % 2, place // 4
+    rows, width = hidden_ref.shape
+    sibling = {"dp": other(place, 1)}
+    x_side = {"dp": other(place, 2)}
+    y_side = {"dp": other(place, 4)}
+    levels = [{"tensor": other(column, k)} for k in range(4)]
+
+    def level_of(k):
+        low_i, high_i, low_k, high_k = column % 2, column // 2, k % 2, k // 2
+        return (low_i + low_k - 2 * low_i * low_k) + 2 * (high_i + high_k - 2 * high_i * high_k)
+
+    def remote(src, dst, sems, which, device):
+        return pltpu.make_async_remote_copy(
+            src_ref=src,
+            dst_ref=dst,
+            send_sem=sems.at[(0, *which)],
+            recv_sem=sems.at[(1, *which)],
+            device_id=device,
+            device_id_type=MESH,
+        )
+
+    load_pre = pltpu.make_async_copy(w_pre_ref, w_pre, load_sems.at[0])
+    load_down = pltpu.make_async_copy(w_down_ref, w_down, load_sems.at[1])
+    load_pre.start()
+    load_down.start()
+
+    def load_grad(c, z):
+        return pltpu.make_async_copy(
+            grad_all_ref.at[:, :, c, z], dy_all.at[z, c], load_sems.at[2 + c * 4 + z]
+        )
+
+    for c in range(2):
+        for z in range(4):
+            load_grad(c, z).start()
+
+    barrier = pltpu.get_barrier_semaphore()
+    partners = [sibling, x_side, y_side] + levels[1:]
+    for partner in partners:
+        pl.semaphore_signal(barrier, inc=1, device_id=partner, device_id_type=MESH)
+    pl.semaphore_wait(barrier, len(partners))
+
+    attn_copies = []
+    for k in (3, 2, 1):
+        copy = remote(
+            part_ref.at[other(column, k)], attn_z.at[k], attn_sems, (k,), levels[k]
+        )
+        copy.start()
+        attn_copies.append(copy)
+    own_part = pltpu.make_async_copy(part_ref.at[column], attn_z.at[0], load_sems.at[10])
+    own_part.start()
+    own_part.wait()
+    for copy in attn_copies:
+        copy.wait()
+    attn = attn_z[0].astype(f32)
+    for k in range(1, 4):
+        attn = attn + attn_z[k].astype(f32)
+    residual = hidden_ref[...].astype(f32) + attn
+    residual_ref[...] = residual
+    scale_rows = lax.rsqrt(jnp.mean(residual * residual, 1, keepdims=True) + epsilon)
+    normed = (residual * scale_rows * gain_ref[...]).astype(bf16)
+    rows_all[column, core, north, east] = normed
+
+    own_slot = rows_all.at[column, core, north, east]
+
+    def z_copy(k):
+        return remote(own_slot, own_slot, zs, (k,), levels[k])
+
+    def block(k, c, y, x, cols=slice(None)):
+        return rows_all.at[level_of(k), c, y, x, :, cols]
+
+    first_half, second_half = pl.ds(0, half), pl.ds(half, width - half)
+
+    def direct_copies(k):
+        own = block(k, core, north, east)
+        return [
+            remote(own, own, links, (0, k), x_side),
+            remote(own, own, links, (1, k), y_side),
+            remote(own, own, cores, (0, k), sibling),
+        ]
+
+    def forward_copies(k):
+        from_x = block(k, core, north, flip(east), first_half)
+        from_y = block(k, core, flip(north), east, second_half)
+        all_x = block(k, core, north, flip(east))
+        all_y = block(k, core, flip(north), east)
+        return [
+            remote(from_x, from_x, links, (2, k), y_side),
+            remote(from_y, from_y, links, (3, k), x_side),
+            remote(all_x, all_x, cores, (1, k), sibling),
+            remote(all_y, all_y, cores, (2, k), sibling),
+        ]
+
+    def corner_copy(k):
+        corner = block(k, core, flip(north), flip(east))
+        return remote(corner, corner, cores, (3, k), sibling)
+
+    def start_direct(k):
+        for copy in direct_copies(k):
+            copy.start()
+
+    def start_forward(k):
+        for copy in direct_copies(k)[:2]:
+            copy.wait_recv()
+        for copy in forward_copies(k):
+            copy.start()
+
+    def start_corner(k):
+        for copy in forward_copies(k)[:2]:
+            copy.wait_recv()
+        corner_copy(k).start()
+
+    def finish_gather(k):
+        direct_copies(k)[2].wait_recv()
+        for copy in forward_copies(k)[2:]:
+            copy.wait_recv()
+        corner_copy(k).wait_recv()
+
+    def core_copy(k):
+        return remote(sums.at[k, flip(core)], got_core.at[k], rs_core, (k,), sibling)
+
+    left, right = pl.ds(0, half), pl.ds(half, wide - half)
+
+    def first_copies(k):
+        return [
+            remote(
+                sums.at[k, core, :, flip(east), :, left],
+                got_x1.at[k],
+                rs_links, (0, k),
+                x_side,
+            ),
+            remote(
+                sums.at[k, core, flip(north), :, :, right],
+                got_y1.at[k],
+                rs_links, (1, k),
+                y_side,
+            ),
+        ]
+
+    def second_copies(k):
+        return [
+            remote(
+                sums.at[k, core, flip(north), east, :, left],
+                got_y2.at[k],
+                rs_links, (2, k),
+                y_side,
+            ),
+            remote(
+                sums.at[k, core, north, flip(east), :, right],
+                got_x2.at[k],
+                rs_links, (3, k),
+                x_side,
+            ),
+        ]
+
+    def level_copy(k, device):
+        return remote(sums.at[k, core, north, east], got_z.at[k], rs_z, (k,), device)
+
+    def add(ref, value):
+        ref[...] = (ref[...].astype(f32) + value.astype(f32)).astype(bf16)
+
+    def after_core(k):
+        core_copy(k).wait_recv()
+        for y in range(2):
+            for x in range(2):
+                add(sums.at[k, core, y, x], got_core[k, y, x])
+        for copy in first_copies(k):
+            copy.start()
+
+    def after_first(k):
+        x_copy, y_copy = first_copies(k)
+        x_copy.wait_recv()
+        for y in range(2):
+            add(sums.at[k, core, y, east, :, left], got_x1[k, y])
+        y_copy.wait_recv()
+        for x in range(2):
+            add(sums.at[k, core, north, x, :, right], got_y1[k, x])
+        for copy in second_copies(k):
+            copy.start()
+
+    def after_second(k):
+        y_copy, x_copy = second_copies(k)
+        y_copy.wait_recv()
+        add(sums.at[k, core, north, east, :, left], got_y2[k])
+        x_copy.wait_recv()
+        add(sums.at[k, core, north, east, :, right], got_x2[k])
+        for level in range(1, 4):
+
+            @pl.when(k == level)
+            def _():
+                level_copy(k, levels[level]).start()
+
+    for k in (1, 2, 3):
+        z_copy(k).start()
+    start_direct(0)
+    load_pre.wait()
+    load_down.wait()
+    for c in range(2):
+        for z in range(4):
+            load_grad(c, z).wait()
+    start_forward(0)
+    z_copy(1).wait_recv()
+    start_direct(1)
+    start_corner(0)
+
+    last = unit_pad - 128
+    lane = lax.broadcasted_iota(jnp.int32, (1, 128), 1)
+    first_lane = shared_pad + expert_units - last
+    in_router = (lane >= first_lane) & (lane < first_lane + experts)
+    is_shared = lane == first_lane + experts
+
+    def routing(logit_block):
+        top = jnp.max(jnp.where(in_router, logit_block, -jnp.inf), 1, keepdims=True)
+        powers = jnp.where(in_router, jnp.exp(jnp.where(in_router, logit_block - top, 0.0)), 0.0)
+        probs = powers / jnp.sum(powers, 1, keepdims=True)
+        shared_logit = jnp.sum(jnp.where(is_shared, logit_block, 0.0), 1, keepdims=True)
+        return probs, jax.nn.sigmoid(shared_logit)
+
+    def compute(k, c):
+        z = level_of(k)
+        row_block = rows_all[z, c].reshape(4 * rows, width)
+        dy_block = dy_all[z, c].reshape(4 * rows, width)
+        pre_gate = product(row_block, w_pre[:, :unit_pad])
+        pre_up = product(row_block, w_pre[:, unit_pad:])
+        down_back = product(dy_block, w_down[...])
+        probs, shared_weight = routing(pre_gate[:, last:])
+        kept = kept_ref[z, c]
+        gate = (
+            jnp.sum(jnp.where(lane == first_lane + place, probs, 0.0), 1, keepdims=True) * kept
+        )
+        dots = []
+        for begin, end, weight in (
+            (0, shared_pad, shared_weight),
+            (shared_pad, unit_pad, gate),
+        ):
+            cols = slice(begin, end)
+            a, b, back = pre_gate[:, cols], pre_up[:, cols], down_back[:, cols]
+            sig = jax.nn.sigmoid(a)
+            silu = a * sig
+            hidden = (silu * b).astype(bf16).astype(f32)
+            dots.append(jnp.sum(hidden * back, 1, keepdims=True))
+            scaled_all[z, c, :, begin:end] = (hidden * weight).astype(bf16)
+            grad = back * weight
+            both_all[z, c, :, unit_pad + begin : unit_pad + end] = (grad * silu).astype(bf16)
+            both_all[z, c, :, begin:end] = (
+                grad * b * sig * (1.0 + a * (1.0 - sig))
+            ).astype(bf16)
+        dot_block = jnp.where(is_shared, dots[0], 0.0) + jnp.where(
+            lane == first_lane + place, dots[1] * kept, 0.0
+        )
+        normed_grad = product_nt(both_all[z, c], w_pre[...]).astype(bf16)
+        sums[k, c, :, :, :, 0:width] = normed_grad.reshape(2, 2, rows, width)
+        sums[k, c, :, :, :, width:wide] = dot_block.astype(bf16).reshape(2, 2, rows, wide - width)
+
+    def store_chunk(k, c):
+        return pltpu.make_async_copy(
+            ffn_chunk, ffn_part_ref.at[level_of(k), c], store_sems.at[c]
+        )
+
+    def chunk(k, carry):
+        @pl.when(k < 3)
+        def _():
+            start_forward(k + 1)
+
+        @pl.when(k < 2)
+        def _():
+            for level in (2, 3):
+
+                @pl.when(k + 2 == level)
+                def _():
+                    z_copy(level).wait_recv()
+
+            start_direct(k + 2)
+
+        finish_gather(k)
+        def rows_of(i, carry):
+            compute(k, (i + 1 + core) % 2)
+
+            @pl.when(i == 0)
+            def _():
+                core_copy(k).start()
+
+            return carry
+
+        lax.fori_loop(0, 2, rows_of, 0)
+
+        @pl.when(k >= 1)
+        def _():
+            after_first(k - 1)
+            store_chunk(k - 1, 1).wait()
+
+        def outputs(c, carry):
+            part = product_nt(scaled_all[level_of(k), c], w_down[...]).astype(bf16)
+
+            @pl.when(c == 1)
+            def _():
+                store_chunk(k, 0).wait()
+
+            ffn_chunk[...] = part.reshape(2, 2, rows, width)
+            store_chunk(k, c).start()
+            return carry
+
+        lax.fori_loop(0, 2, outputs, 0)
+
+        @pl.when(k < 3)
+        def _():
+            start_corner(k + 1)
+
+        after_core(k)
+
+        @pl.when(k >= 1)
+        def _():
+            after_second(k - 1)
+
+        return carry
+
+    lax.fori_loop(0, 4, chunk, 0)
+    store_chunk(3, 1).wait()
+
+    tile = tile_gate.shape[1]
+    tiles = width // tile
+
+    def tile_copies(i, slot):
+        window = pl.ds(pl.multiple_of(i * tile, tile), tile)
+        return [
+            pltpu.make_async_copy(tile_gate.at[slot], e_gate_ref.at[window], tile_sems.at[slot, 0]),
+            pltpu.make_async_copy(tile_up.at[slot], e_up_ref.at[window], tile_sems.at[slot, 1]),
+            pltpu.make_async_copy(tile_down.at[slot], e_down_ref.at[window], tile_sems.at[slot, 2]),
+            pltpu.make_async_copy(
+                tile_shared.at[slot], shared_ref.at[:, window], tile_sems.at[slot, 3]
+            ),
+        ]
+
+    tokens = rows * 32
+
+    def weight_tile(i, carry):
+        slot = i % 2
+
+        @pl.when(i >= 2)
+        def _():
+            for copy in tile_copies(i - 2, slot):
+                copy.wait()
+
+        window = pl.ds(pl.multiple_of(i * tile, tile), tile)
+        expert = slice(shared_pad, shared_pad + expert_units)
+        lhs = rows_all[:, :, :, :, :, window].reshape(tokens, tile)
+        grad = product_tn(lhs, both_all[...].reshape(tokens, 2 * unit_pad))
+        tile_gate[slot] = grad[:, expert]
+        tile_shared[slot, 0] = grad[:, :shared_pad].astype(bf16)
+        tile_up[slot] = grad[:, unit_pad + shared_pad : unit_pad + shared_pad + expert_units]
+        tile_shared[slot, 1] = grad[:, unit_pad : unit_pad + shared_pad].astype(bf16)
+        lhs = dy_all[:, :, :, :, :, window].reshape(tokens, tile)
+        grad = product_tn(lhs, scaled_all[...].reshape(tokens, unit_pad))
+        tile_down[slot] = grad[:, expert]
+        tile_shared[slot, 2] = grad[:, :shared_pad].astype(bf16)
+        for copy in tile_copies(i, slot):
+            copy.start()
+
+        @pl.when(i == 1)
+        def _():
+            after_first(3)
+
+        @pl.when(i == 3)
+        def _():
+            after_second(3)
+
+        return carry
+
+    lax.fori_loop(0, tiles, weight_tile, 0)
+    for i in (tiles - 2, tiles - 1):
+        for copy in tile_copies(i, i % 2):
+            copy.wait()
+
+    total = sums[0, core, north, east].astype(f32)
+    for k in (1, 2, 3):
+        level_copy(k, levels[k]).wait_recv()
+        total = total + got_z[k].astype(f32)
+    dots = total[:, width:]
+    unit = residual_ref[...] * scale_rows
+    own_normed = rows_all[column, core, north, east]
+    side_w = w_pre[:, last:unit_pad]
+    probs, shared_weight = routing(product(own_normed, side_w))
+    router_dots = jnp.where(in_router, dots, 0.0)
+    center = jnp.sum(probs * router_dots, 1, keepdims=True)
+    side = jnp.where(in_router, probs * (router_dots - center), 0.0) + jnp.where(
+        is_shared, dots * shared_weight * (1.0 - shared_weight), 0.0
+    )
+    side = side.astype(bf16)
+    normed_grad = total[:, :width] + product_nt(side, side_w)
+    side_ref[...] = product_tn(own_normed, side)
+    gain_grad_ref[...] = jnp.sum(normed_grad * unit, 0, keepdims=True)
+    grad_f = grad_ref[...].astype(f32) + norm_back(normed_grad, unit, scale_rows, gain_ref[...])
+    res_grad_ref[...] = grad_f
+    res_low_ref[...] = grad_f.astype(bf16)
+
+    for k in (1, 2, 3):
+        z_copy(k).wait_send()
+        level_copy(k, levels[k]).wait_send()
+    for k in range(4):
+        for copy in direct_copies(k) + forward_copies(k) + [corner_copy(k), core_copy(k)]:
+            copy.wait_send()
+        for copy in first_copies(k) + second_copies(k):
+            copy.wait_send()
+
+
+def ffn_layer(
+    attn_part, hidden_own, grad_own, ffn_gain, kept, grad_all, w_pre, w_down, layout
+):
+    shared_pad, expert_units, experts, unit_pad = layout
+    rows, width = hidden_own.shape
+    bf16, f32 = jnp.bfloat16, jnp.float32
+    half = width // 2
+    wide = width + 128
+    tile = 256
+    shape = jax.ShapeDtypeStruct
+    vmem, anywhere = pl.BlockSpec(memory_space=pltpu.VMEM), pl.BlockSpec(memory_space=pl.ANY)
+    dma = pltpu.SemaphoreType.DMA
+    cost = pl.CostEstimate(
+        flops=2 * 24 * 2048 * 2048 * 256, bytes_accessed=60 * 2**20, transcendentals=3 * 2**20
+    )
+    return pl.pallas_call(
+        functools.partial(
+            ffn_kernel, (shared_pad, expert_units, experts, unit_pad, half, wide)
+        ),
+        out_shape=[
+            shape((rows, width), f32),
+            shape((rows, width), f32),
+            shape((rows, width), bf16),
+            shape((4, 2, 2, 2, rows, width), bf16),
+            shape((width, expert_units), f32),
+            shape((width, expert_units), f32),
+            shape((width, expert_units), f32),
+            shape((3, width, shared_pad), bf16),
+            shape((width, 128), f32),
+            shape((1, width), f32),
+        ],
+        in_specs=[anywhere, vmem, vmem, vmem, vmem, anywhere, anywhere, anywhere],
+        out_specs=[vmem, vmem, vmem] + [anywhere] * 5 + [vmem, vmem],
+        scratch_shapes=[
+            pltpu.VMEM((4, 2, 2, 2, rows, width), bf16),
+            pltpu.VMEM((4, 2, 2, 2, rows, width), bf16),
+            pltpu.VMEM(w_pre.shape, bf16),
+            pltpu.VMEM(w_down.shape, bf16),
+            pltpu.VMEM((4, 2, 4 * rows, 2 * unit_pad), bf16),
+            pltpu.VMEM((4, 2, 4 * rows, unit_pad), bf16),
+            pltpu.VMEM((4, 2, 2, 2, rows, wide), bf16),
+            pltpu.VMEM((4, 2, 2, rows, wide), bf16),
+            pltpu.VMEM((4, 2, rows, half), bf16),
+            pltpu.VMEM((4, 2, rows, wide - half), bf16),
+            pltpu.VMEM((4, rows, half), bf16),
+            pltpu.VMEM((4, rows, wide - half), bf16),
+            pltpu.VMEM((4, rows, wide), bf16),
+            pltpu.VMEM((4, rows, width), bf16),
+            pltpu.VMEM((2, 2, rows, width), bf16),
+            pltpu.VMEM((2, tile, expert_units), f32),
+            pltpu.VMEM((2, tile, expert_units), f32),
+            pltpu.VMEM((2, tile, expert_units), f32),
+            pltpu.VMEM((2, 3, tile, shared_pad), bf16),
+            dma((11,)),
+            dma((2,)),
+            dma((2, 4)),
+            dma((2, 4)),
+            dma((2, 4)),
+            dma((2, 4, 4)),
+            dma((2, 4, 4)),
+            dma((2, 4)),
+            dma((2, 4, 4)),
+            dma((2, 4)),
+        ],
+        compiler_params=pltpu.CompilerParams(
+            collective_id=0, has_side_effects=True, vmem_limit_bytes=63 * 2**20
+        ),
+        cost_estimate=cost,
+    )(attn_part, hidden_own, grad_own, ffn_gain, kept, grad_all, w_pre, w_down)
 
 
 def on_device(
@@ -194,24 +826,33 @@
 
     expert_units = expert_w_gate.shape[2]
     shared_units = shared_w_gate.shape[1] // devices
-    units = expert_units + shared_units
+    shared_pad = -(-shared_units // 128) * 128
+    units = shared_pad + expert_units
     units_pad = -(-(units + experts + 1) // 128) * 128
 
     def own_units(matrix):
         return lax.dynamic_slice_in_dim(matrix, place * shared_units, shared_units, 1)
 
-    def pad_to(parts):
-        joined = jnp.concatenate(parts, 1)
-        return jnp.pad(joined, ((0, 0), (0, units_pad - joined.shape[1])))
+    def pad_to(matrix, columns):
+        return jnp.pad(matrix, ((0, 0), (0, columns - matrix.shape[1])))
+
+    def side_by_side(shared, expert):
+        joined = jnp.concatenate([pad_to(own_units(shared), shared_pad), expert[0]], 1)
+        return joined
 
     w_pre = jnp.concatenate(
         [
-            pad_to([expert_w_gate[0], own_units(shared_w_gate), w_router, shared_gate[:, None]]),
-            pad_to([expert_w_up[0], own_units(shared_w_up)]),
+            pad_to(
+                jnp.concatenate(
+                    [side_by_side(shared_w_gate, expert_w_gate), w_router, shared_gate[:, None]], 1
+                ),
+                units_pad,
+            ),
+            pad_to(side_by_side(shared_w_up, expert_w_up), units_pad),
         ],
         1,
     )
-    w_down = pad_to([expert_w_down[0], own_units(shared_w_down)])
+    w_down = pad_to(side_by_side(shared_w_down, expert_w_down), units_pad)
 
     out_all = gather_dp(out_grad)
 
@@ -259,69 +900,61 @@
     key_path, value_path = kv_path[:, :local_width], kv_path[:, local_width:]
     attended, log_total = attend_forward(query_rot, key_path, value_path, allowed, score_scale)
     attended_low = attended.astype(bf16)
-    attn_part = scatter_tensor(product_nt(attended_low, w_out).astype(bf16))
-
-    hidden_own = lax.dynamic_slice_in_dim(hidden_f, column * part_rows, part_rows, 0)
-    out_own = lax.dynamic_slice_in_dim(out_grad, column * part_rows, part_rows, 0).astype(f32)
-    residual = hidden_own + attn_part.astype(f32)
-    ffn_scale, ffn_unit = norm_parts(residual)
-    ffn_normed = (ffn_unit * ffn_gain).astype(bf16)
-    normed_all = gather_all(ffn_normed)
-
-    pre = product(normed_all, w_pre)
-    pre_gate, pre_up = pre[:, :units_pad], pre[:, units_pad:]
-    logits = pre[:, units : units + experts]
-    probs = jax.nn.softmax(logits, 1)
-    shared_weight = jax.nn.sigmoid(pre[:, units + experts])
-    own_expert = jnp.arange(experts, dtype=jnp.int32)[None, :] == place
-    gate_own = jnp.sum(jnp.where(own_expert, probs * kept, 0.0), 1)
-    lane = jnp.arange(units_pad)[None, :]
-    weight = jnp.where(
-        lane < expert_units,
-        gate_own[:, None],
-        jnp.where(lane < units, shared_weight[:, None], 0.0),
-    )
-    down_back = product(out_all, w_down)
-    sigmoid_gate = jax.nn.sigmoid(pre_gate)
-    hidden = (pre_gate * sigmoid_gate * pre_up).astype(bf16).astype(f32)
-    hidden_scaled = (hidden * weight).astype(bf16)
-    hidden_grad = down_back * weight
-    up_rows = (hidden_grad * pre_gate * sigmoid_gate).astype(bf16)
-    gate_rows = (
-        hidden_grad * pre_up * sigmoid_gate * (1.0 + pre_gate * (1.0 - sigmoid_gate))
-    ).astype(bf16)
-    both_rows = jnp.concatenate([gate_rows, up_rows], 1)
-    dots = hidden * down_back
-    gate_dot = jnp.sum(jnp.where(lane < expert_units, dots, 0.0), 1)
-    shared_dot = jnp.sum(jnp.where((lane >= expert_units) & (lane < units), dots, 0.0), 1)
-    dot_parts = jnp.concatenate(
-        [jnp.where(own_expert, gate_dot[:, None] * kept, 0.0), shared_dot[:, None]], 1
-    )
-    ffn_part = product_nt(hidden_scaled, w_down).astype(bf16)
-    normed_part = product_nt(both_rows, w_pre).astype(bf16)
-    grad_pre = product_tn(normed_all, both_rows)
-    grad_down = product_tn(out_all, hidden_scaled)
-
-    dot_own = scatter_all(dot_parts)
+    attn_part = product_nt(attended_low, w_out).astype(bf16)
+
+    hidden_own = lax.dynamic_slice_in_dim(hidden_in, column * part_rows, part_rows, 0)
+    grad_own = lax.dynamic_slice_in_dim(out_grad, column * part_rows, part_rows, 0)
+    layout = (shared_pad, expert_units, experts, units_pad)
+    cube = devices == 8 and columns == 4
+    if cube and all_rows * model_width <= 2**22:
+        kept_own = jnp.sum(jnp.where(jnp.arange(experts)[None, :] == place, kept, 0.0), 1)
+        kept_own = kept_own.reshape(2, 2, 2, columns, part_rows).transpose(3, 2, 0, 1, 4)
+        (
+            residual,
+            residual_grad,
+            residual_low,
+            ffn_part,
+            grad_expert_gate,
+            grad_expert_up,
+            grad_expert_down,
+            grad_shared,
+            grad_side,
+            grad_ffn_gain,
+        ) = ffn_layer(
+            attn_part.reshape(columns, part_rows, model_width),
+            hidden_own,
+            grad_own,
+            ffn_gain[None, :],
+            kept_own.reshape(columns, 2, 4 * part_rows, 1),
+            out_all.reshape(2, 2, 2, columns, part_rows, model_width),
+            w_pre,
+            w_down,
+            layout,
+        )
+        ffn_part = ffn_part.transpose(2, 3, 1, 0, 4, 5).reshape(all_rows, model_width)
+        grad_ffn_gain = grad_ffn_gain[0]
+        side_first = units - (units_pad - 128)
+        grad_side = grad_side[:, side_first : side_first + experts + 1]
+        grad_shared = grad_shared[:, :, :shared_units]
+    else:
+        (
+            residual,
+            residual_grad,
+            residual_low,
+            ffn_part,
+            grad_expert_gate,
+            grad_expert_up,
+            grad_expert_down,
+            grad_shared,
+            grad_side,
+            grad_ffn_gain,
+        ) = ffn_plain(
+            attn_part, hidden_own, grad_own, ffn_gain, kept, out_all, w_pre, w_down, layout
+        )
+        grad_shared = grad_shared[:, :, :shared_units]
     ffn_own = scatter_all(ffn_part).astype(f32)
-    normed_own = scatter_all(normed_part).astype(f32)
     hidden_out = gather_tensor((residual + ffn_own).astype(bf16))
-
-    first = (place * tok_rows) + column * part_rows
-    own = lambda array: lax.dynamic_slice_in_dim(array, first, part_rows, 0)
-    probs_own, shared_own = own(probs), own(shared_weight)
-    prob_grad = dot_own[:, :experts]
-    logit_grad = (
-        probs_own * (prob_grad - jnp.sum(probs_own * prob_grad, 1, keepdims=True))
-    ).astype(bf16)
-    weight_logit_grad = (dot_own[:, experts] * shared_own * (1.0 - shared_own)).astype(bf16)
-    side_grad = jnp.concatenate([logit_grad, weight_logit_grad[:, None]], 1)
-    side_w = jnp.concatenate([w_router, shared_gate[:, None]], 1)
-    normed_grad = normed_own + product_nt(side_grad, side_w)
-    grad_side = product_tn(ffn_normed, side_grad)
-    grad_ffn_gain = jnp.sum(normed_grad * ffn_unit, 0)
-    residual_grad = out_own + norm_back(normed_grad, ffn_unit, ffn_scale, ffn_gain)
-    residual_low = gather_tensor(residual_grad.astype(bf16))
+    residual_low = gather_tensor(residual_low)
     grad_out_proj = product_tn(residual_low, attended_low)
     attended_grad = product(residual_low, w_out).astype(bf16)
 
@@ -366,15 +999,8 @@
     small = scatter_dp(lax.psum(small, "tensor"))
     bias_sums = lax.psum_scatter(bias_grads, "dp", scatter_dimension=2, tiled=True)
     grad_attn = scatter_dp(jnp.concatenate([grad_qkv, grad_out_proj], 1).astype(bf16)).astype(f32)
-    shared_grads = jnp.stack(
-        [
-            grad_pre[:, expert_units:units],
-            grad_pre[:, units_pad + expert_units : units_pad + units],
-            grad_down[:, expert_units:units],
-        ]
-    ).astype(bf16)
     shared_grads = lax.all_to_all(
-        shared_grads, "dp", split_axis=1, concat_axis=2, tiled=True
+        grad_shared, "dp", split_axis=1, concat_axis=2, tiled=True
     ).astype(f32)
     return (
         hidden_out,
@@ -393,9 +1019,9 @@
         shared_grads[0],
         shared_grads[1],
         shared_grads[2],
-        grad_pre[None, :, :expert_units],
-        grad_pre[None, :, units_pad : units_pad + expert_units],
-        grad_down[None, :, :expert_units],
+        grad_expert_gate[None],
+        grad_expert_up[None],
+        grad_expert_down[None],
     )
 
 

time: 932 us -> 737 us (0.79)
  waiting for transfers between devices: 519 us -> 329 us
  Pallas kernels: 0 us -> 132 us
  matrix products: 137 us -> 38.8 us
  other arithmetic: 73.7 us -> 42.1 us
    pallas_call x0 -> x1, Pallas kernels: none -> 132 us  [ffn_layer(): pl.pallas_call(functools.partial(ffn_kernel, (shared_pad, expert_units, e...]
    all_gather x3 -> x2, waiting for transfers between devices: 94.3 us -> 41.9 us  [gather_dp(): return lax.all_gather(rows, 'dp', axis=0, tiled=True)]
    reduce_scatter x6 -> x4, waiting for transfers between devices: 227 us -> 177 us  [scatter_dp(): return lax.psum_scatter(rows, 'dp', scatter_dimension=0, tiled=True)]
    reduce_scatter x4 -> x2, waiting for transfers between devices: 91 us -> 41.8 us  [scatter_tensor(): return lax.psum_scatter(rows, 'tensor', scatter_dimension=0, tiled=True)]
    dot_general x6 -> x4, matrix products: 44.4 us -> 9.17 us  [product(): return jnp.dot(left, right, preferred_element_type=jnp.float32)]
    dot_general x7 -> x4, matrix products: 39.5 us -> 7.41 us  [product_nt(): lax.dot_general(left, right, (((1,), (1,)), ((), ())), preferred_element_...]
    dot_general x5 -> x2, matrix products: 35.6 us -> 7.66 us  [product_tn(): lax.dot_general(left, right, (((0,), (0,)), ((), ())), preferred_element_...]
    unnamed x21 -> x13, waiting for transfers between devices: 23.4 us -> 0.88 us
  transfers between devices with their start and end apart: 20 -> 13, of which waited for: 16 -> 9; matrix products, arithmetic and copies ran while one was open for 24% -> 19% of each run, Pallas kernels for 0% -> 0%
where the time goes in v2:
time: 737 us; the launch traced here: 728 us
  waiting for transfers between devices  329 us (45%)
  Pallas kernels  132 us (18%)
  local copies, waits for them, and re-layouts  126 us (17%)
  other arithmetic  42.1 us (6%)
  matrix products  38.8 us (5%)
  blocking collectives  28 us (4%)
  between operations  25.9 us (4%)
    reduce_scatter x4, waiting for transfers between devices, scatter_dp(): return lax.psum_scatter(rows, 'dp', scatter_dimension=0, tiled=True)  177 us
    pallas_call x1, Pallas kernels, ffn_layer(): pl.pallas_call(functools.partial(ffn_kernel, (shared_pad, expert_units, e...  132 us
    unnamed x111, local copies, waits for them, and re-layouts  46.7 us
    all_gather x2, waiting for transfers between devices, gather_dp(): return lax.all_gather(rows, 'dp', axis=0, tiled=True)  41.9 us
    reduce_scatter x2, waiting for transfers between devices, scatter_tensor(): return lax.psum_scatter(rows, 'tensor', scatter_dimension=0, tiled=True)  41.8 us
    all_to_all x1, waiting for transfers between devices, on_device(): lax.all_to_all(grad_shared, 'dp', split_axis=1, concat_axis=2, tiled=True)  41.5 us
    all_gather x3, waiting for transfers between devices, gather_tensor(): return lax.all_gather(rows, 'tensor', axis=0, tiled=True)  26.1 us
    psum x1, blocking collectives, on_device(): small = scatter_dp(lax.psum(small, 'tensor'))  17.4 us
  transfers between devices with their start and end apart: 13, of which 9 were waited for; matrix products, arithmetic and copies ran while one was open for 19% of the time, Pallas kernels for 0%

profile of v2, /device:TPU:0, one launch (start us, length us, event | category | flops | bytes accessed | tf_op | source)
XLA Modules:
  0.0 727.5 jit_solution(12097165839876511893)
XLA Ops:
  17.2 2.8 convolution_add_fusion.4
  20.2 2.3 convolution_add_fusion.2
  32.9 2.6 copy.230
  37.6 1.9 copy.234
  39.5 10.6 %all_gather.19 = s32[2048,4]{0,1:T(4,128)S(1)} all-gather(s32[256,4]{0,1:T(4,128)S(1)} %copy-done.39), channel_id=1, replica_groups=mesh['dp'=8,'tensor'=4] {'dp'}, dimensions={0}, use_global_device_ids=true | all-gather | bytes 36864 | tf_op jit(solution)/shard_map/all_gather | solution.py:859
  50.6 2.0 reshape.503.kept_ref
  52.6 4.1 constant_dynamic-slice_fusion
  61.5 1.9 constant_dynamic-slice_fusion.2
  65.0 2.2 fusion.9
  67.3 2.8 fusion.2.w_pre_ref
  70.1 4.2 gather_fusion
  74.3 2.9 copy.265
  83.7 41.9 %all-gather.8.cloned.1.call-done = bf16[2048,2048]{1,0:T(8,128)(2,1)} async-done(((bf16[256,2048]{1,0:T(8,128)(2,1)}), bf16[2048,2048]{1,0:T(8,128)(2,1)}) %all-gather.8.cloned.1.call-update) | async-done | bytes 8388624 | tf_op jit(solution)/shard_map/all_gather | solution.py:78
  125.6 132.2 %shard_map.348 = (f32[64,2048]{1,0:T(8,128)}, f32[64,2048]{1,0:T(8,128)}, bf16[64,2048]{1,0:T(8,128)(2,1)}, bf16[4,2,2,2,64,2048]{5,4,3,2,1,0:T(8,128)(2,1)}, f3...) custom-call(bf16[4,64,2048]{2,1,0:T(8,128)(2,1)} %bitcast.193, ...), custom_call_target="tpu_custom_call" | custom-call | flops 51539607552 | bytes 62914560 | tf_op jit(solution)/shard_map/pallas_call | solution.py:735
  267.0 17.7 %all-gather.12.cloned.1.call-done = bf16[256,2048]{1,0:T(8,128)(2,1)} async-done(((bf16[64,2048]{1,0:T(8,128)(2,1)}), bf16[256,2048]{1,0:T(8,128)(2,1)}) %all-gather.12.cloned.1.call-update) | async-done | bytes 1048592 | tf_op jit(solution)/shard_map/all_gather | solution.py:82
  284.7 2.6 convolution_convert_fusion.3
  287.5 4.9 fusion.47
  292.4 3.7 multiply_reduce_fusion
  296.1 1.9 copy.243
  298.0 4.1 multiply_convert_fusion
  305.3 2.9 copy.242
  313.1 2.6 convert_element_type.138
  315.8 8.6 %copy.236 = bf16[2,2,2,4,64,2048]{5,4,3,2,1,0:T(8,128)(2,1)} copy(bf16[2,2,2,4,64,2048]{5,4,1,0,2,3:T(8,128)(2,1)} %bitcast.164) | data formatting | bytes 16777216 | tf_op jit(solution)/shard_map/transpose | solution.py:934
  328.2 38.5 %reduce-scatter.14.cloned.1.call-done = bf16[256,1024]{1,0:T(8,128)(2,1)} async-done(((bf16[2048,1024]{1,0:T(8,128)(2,1)}), bf16[256,1024]{1,0:T(8,128)(2,1)}) %reduce-scatter.14.cloned.1.call-update) | async-done | bytes 524304 | tf_op jit(solution)/shard_map/reduce_scatter | solution.py:90
  370.2 2.5 fusion.57
  374.7 2.4 multiply_reduce_fusion.1
  377.2 64.5 %reduce-scatter.10.cloned.1.call-done = bf16[256,2048]{1,0:T(8,128)(2,1)} async-done(((bf16[2048,2048]{1,0:T(8,128)(2,1)}), bf16[256,2048]{1,0:T(8,128)(2,1)}) %reduce-scatter.10.cloned.1.call-update) | async-done | bytes 1048592 | tf_op jit(solution)/shard_map/reduce_scatter | solution.py:90
  442.4 2.5 slice.220
  454.9 16.7 %reduce-scatter.16.cloned.1.call-done = bf16[64,2048]{1,0:T(8,128)(2,1)} async-done(((bf16[256,2048]{1,0:T(8,128)(2,1)}), bf16[64,2048]{1,0:T(8,128)(2,1)}) %reduce-scatter.16.cloned.1.call-update) | async-done | bytes 262160 | tf_op jit(solution)/shard_map/reduce_scatter | solution.py:94
  472.7 2.0 add_convert_fusion
  474.8 25.0 %reduce-scatter.12.cloned.1.call-done = bf16[64,2048]{1,0:T(8,128)(2,1)} async-done(((bf16[256,2048]{1,0:T(8,128)(2,1)}), bf16[64,2048]{1,0:T(8,128)(2,1)}) %reduce-scatter.12.cloned.1.call-update) | async-done | bytes 262160 | tf_op jit(solution)/shard_map/reduce_scatter | solution.py:94
  499.8 1.9 add_convert_fusion.1
  501.8 2.0 convolution_convert_fusion.1
  503.8 5.6 convolution_convert_fusion
  509.4 7.7 %pad_maximum_fusion = bf16[2048,2048]{0,1:T(8,128)(2,1)} fusion(bf16[2048,512]{0,1:T(8,128)(2,1)S(1)} %convolution_convert_fusion.1, bf16[2048,1536]{0,1:T(8,128)(2,1)} %convolution_convert_fusion), kind=kLoop, calls=%fused_computation.5 | loop fusion | flops 16777216 | bytes 16777216 | tf_op jit(solution)/shard_map/concatenate | solution.py:1001
  517.2 1.9 copy-done.16
  519.0 17.1 %copy.248 = bf16[3,2048,176]{2,0,1:T(4,128)(2,1)} copy(bf16[3,2048,176]{2,1,0:T(8,128)(2,1)S(1)} %bitcast.177) | data formatting | bytes 4325376 | tf_op jit(solution)/shard_map/slice | solution.py:938
  536.1 5.1 all-to-all-start
  541.3 2.3 copy.260
  543.5 3.6 copy.261
  547.2 2.3 copy.262
  549.4 41.5 %all-to-all-done = bf16[3,2048,176]{2,0,1:T(4,128)(2,1)} async-done(((bf16[3,2048,176]{2,0,1:T(4,128)(2,1)}), bf16[3,2048,176]{2,0,1:T(4,128)(2,1)}, u32[]{:S(2)}, u32[]{:S(2)}) %all-to-all-start) | async-done | bytes 2162720 | tf_op jit(solution)/shard_map/all_to_all | solution.py:1002
  590.9 5.5 copy.249
  597.0 2.0 copy.279
  610.6 17.4 %psum.8 = f32[256,11]{0,1:T(8,128)S(1)} all-reduce(f32[256,11]{0,1:T(8,128)} %reduce-scatter.20.cloned.1.call-done), channel_id=1, replica_groups=mesh['dp'=8,'tensor'=4] {'tensor'}, use_global_device_ids=true, to_apply=%region_19.20 | all-reduce | flops 2816 | bytes 22528 | tf_op jit(solution)/shard_map/psum | solution.py:999
  629.3 8.4 %all-gather.10.cloned.1.call-done = bf16[256,2048]{1,0:T(8,128)(2,1)} async-done(((bf16[64,2048]{1,0:T(8,128)(2,1)}), bf16[256,2048]{1,0:T(8,128)(2,1)}) %all-gather.10.cloned.1.call-update) | async-done | bytes 1048592 | tf_op jit(solution)/shard_map/all_gather | solution.py:82
  637.6 74.0 %reduce-scatter.18.cloned.1.call-done = bf16[256,2048]{0,1:T(8,128)(2,1)} async-done(((bf16[2048,2048]{0,1:T(8,128)(2,1)}), bf16[256,2048]{0,1:T(8,128)(2,1)}) %reduce-scatter.18.cloned.1.call-update) | async-done | bytes 1048592 | tf_op jit(solution)/shard_map/reduce_scatter | solution.py:90
  717.0 2.3 copy.291
  (220 shorter events, 83.6 us)
Async XLA Ops:
  7.2 62.9 %all-gather.6.cloned.1.call-start = ((), (), s32[]{:S(2)}) async-start(), calls=%async_computation.8 | async-start | bytes 4718592 | tf_op jit(solution)/shard_map/all_gather | solution.py:78
  13.0 4.1 copy-start.41
  17.2 424.6 %copy-start.35 = (f32[256]{0:T(256)}, f32[256]{0:T(256)S(1)}, u32[]{:S(2)}) copy-start(f32[256]{0:T(256)S(1)} %add_rsqrt_fusion) | copy-start | bytes 3076
  17.2 3.0 copy-start.5
  17.2 3.0 copy-start.33
  17.2 3.0 copy-start.43
  23.8 1.6 copy-start.24
  28.7 1.7 copy-start.42
  28.7 2.7 copy-start.29
  29.6 96.0 %all-gather.8.cloned.1.call-start = ((), (), s32[]{:S(2)}) async-start(), calls=%async_computation.9 | async-start | bytes 9437184 | tf_op jit(solution)/shard_map/all_gather | solution.py:78
  30.3 254.4 %all-gather.12.cloned.1.call-start = ((), (), s32[]{:S(2)}) async-start(), calls=%async_computation.13 | async-start | bytes 1310720 | tf_op jit(solution)/shard_map/all_gather | solution.py:82
  31.4 4.1 copy-start.37
  31.4 5.3 copy-start.34
  35.5 4.0 copy-start.39
  58.7 4.6 copy-start.13
  58.7 4.6 copy-start.10
  63.3 1.5 copy-start.21
  63.4 1.7 copy-start.22
  74.3 2.9 copy-start.38
  77.6 2.3 copy-start.14
  78.6 2.5 copy-start
  79.9 2.0 copy-start.23
  125.5 140.7 %copy-start.40 = (s32[3]{0:T(128)S(1)}, s32[3]{0:T(128)}, u32[]{:S(2)}) copy-start(s32[3]{0:T(128)} %constant.173.clone.1) | copy-start | bytes 40
  257.8 108.9 %reduce-scatter.14.cloned.1.call-start = ((), (), s32[]{:S(2)}) async-start(), calls=%async_computation.14 | async-start | bytes 4718592 | tf_op jit(solution)/shard_map/reduce_scatter | solution.py:90
  287.5 5.0 copy-start.1
  287.5 5.0 copy-start.15
  308.1 1.6 copy-start.2
  315.7 126.0 %reduce-scatter.10.cloned.1.call-start = ((), (), s32[]{:S(2)}) async-start(), calls=%async_computation.10 | async-start | bytes 9437184 | tf_op jit(solution)/shard_map/reduce_scatter | solution.py:90
  324.3 1.8 copy-start.4
  324.4 2.2 copy-start.8
  324.4 147.2 %reduce-scatter.16.cloned.1.call-start = ((), (), s32[]{:S(2)}) async-start(), calls=%async_computation.15 | async-start | bytes 1310720 | tf_op jit(solution)/shard_map/reduce_scatter | solution.py:94
  328.2 40.6 %copy-start.26 = (f32[256,4,128]{0,2,1:T(8,128)S(1)}, f32[256,4,128]{0,2,1:T(8,128)}, u32[]{:S(2)}) copy-start(f32[256,4,128]{0,2,1:T(8,128)} %get-tuple-element.258) | copy-start | bytes 1572868
  328.2 40.6 %copy-start.32 = (f32[256,128]{0,1:T(8,128)S(1)}, f32[256,128]{0,1:T(8,128)}, u32[]{:S(2)}) copy-start(f32[256,128]{0,1:T(8,128)} %get-tuple-element.236) | copy-start | bytes 393220
  370.2 2.5 copy-start.20
  372.7 1.9 copy-start.25
  372.7 2.0 copy-start.28
  377.2 122.7 %reduce-scatter.12.cloned.1.call-start = ((), (), s32[]{:S(2)}) async-start(), calls=%async_computation.11 | async-start | bytes 1310720 | tf_op jit(solution)/shard_map/reduce_scatter | solution.py:94
  441.8 166.1 %reduce-scatter.22.cloned.1.call-start = ((), (), s32[]{:S(2)}) async-start(), calls=%async_computation.19 | async-start | bytes 73728
  453.4 157.3 %reduce-scatter.20.cloned.1.call-start = ((), (), s32[]{:S(2)}) async-start(), calls=%async_computation.18 | async-start | bytes 147456 | tf_op jit(solution)/shard_map/reduce_scatter | solution.py:90
  454.8 174.4 %all-gather.14.cloned.1.call-start = ((), (), s32[]{:S(2)}) async-start(), calls=%async_computation.16 | async-start | bytes 1310720 | tf_op jit(solution)/shard_map/all_gather | solution.py:82
  474.7 29.1 %copy-start.36 = (f32[256]{0:T(256)S(1)}, f32[256]{0:T(256)}, u32[]{:S(2)}) copy-start(f32[256]{0:T(256)} %copy-done.35) | copy-start | bytes 3076
  474.8 162.9 %all-gather.10.cloned.1.call-start = ((), (), s32[]{:S(2)}) async-start(), calls=%async_computation.12 | async-start | bytes 1310720 | tf_op jit(solution)/shard_map/all_gather | solution.py:82
  501.7 209.9 %reduce-scatter.18.cloned.1.call-start = ((), (), s32[]{:S(2)}) async-start(), calls=%async_computation.17 | async-start | bytes 9437184 | tf_op jit(solution)/shard_map/reduce_scatter | solution.py:90
  517.1 1.9 copy-start.16
  536.1 5.1 copy-start.18
  536.1 54.8 %all-to-all-start = ((bf16[3,2048,176]{2,0,1:T(4,128)(2,1)}), bf16[3,2048,176]{2,0,1:T(4,128)(2,1)}, u32[]{:S(2)}, u32[]{:S(2)}) async-start(bf16[3,2048,176]{2,0,1:T(4,128)(2,1)} %copy.248), calls=%async_computation.5 | async-start | bytes 8388608 | tf_op jit(solution)/shard_map/all_to_all | solution.py:1002
  543.5 3.6 copy-start.17
  714.0 5.3 copy-start.30
  (9 other events, 10.1 us)
Sparse Core Ops, SparseCore 0:
  29.7 39.4 all-gather.5
  71.1 54.3 all-gather.7
  257.9 26.7 all-gather.11
  315.9 50.8 reduce-scatter.13
  370.4 71.2 reduce-scatter.9
  444.5 27.1 reduce-scatter.15
  474.0 25.7 reduce-scatter.11
  502.8 31.8 reduce-scatter.21
  538.6 37.3 reduce-scatter.19
  578.0 29.7 all-gather.13
  609.9 27.6 all-gather.9
  640.9 70.6 reduce-scatter.17

commit v3 on v2

--- a/solution.py
+++ b/solution.py
@@ -162,7 +162,7 @@
 
 
 def ffn_plain(attn_part, hidden_own, grad_own, ffn_gain, kept, out_all, w_pre, w_down, layout):
-    shared_pad, expert_units, experts, units_pad = layout
+    _, shared_pad, expert_units, experts, units_pad = layout
     units = shared_pad + expert_units
     bf16, f32 = jnp.bfloat16, jnp.float32
     place, column = lax.axis_index("dp"), lax.axis_index("tensor")
@@ -278,8 +278,7 @@
     e_up_ref,
     e_down_ref,
     shared_ref,
-    side_ref,
-    gain_grad_ref,
+    small_ref,
     rows_all,
     dy_all,
     w_pre,
@@ -310,7 +309,7 @@
     rs_links,
     rs_z,
 ):
-    shared_pad, expert_units, experts, unit_pad, half, wide = units
+    shared_units, shared_pad, expert_units, experts, unit_pad, half, wide = units
     bf16, f32 = jnp.bfloat16, jnp.float32
     place, column = lax.axis_index("dp"), lax.axis_index("tensor")
     core, east, north = place % 2, (place // 2) % 2, place // 4
@@ -641,7 +640,7 @@
             pltpu.make_async_copy(tile_up.at[slot], e_up_ref.at[window], tile_sems.at[slot, 1]),
             pltpu.make_async_copy(tile_down.at[slot], e_down_ref.at[window], tile_sems.at[slot, 2]),
             pltpu.make_async_copy(
-                tile_shared.at[slot], shared_ref.at[:, window], tile_sems.at[slot, 3]
+                tile_shared.at[slot], shared_ref.at[i], tile_sems.at[slot, 3]
             ),
         ]
 
@@ -660,13 +659,13 @@
         lhs = rows_all[:, :, :, :, :, window].reshape(tokens, tile)
         grad = product_tn(lhs, both_all[...].reshape(tokens, 2 * unit_pad))
         tile_gate[slot] = grad[:, expert]
-        tile_shared[slot, 0] = grad[:, :shared_pad].astype(bf16)
+        tile_shared[slot, 0] = grad[:, :shared_pad].T[:shared_units].astype(bf16)
         tile_up[slot] = grad[:, unit_pad + shared_pad : unit_pad + shared_pad + expert_units]
-        tile_shared[slot, 1] = grad[:, unit_pad : unit_pad + shared_pad].astype(bf16)
+        tile_shared[slot, 1] = grad[:, unit_pad : unit_pad + shared_pad].T[:shared_units].astype(bf16)
         lhs = dy_all[:, :, :, :, :, window].reshape(tokens, tile)
         grad = product_tn(lhs, scaled_all[...].reshape(tokens, unit_pad))
         tile_down[slot] = grad[:, expert]
-        tile_shared[slot, 2] = grad[:, :shared_pad].astype(bf16)
+        tile_shared[slot, 2] = grad[:, :shared_pad].T[:shared_units].astype(bf16)
         for copy in tile_copies(i, slot):
             copy.start()
 
@@ -701,8 +700,9 @@
     )
     side = side.astype(bf16)
     normed_grad = total[:, :width] + product_nt(side, side_w)
-    side_ref[...] = product_tn(own_normed, side)
-    gain_grad_ref[...] = jnp.sum(normed_grad * unit, 0, keepdims=True)
+    side_rows = product_tn(side, own_normed)
+    small_ref[...] = side_rows[first_lane : first_lane + small_ref.shape[0]]
+    small_ref[experts + 1 : experts + 2, :] = jnp.sum(normed_grad * unit, 0, keepdims=True)
     grad_f = grad_ref[...].astype(f32) + norm_back(normed_grad, unit, scale_rows, gain_ref[...])
     res_grad_ref[...] = grad_f
     res_low_ref[...] = grad_f.astype(bf16)
@@ -720,7 +720,7 @@
 def ffn_layer(
     attn_part, hidden_own, grad_own, ffn_gain, kept, grad_all, w_pre, w_down, layout
 ):
-    shared_pad, expert_units, experts, unit_pad = layout
+    shared_units, shared_pad, expert_units, experts, unit_pad = layout
     rows, width = hidden_own.shape
     bf16, f32 = jnp.bfloat16, jnp.float32
     half = width // 2
@@ -734,7 +734,7 @@
     )
     return pl.pallas_call(
         functools.partial(
-            ffn_kernel, (shared_pad, expert_units, experts, unit_pad, half, wide)
+            ffn_kernel, (shared_units, shared_pad, expert_units, experts, unit_pad, half, wide)
         ),
         out_shape=[
             shape((rows, width), f32),
@@ -744,12 +744,11 @@
             shape((width, expert_units), f32),
             shape((width, expert_units), f32),
             shape((width, expert_units), f32),
-            shape((3, width, shared_pad), bf16),
-            shape((width, 128), f32),
-            shape((1, width), f32),
+            shape((width // tile, 3, shared_units, tile), bf16),
+            shape((16, width), f32),
         ],
         in_specs=[anywhere, vmem, vmem, vmem, vmem, anywhere, anywhere, anywhere],
-        out_specs=[vmem, vmem, vmem] + [anywhere] * 5 + [vmem, vmem],
+        out_specs=[vmem, vmem, vmem] + [anywhere] * 5 + [vmem],
         scratch_shapes=[
             pltpu.VMEM((4, 2, 2, 2, rows, width), bf16),
             pltpu.VMEM((4, 2, 2, 2, rows, width), bf16),
@@ -769,7 +768,7 @@
             pltpu.VMEM((2, tile, expert_units), f32),
             pltpu.VMEM((2, tile, expert_units), f32),
             pltpu.VMEM((2, tile, expert_units), f32),
-            pltpu.VMEM((2, 3, tile, shared_pad), bf16),
+            pltpu.VMEM((2, 3, shared_units, tile), bf16),
             dma((11,)),
             dma((2,)),
             dma((2, 4)),
@@ -786,6 +785,612 @@
         ),
         cost_estimate=cost,
     )(attn_part, hidden_own, grad_own, ffn_gain, kept, grad_all, w_pre, w_down)
+
+
+class PlaneSum:
+    def __init__(self, mine, theirs, got_core, got_x1, got_y1, got_y2, got_x2, core_sems, sems):
+        self.mine, self.theirs = mine, theirs
+        self.got = (got_core, got_x1, got_y1, got_y2, got_x2)
+        self.core_sems, self.sems = core_sems, sems
+        self.wide = got_core.shape[-1]
+        self.half = got_x1.shape[-1]
+        self.left, self.right = pl.ds(0, self.half), pl.ds(self.half, self.wide - self.half)
+        place = lax.axis_index("dp")
+        self.core, self.east, self.north = place % 2, (place // 2) % 2, place // 4
+        self.sibling = {"dp": other(place, 1)}
+        self.x_side, self.y_side = {"dp": other(place, 2)}, {"dp": other(place, 4)}
+
+    def remote(self, src, dst, sems, which, device):
+        return pltpu.make_async_remote_copy(
+            src_ref=src,
+            dst_ref=dst,
+            send_sem=sems.at[(0, *which)],
+            recv_sem=sems.at[(1, *which)],
+            device_id=device,
+            device_id_type=MESH,
+        )
+
+    def core_copy(self, k):
+        return self.remote(
+            self.theirs(k), self.got[0].at[k], self.core_sems, (k,), self.sibling
+        )
+
+    def first_copies(self, k):
+        mine = self.mine(k)
+        return [
+            self.remote(
+                mine.at[:, flip(self.east), :, self.left],
+                self.got[1].at[k],
+                self.sems,
+                (0, k),
+                self.x_side,
+            ),
+            self.remote(
+                mine.at[flip(self.north), :, :, self.right],
+                self.got[2].at[k],
+                self.sems,
+                (1, k),
+                self.y_side,
+            ),
+        ]
+
+    def second_copies(self, k):
+        mine = self.mine(k)
+        return [
+            self.remote(
+                mine.at[flip(self.north), self.east, :, self.left],
+                self.got[3].at[k],
+                self.sems,
+                (2, k),
+                self.y_side,
+            ),
+            self.remote(
+                mine.at[self.north, flip(self.east), :, self.right],
+                self.got[4].at[k],
+                self.sems,
+                (3, k),
+                self.x_side,
+            ),
+        ]
+
+    def add(self, ref, value):
+        ref[...] = (ref[...].astype(jnp.float32) + value.astype(jnp.float32)).astype(jnp.bfloat16)
+
+    def start(self, k):
+        self.core_copy(k).start()
+
+    def after_core(self, k):
+        self.core_copy(k).wait_recv()
+        mine = self.mine(k)
+        for y in range(2):
+            for x in range(2):
+                self.add(mine.at[y, x], self.got[0][k, y, x])
+        for copy in self.first_copies(k):
+            copy.start()
+
+    def after_first(self, k):
+        x_copy, y_copy = self.first_copies(k)
+        mine = self.mine(k)
+        x_copy.wait_recv()
+        for y in range(2):
+            self.add(mine.at[y, self.east, :, self.left], self.got[1][k, y])
+        y_copy.wait_recv()
+        for x in range(2):
+            self.add(mine.at[self.north, x, :, self.right], self.got[2][k, x])
+        for copy in self.second_copies(k):
+            copy.start()
+
+    def after_second(self, k):
+        y_copy, x_copy = self.second_copies(k)
+        own = self.mine(k).at[self.north, self.east]
+        y_copy.wait_recv()
+        self.add(own.at[:, self.left], self.got[3][k])
+        x_copy.wait_recv()
+        self.add(own.at[:, self.right], self.got[4][k])
+        return own
+
+    def wait_sends(self, k):
+        self.core_copy(k).wait_send()
+        for copy in self.first_copies(k) + self.second_copies(k):
+            copy.wait_send()
+
+
+def plane_scratch(count, rows, wide):
+    half = wide // 2
+    bf16, dma = jnp.bfloat16, pltpu.SemaphoreType.DMA
+    return [
+        pltpu.VMEM((count, 2, 2, rows, wide), bf16),
+        pltpu.VMEM((count, 2, rows, half), bf16),
+        pltpu.VMEM((count, 2, rows, wide - half), bf16),
+        pltpu.VMEM((count, rows, half), bf16),
+        pltpu.VMEM((count, rows, wide - half), bf16),
+        dma((2, count)),
+        dma((2, 4, count)),
+    ]
+
+
+def unturn(grad, cosine, sine):
+    heads = []
+    for begin in range(0, grad.shape[1], HEAD_DIM):
+        head = grad[:, begin : begin + HEAD_DIM]
+        heads.append(head * cosine - pltpu.roll(head, HEAD_DIM // 2, 1) * sine)
+    return jnp.concatenate(heads, 1)
+
+
+def back_kernel(
+    score_scale,
+    gain_row,
+    residual_ref,
+    res_grad_ref,
+    res_low_ref,
+    ffn_part_ref,
+    shared_ref,
+    small_ref,
+    query_ref,
+    key_ref,
+    value_ref,
+    level_mask_ref,
+    level_spots_ref,
+    log_total_ref,
+    attended_ref,
+    normed_ref,
+    hidden_ref,
+    gain_ref,
+    cosine_ref,
+    sine_ref,
+    w_out_ref,
+    w_query_ref,
+    w_key_ref,
+    w_value_ref,
+    hidden_out_ref,
+    hidden_grad_ref,
+    grad_query_ref,
+    grad_key_ref,
+    grad_value_ref,
+    grad_out_ref,
+    grad_shared_ref,
+    small_out_ref,
+    bias_out_ref,
+    low_all,
+    w_qkv,
+    out_mine,
+    out_z,
+    kv_sums,
+    w_sums,
+    kv_path,
+    attended_grad,
+    query_grad,
+    pre_grads,
+    part,
+    part_send,
+    part_z,
+    hidden_stage,
+    shared_got,
+    shared_stage,
+    small_send,
+    small_got,
+    small_z,
+    *rest,
+):
+    bf16, f32 = jnp.bfloat16, jnp.float32
+    out_scr, rest = rest[:7], rest[7:]
+    kv_scr, rest = rest[:7], rest[7:]
+    w_scr, rest = rest[:7], rest[7:]
+    wkv_sems, rest = rest[:2], rest[2:]
+    load_sems, low_sems, out_sems, part_sems, end_sems, shared_sems, small_sems, small_z_sems = rest
+    place, column = lax.axis_index("dp"), lax.axis_index("tensor")
+    core, east, north = place % 2, (place // 2) % 2, place // 4
+    rows, width = residual_ref.shape
+    tok_rows, local_width = query_ref.shape
+    levels = [{"tensor": other(column, k)} for k in range(4)]
+    peers = [{"dp": other(place, j)} for j in range(8)]
+
+    def remote(src, dst, sems, which, device):
+        return pltpu.make_async_remote_copy(
+            src_ref=src,
+            dst_ref=dst,
+            send_sem=sems.at[(0, *which)],
+            recv_sem=sems.at[(1, *which)],
+            device_id=device,
+            device_id_type=MESH,
+        )
+
+    def load_out(z):
+        return pltpu.make_async_copy(ffn_part_ref.at[z, core], out_mine.at[z], load_sems.at[z])
+
+    loads = [
+        pltpu.make_async_copy(w_query_ref, w_qkv.at[0], load_sems.at[5]),
+        pltpu.make_async_copy(w_key_ref, w_qkv.at[1], load_sems.at[6]),
+        pltpu.make_async_copy(w_out_ref, w_qkv.at[2], load_sems.at[4]),
+    ]
+    load_value = pltpu.make_async_copy(w_value_ref, w_qkv.at[2], load_sems.at[7])
+    for z in range(4):
+        load_out(z).start()
+    for copy in loads:
+        copy.start()
+
+    barrier = pltpu.get_barrier_semaphore()
+    partners = peers[1:] + levels[1:]
+    for partner in partners:
+        pl.semaphore_signal(barrier, inc=1, device_id=partner, device_id_type=MESH)
+    pl.semaphore_wait(barrier, len(partners))
+
+    out_sum = PlaneSum(
+        lambda k: out_mine.at[k], lambda k: ffn_part_ref.at[k, flip(core)], *out_scr
+    )
+    kv_sum = PlaneSum(
+        lambda k: kv_sums.at[core], lambda k: kv_sums.at[flip(core)], *kv_scr
+    )
+    w_sum = PlaneSum(
+        lambda k: w_sums.at[k, core], lambda k: w_sums.at[k, flip(core)], *w_scr
+    )
+    wkv_sum = PlaneSum(
+        lambda k: kv_sums.at[core], lambda k: kv_sums.at[flip(core)], *kv_scr[:5], *wkv_sems
+    )
+
+    low_all[column] = res_low_ref[...]
+    own_low = low_all.at[column]
+    low_copies = [remote(own_low, own_low, low_sems, (k,), levels[k]) for k in (3, 2, 1)]
+    for copy in low_copies:
+        copy.start()
+    for z in range(4):
+        out_sum.start(z)
+    for z in range(4):
+        load_out(z).wait()
+        out_sum.after_core(z)
+    for copy in loads:
+        copy.wait()
+    for copy in low_copies:
+        copy.wait_recv()
+
+    low_rows = low_all[...].reshape(tok_rows, width)
+    attended_grad[...] = product(low_rows, w_qkv[2]).astype(bf16)
+    load_value.start()
+
+    def block_index(place_of):
+        return place_of % 2, place_of // 4, (place_of // 2) % 2
+
+    def out_weights(i, carry):
+        c, y, x = block_index(i)
+        window = pl.ds(pl.multiple_of(i * tok_rows, tok_rows), tok_rows)
+        lhs = low_all[:, :, window].reshape(tok_rows, tok_rows)
+        w_sums[0, c, y, x] = product_tn(lhs, attended_ref[...]).astype(bf16)
+        return carry
+
+    lax.fori_loop(0, 8, out_weights, 0)
+    w_sum.start(0)
+
+    key_rows = key_ref.shape[0]
+    row_id = lax.broadcasted_iota(jnp.int32, (tok_rows, key_rows), 0)
+    col_id = lax.broadcasted_iota(jnp.int32, (tok_rows, key_rows), 1)
+
+    def head(h, carry):
+        cols = pl.ds(pl.multiple_of(h * HEAD_DIM, HEAD_DIM), HEAD_DIM)
+        value_cols = pl.ds(pl.multiple_of(local_width + h * HEAD_DIM, HEAD_DIM), HEAD_DIM)
+        query, key, value = query_ref[:, cols], key_ref[:, cols], value_ref[:, cols]
+        grad = attended_grad[:, cols]
+        scores = product_nt(query, key) * score_scale + level_mask_ref[...]
+        scores = jnp.where((col_id >= tok_rows) | (row_id >= col_id), scores, -jnp.inf)
+        weights = jnp.exp(scores - log_total_ref[h])
+        weight_grad = product_nt(grad, value)
+        center = jnp.sum(weights * weight_grad, 1, keepdims=True)
+        score_grad = (weights * (weight_grad - center)).astype(bf16)
+        query_grad[:, cols] = product(score_grad, key) * score_scale
+        kv_path[:, cols] = (product_tn(score_grad, query) * score_scale).astype(bf16)
+        kv_path[:, value_cols] = product_tn(weights.astype(bf16), grad).astype(bf16)
+        return carry
+
+    lax.fori_loop(0, 2, head, 0)
+    for z in range(4):
+        out_sum.after_first(z)
+    w_sum.after_core(0)
+    lax.fori_loop(2, 4, head, 0)
+
+    def kv_blocks(q, c):
+        y, x = q // 2, q % 2
+        segment = 4 * y + 2 * x + c
+        total = jnp.zeros((tok_rows, 2 * local_width), f32)
+        for level in range(1, LEVELS):
+            spot = level_spots_ref[segment * LEVELS + level]
+            total = total + spot * kv_path[level * tok_rows : (level + 1) * tok_rows].astype(f32)
+        kv_sums[c, y, x] = total.astype(bf16)
+        return c
+
+    lax.fori_loop(0, 4, kv_blocks, flip(core))
+    kv_sum.start(0)
+    lax.fori_loop(0, 4, kv_blocks, core)
+    own_kv = kv_sums.at[core, north, east]
+    own_kv[...] = (own_kv[...].astype(f32) + kv_path[0:tok_rows].astype(f32)).astype(bf16)
+    kv_sum.after_core(0)
+
+    def cast_pre(which, grad):
+        low = grad.astype(bf16)
+        pre_grads[which] = low
+        bias = jnp.sum(low.astype(f32), 0, keepdims=True)
+        for h in range(local_width // HEAD_DIM):
+            small_send[0, 4 * which + h : 4 * which + h + 1, 2 * HEAD_DIM :] = bias[
+                :, h * HEAD_DIM : (h + 1) * HEAD_DIM
+            ]
+
+    small_send[0, :, 2 * HEAD_DIM :] = jnp.zeros((16, HEAD_DIM), f32)
+    cast_pre(0, unturn(query_grad[...], cosine_ref[...], sine_ref[...]))
+
+    def query_weights(i, carry):
+        c, y, x = block_index(i)
+        window = pl.ds(pl.multiple_of(i * tok_rows, tok_rows), tok_rows)
+        w_sums[1, c, y, x] = product_tn(normed_ref[:, window], pre_grads[0]).astype(bf16)
+        return carry
+
+    lax.fori_loop(0, 8, query_weights, 0)
+    w_sum.start(1)
+    part[...] = product_nt(pre_grads[0], w_qkv[0])
+    kv_sum.after_first(0)
+
+    def out_level(k):
+        return remote(
+            out_mine.at[other(column, k), north, east],
+            out_z.at[k],
+            out_sems,
+            (0, k),
+            levels[k],
+        )
+
+    w_sum.after_first(0)
+    for z in range(4):
+        out_sum.after_second(z)
+    for k in (3, 2, 1):
+        out_level(k).start()
+    w_sum.after_core(1)
+
+    own_kv = kv_sum.after_second(0)
+    cast_pre(1, unturn(own_kv[:, :local_width].astype(f32), cosine_ref[...], sine_ref[...]))
+    cast_pre(2, own_kv[:, local_width:].astype(f32))
+    load_value.wait()
+    for which in (1, 2):
+        part[...] += product_nt(pre_grads[which], w_qkv[which])
+
+    hidden_f = hidden_ref[...].astype(f32)
+    unit_scale = lax.rsqrt(jnp.mean(hidden_f * hidden_f, 1, keepdims=True) + epsilon)
+    part_send[...] = part[...].astype(bf16).reshape(4, rows, width)
+
+    def part_copy(k):
+        return remote(part_send.at[other(column, k)], part_z.at[k], part_sems, (k,), levels[k])
+
+    for k in (3, 2, 1):
+        part_copy(k).start()
+    attn_gain_row = jnp.sum(part[...] * (hidden_f * unit_scale), 0, keepdims=True)
+
+    kv_sum.wait_sends(0)
+
+    def key_value_weights(i, carry):
+        c, y, x = block_index(i)
+        window = pl.ds(pl.multiple_of(i * tok_rows, tok_rows), tok_rows)
+        lhs = normed_ref[:, window]
+        kv_sums[c, y, x, :, :local_width] = product_tn(lhs, pre_grads[1]).astype(bf16)
+        kv_sums[c, y, x, :, local_width:] = product_tn(lhs, pre_grads[2]).astype(bf16)
+        return carry
+
+    lax.fori_loop(0, 8, key_value_weights, 0)
+    wkv_sum.start(0)
+
+    bias_rows = small_send[0, :, 2 * HEAD_DIM :]
+    for d in range(8):
+        small_send[d, :, : 2 * HEAD_DIM] = small_ref[:, d * tok_rows : (d + 1) * tok_rows]
+        small_send[d, gain_row : gain_row + 1, : 2 * HEAD_DIM] = attn_gain_row[
+            :, d * tok_rows : (d + 1) * tok_rows
+        ]
+        small_send[d, :, 2 * HEAD_DIM :] = bias_rows
+
+    def small_copy(j):
+        return remote(
+            small_send.at[other(place, j)], small_got.at[j], small_sems, (j,), peers[j]
+        )
+
+    for j in range(1, 8):
+        small_copy(j).start()
+
+    def shared_copy(j):
+        return remote(
+            shared_ref.at[other(place, j)], shared_got.at[place], shared_sems, (j,), peers[j]
+        )
+
+    w_sum.after_first(1)
+    wkv_sum.after_core(0)
+    grad_out_ref[...] = w_sum.after_second(0)[...].astype(f32)
+    for j in (6, 7, 2, 3, 4, 5, 1):
+        shared_copy(j).start()
+    own_shared = pltpu.make_async_copy(shared_ref.at[place], shared_got.at[place], load_sems.at[8])
+    own_shared.start()
+
+    total = small_send[place]
+    for j in range(1, 8):
+        small_copy(j).wait_recv()
+        total = total + small_got[j]
+    bias_out_ref[...] = total[:, 2 * HEAD_DIM :]
+    small_z[column] = total[:, : 2 * HEAD_DIM]
+    own_small = small_z.at[column]
+    small_levels = [
+        remote(own_small, own_small, small_z_sems, (k,), levels[k]) for k in (1, 2, 3)
+    ]
+    for copy in small_levels:
+        copy.start()
+
+    mine = pl.ds(pl.multiple_of(column * rows, rows), rows)
+    attn_grad = part_send[column].astype(f32)
+    for k in (1, 2, 3):
+        part_copy(k).wait_recv()
+        attn_grad = attn_grad + part_z[k].astype(f32)
+    own_hidden = hidden_ref[mine, :].astype(f32)
+    own_scale = lax.rsqrt(jnp.mean(own_hidden * own_hidden, 1, keepdims=True) + epsilon)
+    hidden_stage[0, column] = (
+        res_grad_ref[...] + norm_back(attn_grad, own_hidden * own_scale, own_scale, gain_ref[...])
+    ).astype(bf16)
+
+    def end_copy(which, k):
+        own = hidden_stage.at[which, column]
+        return remote(own, own, end_sems, (which, k), levels[k])
+
+    for k in (3, 2, 1):
+        end_copy(0, k).start()
+
+    out = residual_ref[...] + out_mine[column, north, east].astype(f32)
+    for k in (1, 2, 3):
+        out_level(k).wait_recv()
+        out = out + out_z[k].astype(f32)
+    hidden_stage[1, column] = out.astype(bf16)
+    for k in (3, 2, 1):
+        end_copy(1, k).start()
+
+    wkv_sum.after_first(0)
+    grad_query_ref[...] = w_sum.after_second(1)[...].astype(f32)
+    for copy in small_levels:
+        copy.wait_recv()
+    small_out_ref[...] = (small_z[0] + small_z[1]) + (small_z[2] + small_z[3])
+    own_wkv = wkv_sum.after_second(0)
+    grad_key_ref[...] = own_wkv[:, :local_width].astype(f32)
+    grad_value_ref[...] = own_wkv[:, local_width:].astype(f32)
+
+    own_shared.wait()
+    for j in range(1, 8):
+        shared_copy(j).wait_recv()
+
+    def store_shared(which):
+        return pltpu.make_async_copy(
+            shared_stage, grad_shared_ref.at[which], load_sems.at[9]
+        )
+
+    for which in range(3):
+        units = shared_got[:, which].astype(f32)
+        turned = units.reshape(-1, units.shape[-1]).T
+        if which:
+            store_shared(which - 1).wait()
+        shared_stage[...] = turned
+        store_shared(which).start()
+
+    for k in (1, 2, 3):
+        end_copy(0, k).wait_recv()
+        end_copy(1, k).wait_recv()
+    ends = [
+        pltpu.make_async_copy(hidden_stage.at[0], hidden_grad_ref, load_sems.at[10]),
+        pltpu.make_async_copy(hidden_stage.at[1], hidden_out_ref, load_sems.at[11]),
+    ]
+    for copy in ends:
+        copy.start()
+    store_shared(2).wait()
+    for copy in ends:
+        copy.wait()
+
+    for copy in low_copies + small_levels:
+        copy.wait_send()
+    for z in range(4):
+        out_sum.wait_sends(z)
+    for k in (1, 2, 3):
+        out_level(k).wait_send()
+        part_copy(k).wait_send()
+        end_copy(0, k).wait_send()
+        end_copy(1, k).wait_send()
+    for k in range(2):
+        w_sum.wait_sends(k)
+    wkv_sum.wait_sends(0)
+    for j in range(1, 8):
+        small_copy(j).wait_send()
+        shared_copy(j).wait_send()
+
+
+def back_layer(score_scale, gain_row, operands):
+    (
+        residual,
+        res_grad,
+        res_low,
+        ffn_part,
+        grad_shared,
+        small,
+        query,
+        key,
+        value,
+        level_mask,
+        level_spots,
+        log_total,
+        attended,
+        normed,
+        hidden,
+        gain,
+        cosine,
+        sine,
+        w_out,
+        w_query,
+        w_key,
+        w_value,
+    ) = operands
+    rows, width = residual.shape
+    tok_rows, local_width = query.shape
+    units = grad_shared.shape[2]
+    bf16, f32 = jnp.bfloat16, jnp.float32
+    shape = jax.ShapeDtypeStruct
+    vmem, anywhere = pl.BlockSpec(memory_space=pltpu.VMEM), pl.BlockSpec(memory_space=pl.ANY)
+    smem = pl.BlockSpec(memory_space=pltpu.SMEM)
+    dma = pltpu.SemaphoreType.DMA
+    return pl.pallas_call(
+        functools.partial(back_kernel, score_scale, gain_row),
+        out_shape=[
+            shape((4, rows, width), bf16),
+            shape((4, rows, width), bf16),
+            shape((tok_rows, local_width), f32),
+            shape((tok_rows, local_width), f32),
+            shape((tok_rows, local_width), f32),
+            shape((tok_rows, local_width), f32),
+            shape((3, tok_rows, 8 * units), f32),
+            shape((16, tok_rows), f32),
+            shape((16, HEAD_DIM), f32),
+        ],
+        in_specs=[vmem, vmem, vmem, anywhere, anywhere, vmem]
+        + [vmem] * 4
+        + [smem]
+        + [vmem] * 7
+        + [anywhere] * 4,
+        out_specs=[anywhere] * 2 + [vmem] * 4 + [anywhere, vmem, vmem],
+        scratch_shapes=[
+            pltpu.VMEM((4, rows, width), bf16),
+            pltpu.VMEM((3, width, local_width), bf16),
+            pltpu.VMEM((4, 2, 2, rows, width), bf16),
+            pltpu.VMEM((4, rows, width), bf16),
+            pltpu.VMEM((2, 2, 2, tok_rows, 2 * local_width), bf16),
+            pltpu.VMEM((2, 2, 2, 2, tok_rows, local_width), bf16),
+            pltpu.VMEM((LEVELS * tok_rows, 2 * local_width), bf16),
+            pltpu.VMEM((tok_rows, local_width), bf16),
+            pltpu.VMEM((tok_rows, local_width), f32),
+            pltpu.VMEM((3, tok_rows, local_width), bf16),
+            pltpu.VMEM((tok_rows, width), f32),
+            pltpu.VMEM((4, rows, width), bf16),
+            pltpu.VMEM((4, rows, width), bf16),
+            pltpu.VMEM((2, 4, rows, width), bf16),
+            pltpu.VMEM((8, 3, units, tok_rows), bf16),
+            pltpu.VMEM((tok_rows, 8 * units), f32),
+            pltpu.VMEM((8, 16, 2 * HEAD_DIM + HEAD_DIM), f32),
+            pltpu.VMEM((8, 16, 2 * HEAD_DIM + HEAD_DIM), f32),
+            pltpu.VMEM((4, 16, 2 * HEAD_DIM), f32),
+        ]
+        + plane_scratch(4, rows, width)
+        + plane_scratch(1, tok_rows, 2 * local_width)
+        + plane_scratch(2, tok_rows, local_width)
+        + plane_scratch(1, tok_rows, 2 * local_width)[5:]
+        + [
+            dma((12,)),
+            dma((2, 4)),
+            dma((2, 1, 4)),
+            dma((2, 4)),
+            dma((2, 2, 4)),
+            dma((2, 8)),
+            dma((2, 8)),
+            dma((2, 4)),
+        ],
+        compiler_params=pltpu.CompilerParams(
+            collective_id=1, has_side_effects=True, vmem_limit_bytes=63 * 2**20
+        ),
+        cost_estimate=pl.CostEstimate(
+            flops=2 * 12 * 2**30, bytes_accessed=40 * 2**20, transcendentals=2**20
+        ),
+    )(*operands)
 
 
 def on_device(
@@ -904,7 +1509,7 @@
 
     hidden_own = lax.dynamic_slice_in_dim(hidden_in, column * part_rows, part_rows, 0)
     grad_own = lax.dynamic_slice_in_dim(out_grad, column * part_rows, part_rows, 0)
-    layout = (shared_pad, expert_units, experts, units_pad)
+    layout = (shared_units, shared_pad, expert_units, experts, units_pad)
     cube = devices == 8 and columns == 4
     if cube and all_rows * model_width <= 2**22:
         kept_own = jnp.sum(jnp.where(jnp.arange(experts)[None, :] == place, kept, 0.0), 1)
@@ -918,8 +1523,7 @@
             grad_expert_up,
             grad_expert_down,
             grad_shared,
-            grad_side,
-            grad_ffn_gain,
+            small,
         ) = ffn_layer(
             attn_part.reshape(columns, part_rows, model_width),
             hidden_own,
@@ -931,27 +1535,93 @@
             w_down,
             layout,
         )
-        ffn_part = ffn_part.transpose(2, 3, 1, 0, 4, 5).reshape(all_rows, model_width)
-        grad_ffn_gain = grad_ffn_gain[0]
-        side_first = units - (units_pad - 128)
-        grad_side = grad_side[:, side_first : side_first + experts + 1]
-        grad_shared = grad_shared[:, :, :shared_units]
-    else:
+        spots = jnp.where(reachable[None, :], path[None, :], -1) == jnp.arange(devices)[:, None]
+        level_mask = jnp.repeat(jnp.where(reachable, 0.0, -jnp.inf), tok_rows)[None, :]
+        sign = jnp.where(jnp.arange(HEAD_DIM) < HEAD_DIM // 2, -1.0, 1.0)
         (
-            residual,
-            residual_grad,
-            residual_low,
-            ffn_part,
-            grad_expert_gate,
-            grad_expert_up,
-            grad_expert_down,
-            grad_shared,
-            grad_side,
-            grad_ffn_gain,
-        ) = ffn_plain(
-            attn_part, hidden_own, grad_own, ffn_gain, kept, out_all, w_pre, w_down, layout
+            hidden_out,
+            hidden_in_grad,
+            sum_query,
+            sum_key,
+            sum_value,
+            sum_out,
+            shared_grads,
+            small,
+            bias_sums,
+        ) = back_layer(
+            score_scale,
+            experts + 2,
+            (
+                residual,
+                residual_grad,
+                residual_low,
+                ffn_part,
+                grad_shared,
+                small,
+                query_rot,
+                key_path,
+                value_path,
+                level_mask,
+                spots.astype(f32).reshape(-1),
+                log_total,
+                attended_low,
+                attn_normed,
+                hidden_in,
+                attn_gain[None, :],
+                cosine[:, 0],
+                sine[:, 0] * sign[None, :],
+                w_out,
+                w_query,
+                w_key,
+                w_value,
+            ),
         )
-        grad_shared = grad_shared[:, :, :shared_units]
+        hidden_out = hidden_out.reshape(tok_rows, model_width)
+        hidden_in_grad = hidden_in_grad.reshape(tok_rows, model_width)
+        small = small.T
+        bias_sums = lax.dynamic_slice_in_dim(
+            bias_sums[: 3 * b_query.shape[0]].reshape(3, *b_query.shape),
+            place * (HEAD_DIM // devices),
+            HEAD_DIM // devices,
+            2,
+        )
+        return (
+            hidden_out,
+            hidden_in_grad,
+            small[:, experts + 2],
+            sum_query,
+            sum_key,
+            sum_value,
+            bias_sums[0],
+            bias_sums[1],
+            bias_sums[2],
+            sum_out,
+            small[:, experts + 1],
+            small[:, :experts],
+            small[:, experts],
+            shared_grads[0],
+            shared_grads[1],
+            shared_grads[2],
+            grad_expert_gate[None],
+            grad_expert_up[None],
+            grad_expert_down[None],
+        )
+
+    (
+        residual,
+        residual_grad,
+        residual_low,
+        ffn_part,
+        grad_expert_gate,
+        grad_expert_up,
+        grad_expert_down,
+        grad_shared,
+        grad_side,
+        grad_ffn_gain,
+    ) = ffn_plain(
+        attn_part, hidden_own, grad_own, ffn_gain, kept, out_all, w_pre, w_down, layout
+    )
+    grad_shared = grad_shared[:, :, :shared_units]
     ffn_own = scatter_all(ffn_part).astype(f32)
     hidden_out = gather_tensor((residual + ffn_own).astype(bf16))
     residual_low = gather_tensor(residual_low)

time: 737 us -> 449 us (0.61)
  waiting for transfers between devices: 329 us -> 36.3 us
  Pallas kernels: 132 us -> 289 us
  local copies, waits for them, and re-layouts: 126 us -> 59.3 us
  other arithmetic: 42.1 us -> 15.7 us
  matrix products: 38.8 us -> 12.7 us
  blocking collectives: 28 us -> 10.5 us
  between operations: 25.9 us -> 17.6 us
    reduce_scatter x6 -> x0, waiting for transfers between devices: 219 us -> none  [the longest x4 177 us: scatter_dp(): return lax.psum_scatter(rows, 'dp', scatter_dimension=0, tiled=True)]
    pallas_call x1 -> x2, Pallas kernels: 132 us -> 289 us  [the longest x1 157 us: back_layer(): pl.pallas_call(functools.partial(back_kernel, score_scale, gain_row), out...]
    all_to_all x1 -> x0, waiting for transfers between devices: 41.5 us -> none  [on_device(): lax.all_to_all(grad_shared, 'dp', split_axis=1, concat_axis=2, tiled=True)]
    slice x10 -> x0, local copies, waits for them, and re-layouts: 27.4 us -> none  [the longest x1 17.1 us: on_device(): grad_shared = grad_shared[:, :, :shared_units]]
    all_gather x3 -> x0, waiting for transfers between devices: 26.1 us -> none  [gather_tensor(): return lax.all_gather(rows, 'tensor', axis=0, tiled=True)]
    unnamed x111 -> x67, local copies, waits for them, and re-layouts: 46.7 us -> 24.5 us
    dot_general x6 -> x0, matrix products: 19.7 us -> none  [the longest x2 7.66 us: product_tn(): lax.dot_general(left, right, (((0,), (0,)), ((), ())), preferred_element_...]
    psum x1 -> x0, blocking collectives: 17.4 us -> none  [on_device(): small = scatter_dp(lax.psum(small, 'tensor'))]
  transfers between devices with their start and end apart: 13 -> 2, of which waited for: 9 -> 1; matrix products, arithmetic and copies ran while one was open for 19% -> 10% of each run, Pallas kernels for 0% -> 0%
where the time goes in v3:
time: 449 us; the launch traced here: 441 us
  Pallas kernels  289 us (64%)
  local copies, waits for them, and re-layouts  59.3 us (13%)
  waiting for transfers between devices  36.3 us (8%)
  between operations  17.6 us (4%)
  other arithmetic  15.7 us (3%)
  matrix products  12.7 us (3%)
  blocking collectives  10.5 us (2%)
    pallas_call x1, Pallas kernels, back_layer(): pl.pallas_call(functools.partial(back_kernel, score_scale, gain_row), out...  157 us
    pallas_call x1, Pallas kernels, ffn_layer(): pl.pallas_call(functools.partial(ffn_kernel, (shared_units, shared_pad, e...  132 us
    all_gather x2, waiting for transfers between devices, gather_dp(): return lax.all_gather(rows, 'dp', axis=0, tiled=True)  35.6 us
    unnamed x67, local copies, waits for them, and re-layouts  24.5 us
    all_gather x1, blocking collectives, on_device(): routes_all = lax.all_gather(routes, 'dp', axis=0, tiled=True)  10.5 us
  transfers between devices with their start and end apart: 2, of which 1 were waited for; matrix products, arithmetic and copies ran while one was open for 10% of the time, Pallas kernels for 0%

profile of v3, /device:TPU:0, one launch (start us, length us, event | category | flops | bytes accessed | tf_op | source)
XLA Modules:
  0.0 441.4 jit_solution(4201997675436658326)
XLA Ops:
  7.3 1.2 dynamic_slice.27
  9.2 1.2 dynamic_slice.28
  11.1 1.2 dynamic_slice.29
  14.3 1.7 fusion.12
  16.0 1.5 fusion.14.normed_ref
  18.5 2.3 convolution_add_fusion
  21.1 1.2 broadcast_multiply_fusion
  23.0 0.7 fusion.20
  24.5 1.0 fusion.31
  25.5 0.9 pad_maximum_fusion
  27.4 0.9 copy.76
  28.3 1.9 copy.73
  30.1 1.1 broadcast_in_dim.133
  31.3 1.0 copy.74
  32.3 2.6 copy.77
  34.8 10.5 %all_gather.10 = s32[2048,4]{0,1:T(4,128)S(1)} all-gather(s32[256,4]{0,1:T(4,128)S(1)} %copy-done.20), channel_id=1, replica_groups=mesh['dp'=8,'tensor'=4] {'dp'}, dimensions={0}, use_global_device_ids=true | all-gather | bytes 36864 | tf_op jit(solution)/shard_map/all_gather | solution.py:1464
  45.8 2.0 reshape.385.kept_ref
  49.1 4.1 constant_dynamic-slice_fusion
  53.5 1.7 pad.26.w_down_ref
  55.4 1.7 constant_dynamic-slice_fusion.3.grad_ref
  57.1 1.7 constant_dynamic-slice_fusion.4.hidden_ref
  58.9 1.9 constant_dynamic-slice_fusion.2
  62.0 1.9 fusion.9
  63.9 2.8 fusion.2.w_pre_ref
  66.8 2.9 gather_fusion
  70.1 1.3 fusion.44
  71.9 1.9 fusion.6
  73.8 1.9 copy-done.3
  75.8 1.2 exponential_reduce_fusion
  77.0 1.0 copy.79.log_total_ref
  78.1 4.2 fusion.21
  82.3 1.8 copy.84.attended_ref
  84.1 2.7 convolution_convert_fusion
  86.8 35.6 %all-gather.5.cloned.1.call-done = bf16[2048,2048]{1,0:T(8,128)(2,1)} async-done(((bf16[256,2048]{1,0:T(8,128)(2,1)}), bf16[2048,2048]{1,0:T(8,128)(2,1)}) %all-gather.5.cloned.1.call-update) | async-done | bytes 8388624 | tf_op jit(solution)/shard_map/all_gather | solution.py:78
  122.3 132.4 %shard_map.348 = (f32[64,2048]{1,0:T(8,128)}, f32[64,2048]{1,0:T(8,128)}, bf16[64,2048]{1,0:T(8,128)(2,1)}, bf16[4,2,2,2,64,2048]{5,4,3,2,1,0:T(8,128)(2,1)}, f3...) custom-call(bf16[4,64,2048]{2,1,0:T(8,128)(2,1)} %bitcast.128, ...), custom_call_target="tpu_custom_call" | custom-call | flops 51539607552 | bytes 62914560 | tf_op jit(solution)/shard_map/pallas_call | solution.py:735
  254.8 156.8 %shard_map.349 = (bf16[4,64,2048]{2,1,0:T(8,128)(2,1)}, bf16[4,64,2048]{2,1,0:T(8,128)(2,1)}, f32[256,512]{1,0:T(8,128)}, f32[256,512]{1,0:T(8,128)}, f32[256,51...) custom-call(f32[64,2048]{1,0:T(8,128)} %get-tuple-element.37.residual_ref, ...), custom_call_target="tpu_custom_call" | custom-call | flops 25769803776 | bytes 41943040 | tf_op jit(solution)/shard_map/pallas_call | solution.py:1333
  411.6 1.3 slice.82
  412.8 1.4 fusion.45
  414.2 4.5 %slice_bitcast_fusion = (f32[256,1408]{1,0:T(8,128)}, f32[256,1408]{1,0:T(8,128)}, f32[256,1408]{1,0:T(8,128)}) fusion(f32[3,256,1408]{2,1,0:T(8,128)} %get-tuple-element.51), kind=kLoop, calls=%fused_computation.32 | loop fusion | bytes 8650752 | tf_op jit(solution)/shard_map/squeeze | solution.py:1604
  418.8 2.3 copy.80
  421.0 3.6 copy.81
  424.6 2.3 copy.82
  427.6 2.4 copy.113
  429.9 1.0 copy.114
  430.9 0.8 copy.115
  431.7 0.8 copy.116
  432.5 0.8 copy.117
  433.3 0.8 copy.118
  (99 shorter events, 9.4 us)
Async XLA Ops:
  7.2 10.4 %copy-start.23 = (f32[4,128]{1,0:T(4,128)S(1)}, f32[4,128]{1,0:T(4,128)}, u32[]{:S(2)}) copy-start(f32[4,128]{1,0:T(4,128)} %param.30) | copy-start | bytes 6148
  7.2 59.6 %all-gather.3.cloned.1.call-start = ((), (), s32[]{:S(2)}) async-start(), calls=%async_computation | async-start | bytes 4718592 | tf_op jit(solution)/shard_map/all_gather | solution.py:78
  14.3 3.3 copy-start.22
  17.6 5.4 %copy-start.11 = (bf16[256,2048]{1,0:T(8,128)(2,1)}, bf16[256,2048]{1,0:T(8,128)(2,1)S(1)}, u32[]{:S(2)}) copy-start(bf16[256,2048]{1,0:T(8,128)(2,1)S(1)} %fusion.14.normed_ref) | copy-start | bytes 3145732
  17.6 0.9 copy-start.24
  21.0 1.9 copy-start.21
  21.0 1.9 copy-start.25
  22.3 2.0 copy-start.12
  25.5 1.9 copy-start.9
  26.3 96.0 %all-gather.5.cloned.1.call-start = ((), (), s32[]{:S(2)}) async-start(), calls=%async_computation.1 | async-start | bytes 9437184 | tf_op jit(solution)/shard_map/all_gather | solution.py:78
  27.4 2.7 copy-start.19
  27.4 3.9 copy-start.17
  30.1 4.7 %copy-start.20 = (s32[256,4]{0,1:T(4,128)S(1)}, s32[256,4]{0,1:T(4,128)}, u32[]{:S(2)}) copy-start(s32[256,4]{0,1:T(4,128)} %param.24) | copy-start | bytes 12292
  49.1 4.1 copy-start
  55.2 5.5 %copy-start.1 = (bf16[2048,176]{1,0:T(8,128)(2,1)S(1)}, bf16[2048,176]{1,0:T(8,128)(2,1)}, u32[]{:S(2)}) copy-start(bf16[2048,176]{1,0:T(8,128)(2,1)} %get-tuple-element.146) | copy-start | bytes 2162692
  60.8 1.0 copy-start.6
  60.8 1.2 copy-start.7
  71.4 2.4 copy-start.2
  73.8 2.0 copy-start.3
  78.1 6.0 %copy-start.8 = (bf16[2048,512]{1,0:T(8,128)(2,1)S(1)}, bf16[2048,512]{1,0:T(8,128)(2,1)}, u32[]{:S(2)}) copy-start(bf16[2048,512]{1,0:T(8,128)(2,1)} %w_out_ref.1) | copy-start | bytes 6291460
  414.2 4.5 %copy-start.18 = (f32[16,128]{1,0:T(8,128)S(1)}, f32[16,128]{1,0:T(8,128)}, u32[]{:S(2)}) copy-start(f32[16,128]{1,0:T(8,128)} %get-tuple-element.49) | copy-start | bytes 24580
  414.2 4.5 %copy-start.5 = (f32[2048,352]{1,0:T(8,128)S(1)}, f32[2048,352]{1,0:T(8,128)}, u32[]{:S(2)}) copy-start(f32[2048,352]{1,0:T(8,128)} %get-tuple-element.52) | copy-start | bytes 8650756
  421.0 3.6 copy-start.4
  426.9 3.0 copy-start.10
  426.9 4.0 copy-start.16
  427.6 4.1 copy-start.15
  429.9 2.6 copy-start.14
  429.9 3.4 copy-start.13
Sparse Core Ops, SparseCore 0:
  26.5 39.5 all-gather.2
  67.9 54.3 all-gather.4

commit v4 on v3

--- a/solution.py
+++ b/solution.py
@@ -262,15 +262,12 @@
 
 def ffn_kernel(
     units,
-    part_ref,
-    hidden_ref,
-    grad_ref,
+    residual_ref,
     gain_ref,
-    kept_ref,
+    hits_ref,
     grad_all_ref,
     w_pre_ref,
     w_down_ref,
-    residual_ref,
     res_grad_ref,
     res_low_ref,
     ffn_part_ref,
@@ -292,7 +289,7 @@
     got_y2,
     got_x2,
     got_z,
-    attn_z,
+    kept_ref,
     ffn_chunk,
     tile_gate,
     tile_up,
@@ -301,7 +298,6 @@
     load_sems,
     store_sems,
     tile_sems,
-    attn_sems,
     zs,
     links,
     cores,
@@ -309,11 +305,11 @@
     rs_links,
     rs_z,
 ):
-    shared_units, shared_pad, expert_units, experts, unit_pad, half, wide = units
+    shared_units, shared_pad, expert_units, experts, unit_pad, half, wide, capacity = units
     bf16, f32 = jnp.bfloat16, jnp.float32
     place, column = lax.axis_index("dp"), lax.axis_index("tensor")
     core, east, north = place % 2, (place // 2) % 2, place // 4
-    rows, width = hidden_ref.shape
+    rows, width = residual_ref.shape
     sibling = {"dp": other(place, 1)}
     x_side = {"dp": other(place, 2)}
     y_side = {"dp": other(place, 4)}
@@ -353,23 +349,7 @@
         pl.semaphore_signal(barrier, inc=1, device_id=partner, device_id_type=MESH)
     pl.semaphore_wait(barrier, len(partners))
 
-    attn_copies = []
-    for k in (3, 2, 1):
-        copy = remote(
-            part_ref.at[other(column, k)], attn_z.at[k], attn_sems, (k,), levels[k]
-        )
-        copy.start()
-        attn_copies.append(copy)
-    own_part = pltpu.make_async_copy(part_ref.at[column], attn_z.at[0], load_sems.at[10])
-    own_part.start()
-    own_part.wait()
-    for copy in attn_copies:
-        copy.wait()
-    attn = attn_z[0].astype(f32)
-    for k in range(1, 4):
-        attn = attn + attn_z[k].astype(f32)
-    residual = hidden_ref[...].astype(f32) + attn
-    residual_ref[...] = residual
+    residual = residual_ref[...]
     scale_rows = lax.rsqrt(jnp.mean(residual * residual, 1, keepdims=True) + epsilon)
     normed = (residual * scale_rows * gain_ref[...]).astype(bf16)
     rows_all[column, core, north, east] = normed
@@ -506,6 +486,38 @@
     for k in (1, 2, 3):
         z_copy(k).start()
     start_direct(0)
+
+    tokens_dev = 4 * rows
+    expert_id = lax.broadcasted_iota(jnp.int32, hits_ref.shape, 1)
+    hits = jnp.sum(jnp.where(expert_id == place, hits_ref[...], 0.0), 1)
+    earlier = lax.broadcasted_iota(jnp.int32, (tokens_dev, tokens_dev), 0)
+    later = lax.broadcasted_iota(jnp.int32, (tokens_dev, tokens_dev), 1)
+    slots = product(hits.astype(bf16), (earlier < later).astype(bf16))
+    counts = jnp.sum(hits, 1, keepdims=True)
+    counts_wide = jnp.broadcast_to(counts, (8, 128))
+    order_row = lax.broadcasted_iota(jnp.int32, (8, 8), 0)
+    order_col = lax.broadcasted_iota(jnp.int32, (8, 8), 1)
+    before = lax.dot_general(
+        (order_col < order_row).astype(f32),
+        counts_wide,
+        (((1,), (0,)), ((), ())),
+        precision=highest,
+        preferred_element_type=f32,
+    )
+    kept = jnp.where(slots + before[:, :1] < capacity, hits, 0.0).astype(bf16)
+    eye = (
+        lax.broadcasted_iota(jnp.int32, (8, 128), 0)
+        == lax.broadcasted_iota(jnp.int32, (8, 128), 1)
+    ).astype(bf16)
+    kept_columns = product_tn(kept, eye)
+    for d in range(8):
+        y, x, c = d // 4, (d // 2) % 2, d % 2
+        for z in range(4):
+            first = (2 * y + x) * rows
+            kept_ref[z, c, first : first + rows, :] = kept_columns[
+                z * rows : (z + 1) * rows, d : d + 1
+            ]
+
     load_pre.wait()
     load_down.wait()
     for c in range(2):
@@ -703,7 +715,8 @@
     side_rows = product_tn(side, own_normed)
     small_ref[...] = side_rows[first_lane : first_lane + small_ref.shape[0]]
     small_ref[experts + 1 : experts + 2, :] = jnp.sum(normed_grad * unit, 0, keepdims=True)
-    grad_f = grad_ref[...].astype(f32) + norm_back(normed_grad, unit, scale_rows, gain_ref[...])
+    own_grad = dy_all[column, core, north, east].astype(f32)
+    grad_f = own_grad + norm_back(normed_grad, unit, scale_rows, gain_ref[...])
     res_grad_ref[...] = grad_f
     res_low_ref[...] = grad_f.astype(bf16)
 
@@ -717,11 +730,9 @@
             copy.wait_send()
 
 
-def ffn_layer(
-    attn_part, hidden_own, grad_own, ffn_gain, kept, grad_all, w_pre, w_down, layout
-):
+def ffn_layer(residual, ffn_gain, hits, grad_all, w_pre, w_down, layout, capacity):
     shared_units, shared_pad, expert_units, experts, unit_pad = layout
-    rows, width = hidden_own.shape
+    rows, width = residual.shape
     bf16, f32 = jnp.bfloat16, jnp.float32
     half = width // 2
     wide = width + 128
@@ -734,10 +745,10 @@
     )
     return pl.pallas_call(
         functools.partial(
-            ffn_kernel, (shared_units, shared_pad, expert_units, experts, unit_pad, half, wide)
+            ffn_kernel,
+            (shared_units, shared_pad, expert_units, experts, unit_pad, half, wide, capacity),
         ),
         out_shape=[
-            shape((rows, width), f32),
             shape((rows, width), f32),
             shape((rows, width), bf16),
             shape((4, 2, 2, 2, rows, width), bf16),
@@ -747,8 +758,8 @@
             shape((width // tile, 3, shared_units, tile), bf16),
             shape((16, width), f32),
         ],
-        in_specs=[anywhere, vmem, vmem, vmem, vmem, anywhere, anywhere, anywhere],
-        out_specs=[vmem, vmem, vmem] + [anywhere] * 5 + [vmem],
+        in_specs=[vmem, vmem, vmem, anywhere, anywhere, anywhere],
+        out_specs=[vmem, vmem] + [anywhere] * 5 + [vmem],
         scratch_shapes=[
             pltpu.VMEM((4, 2, 2, 2, rows, width), bf16),
             pltpu.VMEM((4, 2, 2, 2, rows, width), bf16),
@@ -763,15 +774,14 @@
             pltpu.VMEM((4, rows, half), bf16),
             pltpu.VMEM((4, rows, wide - half), bf16),
             pltpu.VMEM((4, rows, wide), bf16),
-            pltpu.VMEM((4, rows, width), bf16),
+            pltpu.VMEM((4, 2, 4 * rows, 1), f32),
             pltpu.VMEM((2, 2, rows, width), bf16),
             pltpu.VMEM((2, tile, expert_units), f32),
             pltpu.VMEM((2, tile, expert_units), f32),
             pltpu.VMEM((2, tile, expert_units), f32),
             pltpu.VMEM((2, 3, shared_units, tile), bf16),
-            dma((11,)),
+            dma((10,)),
             dma((2,)),
-            dma((2, 4)),
             dma((2, 4)),
             dma((2, 4)),
             dma((2, 4, 4)),
@@ -784,7 +794,428 @@
             collective_id=0, has_side_effects=True, vmem_limit_bytes=63 * 2**20
         ),
         cost_estimate=cost,
-    )(attn_part, hidden_own, grad_own, ffn_gain, kept, grad_all, w_pre, w_down)
+    )(residual, ffn_gain, hits, grad_all, w_pre, w_down)
+
+
+def path_scalars(parents_ref, segment):
+    path = [segment]
+    for _ in range(LEVELS - 1):
+        last = path[-1]
+        parent = parents_ref[jnp.maximum(last, 0)]
+        path.append(jnp.where(last >= 0, parent, -1))
+    return path
+
+
+class PlaneGather:
+    def __init__(self, block, width, link_sems, core_sems):
+        self.block, self.link_sems, self.core_sems = block, link_sems, core_sems
+        place = lax.axis_index("dp")
+        self.x, self.y, self.corner = other(place, 2), other(place, 4), other(place, 6)
+        self.place = place
+        self.x_side, self.y_side = {"dp": self.x}, {"dp": self.y}
+        self.sibling = {"dp": other(place, 1)}
+        self.halves = (pl.ds(0, width // 2), pl.ds(width // 2, width - width // 2))
+
+    def copy(self, ref, sems, which, device):
+        return pltpu.make_async_remote_copy(
+            src_ref=ref,
+            dst_ref=ref,
+            send_sem=sems.at[0, which],
+            recv_sem=sems.at[1, which],
+            device_id=device,
+            device_id_type=MESH,
+        )
+
+    def direct(self):
+        own = self.block(self.place)
+        return [
+            self.copy(own, self.link_sems, 0, self.x_side),
+            self.copy(own, self.link_sems, 1, self.y_side),
+            self.copy(own, self.core_sems, 0, self.sibling),
+        ]
+
+    def forward(self):
+        return [
+            self.copy(self.block(self.x, self.halves[0]), self.link_sems, 2, self.y_side),
+            self.copy(self.block(self.y, self.halves[1]), self.link_sems, 3, self.x_side),
+            self.copy(self.block(self.x), self.core_sems, 1, self.sibling),
+            self.copy(self.block(self.y), self.core_sems, 2, self.sibling),
+        ]
+
+    def last(self):
+        return self.copy(self.block(self.corner), self.core_sems, 3, self.sibling)
+
+    def start(self):
+        for copy in self.direct():
+            copy.start()
+
+    def start_forward(self):
+        for copy in self.direct()[:2]:
+            copy.wait_recv()
+        for copy in self.forward():
+            copy.start()
+
+    def start_last(self):
+        for copy in self.forward()[:2]:
+            copy.wait_recv()
+        self.last().start()
+
+    def finish(self):
+        self.direct()[2].wait_recv()
+        for copy in self.forward()[2:]:
+            copy.wait_recv()
+        self.last().wait_recv()
+
+    def wait_sends(self):
+        for copy in self.direct() + self.forward() + [self.last()]:
+            copy.wait_send()
+
+
+def turn(values, cosine, sine):
+    heads = []
+    for begin in range(0, values.shape[1], HEAD_DIM):
+        head = values[:, begin : begin + HEAD_DIM]
+        heads.append(head * cosine + pltpu.roll(head, HEAD_DIM // 2, 1) * sine)
+    return jnp.concatenate(heads, 1)
+
+
+def front_kernel(
+    score_scale,
+    layout,
+    parents_ref,
+    hidden_ref,
+    gain_ref,
+    bias_ref,
+    freqs_ref,
+    hits_ref,
+    side_ref,
+    out_grad_ref,
+    w_query_ref,
+    w_key_ref,
+    w_value_ref,
+    w_out_ref,
+    e_gate_ref,
+    e_up_ref,
+    e_down_ref,
+    s_gate_ref,
+    s_up_ref,
+    s_down_ref,
+    residual_ref,
+    query_ref,
+    key_ref,
+    value_ref,
+    log_total_ref,
+    attended_ref,
+    normed_ref,
+    cosine_ref,
+    sine_ref,
+    hits_all_ref,
+    grad_all_ref,
+    w_pre_ref,
+    w_down_ref,
+    weights,
+    kv_all,
+    hits_all,
+    part_send,
+    part_z,
+    e_tiles,
+    s_tiles,
+    pre_tiles,
+    down_tiles,
+    load_sems,
+    tile_sems,
+    store_sems,
+    hit_sems,
+    part_sems,
+    kv_links,
+    kv_cores,
+    head_links,
+    head_cores,
+    tail_links,
+    tail_cores,
+):
+    shared_units, shared_pad, expert_units, experts, unit_pad = layout
+    bf16, f32 = jnp.bfloat16, jnp.float32
+    place, column = lax.axis_index("dp"), lax.axis_index("tensor")
+    tok_rows, width = hidden_ref.shape
+    rows = tok_rows // 4
+    local_width = w_query_ref.shape[1]
+    levels = [{"tensor": other(column, k)} for k in range(4)]
+    peers = [{"dp": other(place, j)} for j in range(8)]
+
+    loads = [
+        pltpu.make_async_copy(ref, weights.at[i], load_sems.at[i])
+        for i, ref in enumerate((w_query_ref, w_key_ref, w_value_ref, w_out_ref))
+    ]
+    own_grad = pltpu.make_async_copy(out_grad_ref, grad_all_ref.at[place], load_sems.at[4])
+    for copy in loads:
+        copy.start()
+    own_grad.start()
+    hits_all[place] = hits_ref[...]
+
+    barrier = pltpu.get_barrier_semaphore()
+    partners = peers[1:] + levels[1:]
+    for partner in partners:
+        pl.semaphore_signal(barrier, inc=1, device_id=partner, device_id_type=MESH)
+    pl.semaphore_wait(barrier, len(partners))
+
+    def grad_block(first, count):
+        def block(d, cols=slice(None)):
+            return grad_all_ref.at[d, pl.ds(first, count), :, cols]
+
+        return block
+
+    head_gather = PlaneGather(grad_block(0, 1), width, head_links, head_cores)
+    tail_gather = PlaneGather(grad_block(1, 3), width, tail_links, tail_cores)
+    kv_gather = PlaneGather(
+        lambda d, cols=slice(None): kv_all.at[d, :, cols], 2 * local_width, kv_links, kv_cores
+    )
+    own_grad.wait()
+    head_gather.start()
+
+    def hit_copy(j):
+        return pltpu.make_async_remote_copy(
+            src_ref=hits_all.at[place],
+            dst_ref=hits_all.at[place],
+            send_sem=hit_sems.at[0, j],
+            recv_sem=hit_sems.at[1, j],
+            device_id=peers[j],
+            device_id_type=MESH,
+        )
+
+    for j in range(1, 8):
+        hit_copy(j).start()
+
+    path = path_scalars(parents_ref, place)
+    depth = jnp.float32(-1.0)
+    for segment in path:
+        depth = depth + jnp.where(segment >= 0, 1.0, 0.0)
+    row_ids = lax.broadcasted_iota(jnp.int32, (tok_rows, HEAD_DIM), 0).astype(f32)
+    lane = lax.broadcasted_iota(jnp.int32, (tok_rows, HEAD_DIM), 1)
+    angles = (depth * SEG + row_ids) * freqs_ref[...]
+    cosine = jnp.cos(angles)
+    sine = jnp.where(lane < HEAD_DIM // 2, -1.0, 1.0) * jnp.sin(angles)
+    cosine_ref[...] = cosine
+    sine_ref[...] = sine
+    hidden_f = hidden_ref[...].astype(f32)
+    scale_rows = lax.rsqrt(jnp.mean(hidden_f * hidden_f, 1, keepdims=True) + epsilon)
+    normed_ref[...] = (hidden_f * scale_rows * gain_ref[...]).astype(bf16)
+    for copy in loads[1:3]:
+        copy.wait()
+    key = product(normed_ref[...], weights[1]) + bias_ref[1:2, :]
+    kv_all[place, :, :local_width] = turn(key, cosine, sine).astype(bf16)
+    value = product(normed_ref[...], weights[2]) + bias_ref[2:3, :]
+    kv_all[place, :, local_width:] = value.astype(bf16)
+    kv_gather.start()
+    loads[0].wait()
+    query = product(normed_ref[...], weights[0]) + bias_ref[0:1, :]
+    query_ref[...] = turn(query, cosine, sine).astype(bf16)
+
+    tile = e_tiles.shape[2]
+    shared_first = place * shared_units
+    span = s_tiles.shape[3]
+    shared_base = jnp.minimum(shared_first // 128 * 128, s_gate_ref.shape[1] - span)
+    shift = (span - (shared_first - shared_base)) % span
+
+    def tile_loads(i, slot):
+        window = pl.ds(pl.multiple_of(i * tile, tile), tile)
+        columns = pl.ds(pl.multiple_of(shared_base, 128), span)
+        copies = []
+        for j, ref in enumerate((e_gate_ref, e_up_ref, e_down_ref)):
+            copies.append(
+                pltpu.make_async_copy(ref.at[window], e_tiles.at[slot, j], tile_sems.at[slot, j])
+            )
+        for j, ref in enumerate((s_gate_ref, s_up_ref, s_down_ref)):
+            copies.append(
+                pltpu.make_async_copy(
+                    ref.at[window, columns], s_tiles.at[slot, j], tile_sems.at[slot, 3 + j]
+                )
+            )
+        return copies
+
+    def tile_stores(i, slot):
+        window = pl.ds(pl.multiple_of(i * tile, tile), tile)
+        return [
+            pltpu.make_async_copy(pre_tiles.at[slot], w_pre_ref.at[window], store_sems.at[slot, 0]),
+            pltpu.make_async_copy(
+                down_tiles.at[slot], w_down_ref.at[window], store_sems.at[slot, 1]
+            ),
+        ]
+
+    tiles = width // tile
+    whole = expert_units // 128 * 128
+    tail = expert_units - whole
+    shared_lane = lax.broadcasted_iota(jnp.int32, (tile, shared_pad), 1)
+    end_first = shared_pad + whole
+
+    def pack(i, carry):
+        slot = i % 2
+
+        @pl.when(i + 1 < tiles)
+        def _():
+            for copy in tile_loads(i + 1, (i + 1) % 2):
+                copy.start()
+
+        for copy in tile_loads(i, slot):
+            copy.wait()
+
+        @pl.when(i >= 2)
+        def _():
+            for copy in tile_stores(i - 2, slot):
+                copy.wait()
+
+        window = pl.ds(pl.multiple_of(i * tile, tile), tile)
+        for j, (target, first) in enumerate(
+            ((pre_tiles, 0), (pre_tiles, unit_pad), (down_tiles, 0))
+        ):
+            shared = pltpu.roll(s_tiles[slot, j].astype(f32), shift, 1)[:, :shared_pad]
+            shared = jnp.where(shared_lane < shared_units, shared, 0.0)
+            target[slot, :, first : first + shared_pad] = shared.astype(bf16)
+            target[slot, :, first + shared_pad : first + end_first] = e_tiles[slot, j, :, :whole]
+            end = e_tiles[slot, j, :, whole:].astype(f32)
+            end = jnp.concatenate([end, jnp.zeros((tile, 128 - tail), f32)], 1)
+            if j == 0:
+                end = end + side_ref[window, :].astype(f32)
+            target[slot, :, first + end_first : first + unit_pad] = end.astype(bf16)
+        for copy in tile_stores(i, slot):
+            copy.start()
+        return carry
+
+    for copy in tile_loads(0, 0):
+        copy.start()
+    lax.fori_loop(0, tiles // 2, pack, 0)
+    kv_gather.start_forward()
+    lax.fori_loop(tiles // 2, tiles, pack, 0)
+    kv_gather.start_last()
+    head_gather.start_forward()
+    for i in (tiles - 2, tiles - 1):
+        for copy in tile_stores(i, i % 2):
+            copy.wait()
+    kv_gather.finish()
+    tail_gather.start()
+
+    for level, segment in enumerate(path):
+        block = kv_all[jnp.maximum(segment, 0)]
+        key_ref[level * tok_rows : (level + 1) * tok_rows, :] = block[:, :local_width]
+        value_ref[level * tok_rows : (level + 1) * tok_rows, :] = block[:, local_width:]
+    key_rows = key_ref.shape[0]
+    row_id = lax.broadcasted_iota(jnp.int32, (tok_rows, key_rows), 0)
+    col_id = lax.broadcasted_iota(jnp.int32, (tok_rows, key_rows), 1)
+    allowed = row_id >= col_id
+    for level in range(1, LEVELS):
+        barred = jnp.where(path[level] >= 0, key_rows, 0)
+        inside = (col_id >= level * tok_rows) & (col_id < (level + 1) * tok_rows)
+        allowed = allowed | (inside & (col_id < barred))
+
+    def head(h, carry):
+        cols = pl.ds(pl.multiple_of(h * HEAD_DIM, HEAD_DIM), HEAD_DIM)
+        scores = product_nt(query_ref[:, cols], key_ref[:, cols]) * score_scale
+        scores = jnp.where(allowed, scores, -jnp.inf)
+        top = jnp.max(scores, 1, keepdims=True)
+        powers = jnp.exp(scores - top)
+        total = jnp.sum(powers, 1, keepdims=True)
+        log_total_ref[h] = top + jnp.log(total)
+        probs = (powers * (1.0 / total)).astype(bf16)
+        attended_ref[:, cols] = product(probs, value_ref[:, cols]).astype(bf16)
+        return carry
+
+    lax.fori_loop(0, local_width // HEAD_DIM, head, 0)
+
+    loads[3].wait()
+    for quarter in range(4):
+        mine = slice(quarter * rows, (quarter + 1) * rows)
+        part_send[quarter] = product_nt(attended_ref[mine, :], weights[3]).astype(bf16)
+
+    def part_copy(k):
+        return pltpu.make_async_remote_copy(
+            src_ref=part_send.at[other(column, k)],
+            dst_ref=part_z.at[k],
+            send_sem=part_sems.at[0, k],
+            recv_sem=part_sems.at[1, k],
+            device_id=levels[k],
+            device_id_type=MESH,
+        )
+
+    for k in (3, 2, 1):
+        part_copy(k).start()
+    head_gather.start_last()
+    tail_gather.start_forward()
+    attn = part_send[column].astype(f32)
+    for k in (1, 2, 3):
+        part_copy(k).wait_recv()
+        attn = attn + part_z[k].astype(f32)
+    own_rows = pl.ds(pl.multiple_of(column * rows, rows), rows)
+    residual_ref[...] = hidden_ref[own_rows, :].astype(f32) + attn
+    tail_gather.start_last()
+    head_gather.finish()
+    for j in range(1, 8):
+        hit_copy(j).wait_recv()
+    hits_all_ref[...] = hits_all[...]
+    tail_gather.finish()
+
+    for gather in (kv_gather, head_gather, tail_gather):
+        gather.wait_sends()
+    for j in range(1, 8):
+        hit_copy(j).wait_send()
+    for k in (1, 2, 3):
+        part_copy(k).wait_send()
+
+
+def front_layer(score_scale, layout, operands):
+    shared_units, shared_pad, expert_units, experts, unit_pad = layout
+    hidden, w_query = operands[1], operands[8]
+    tok_rows, width = hidden.shape
+    rows, local_width = tok_rows // 4, w_query.shape[1]
+    heads = local_width // HEAD_DIM
+    tile, span = 256, 384
+    bf16, f32 = jnp.bfloat16, jnp.float32
+    shape = jax.ShapeDtypeStruct
+    vmem, anywhere = pl.BlockSpec(memory_space=pltpu.VMEM), pl.BlockSpec(memory_space=pl.ANY)
+    smem = pl.BlockSpec(memory_space=pltpu.SMEM)
+    dma = pltpu.SemaphoreType.DMA
+    return pl.pallas_call(
+        functools.partial(front_kernel, score_scale, layout),
+        out_shape=[
+            shape((rows, width), f32),
+            shape((tok_rows, local_width), bf16),
+            shape((LEVELS * tok_rows, local_width), bf16),
+            shape((LEVELS * tok_rows, local_width), bf16),
+            shape((heads, tok_rows, 1), f32),
+            shape((tok_rows, local_width), bf16),
+            shape((tok_rows, width), bf16),
+            shape((tok_rows, HEAD_DIM), f32),
+            shape((tok_rows, HEAD_DIM), f32),
+            shape((8, 16, tok_rows), f32),
+            shape((8, 4, rows, width), bf16),
+            shape((width, 2 * unit_pad), bf16),
+            shape((width, unit_pad), bf16),
+        ],
+        in_specs=[smem] + [vmem] * 6 + [anywhere] * 11,
+        out_specs=[vmem] * 10 + [anywhere] * 3,
+        scratch_shapes=[
+            pltpu.VMEM((4, width, local_width), bf16),
+            pltpu.VMEM((8, tok_rows, 2 * local_width), bf16),
+            pltpu.VMEM((8, 16, tok_rows), f32),
+            pltpu.VMEM((4, rows, width), bf16),
+            pltpu.VMEM((4, rows, width), bf16),
+            pltpu.VMEM((2, 3, tile, expert_units), bf16),
+            pltpu.VMEM((2, 3, tile, span), bf16),
+            pltpu.VMEM((2, tile, 2 * unit_pad), bf16),
+            pltpu.VMEM((2, tile, unit_pad), bf16),
+            dma((5,)),
+            dma((2, 6)),
+            dma((2, 2)),
+            dma((2, 8)),
+            dma((2, 4)),
+        ]
+        + [dma((2, 4))] * 6,
+        compiler_params=pltpu.CompilerParams(
+            collective_id=2, has_side_effects=True, vmem_limit_bytes=56 * 2**20
+        ),
+        cost_estimate=pl.CostEstimate(
+            flops=2 * 2**31, bytes_accessed=40 * 2**20, transcendentals=2**21
+        ),
+    )(*operands)
 
 
 class PlaneSum:
@@ -929,8 +1360,7 @@
     query_ref,
     key_ref,
     value_ref,
-    level_mask_ref,
-    level_spots_ref,
+    parents_ref,
     log_total_ref,
     attended_ref,
     normed_ref,
@@ -1063,14 +1493,19 @@
     key_rows = key_ref.shape[0]
     row_id = lax.broadcasted_iota(jnp.int32, (tok_rows, key_rows), 0)
     col_id = lax.broadcasted_iota(jnp.int32, (tok_rows, key_rows), 1)
+    path = path_scalars(parents_ref, place)
+    allowed = row_id >= col_id
+    for level in range(1, LEVELS):
+        barred = jnp.where(path[level] >= 0, key_rows, 0)
+        inside = (col_id >= level * tok_rows) & (col_id < (level + 1) * tok_rows)
+        allowed = allowed | (inside & (col_id < barred))
 
     def head(h, carry):
         cols = pl.ds(pl.multiple_of(h * HEAD_DIM, HEAD_DIM), HEAD_DIM)
         value_cols = pl.ds(pl.multiple_of(local_width + h * HEAD_DIM, HEAD_DIM), HEAD_DIM)
         query, key, value = query_ref[:, cols], key_ref[:, cols], value_ref[:, cols]
         grad = attended_grad[:, cols]
-        scores = product_nt(query, key) * score_scale + level_mask_ref[...]
-        scores = jnp.where((col_id >= tok_rows) | (row_id >= col_id), scores, -jnp.inf)
+        scores = jnp.where(allowed, product_nt(query, key) * score_scale, -jnp.inf)
         weights = jnp.exp(scores - log_total_ref[h])
         weight_grad = product_nt(grad, value)
         center = jnp.sum(weights * weight_grad, 1, keepdims=True)
@@ -1091,7 +1526,7 @@
         segment = 4 * y + 2 * x + c
         total = jnp.zeros((tok_rows, 2 * local_width), f32)
         for level in range(1, LEVELS):
-            spot = level_spots_ref[segment * LEVELS + level]
+            spot = jnp.where(path[level] == segment, 1.0, 0.0)
             total = total + spot * kv_path[level * tok_rows : (level + 1) * tok_rows].astype(f32)
         kv_sums[c, y, x] = total.astype(bf16)
         return c
@@ -1308,8 +1743,7 @@
         query,
         key,
         value,
-        level_mask,
-        level_spots,
+        parents,
         log_total,
         attended,
         normed,
@@ -1344,7 +1778,7 @@
             shape((16, HEAD_DIM), f32),
         ],
         in_specs=[vmem, vmem, vmem, anywhere, anywhere, vmem]
-        + [vmem] * 4
+        + [vmem] * 3
         + [smem]
         + [vmem] * 7
         + [anywhere] * 4,
@@ -1393,7 +1827,7 @@
     )(*operands)
 
 
-def on_device(
+def on_slice(
     hidden_in,
     out_grad,
     parents,
@@ -1510,103 +1944,6 @@
     hidden_own = lax.dynamic_slice_in_dim(hidden_in, column * part_rows, part_rows, 0)
     grad_own = lax.dynamic_slice_in_dim(out_grad, column * part_rows, part_rows, 0)
     layout = (shared_units, shared_pad, expert_units, experts, units_pad)
-    cube = devices == 8 and columns == 4
-    if cube and all_rows * model_width <= 2**22:
-        kept_own = jnp.sum(jnp.where(jnp.arange(experts)[None, :] == place, kept, 0.0), 1)
-        kept_own = kept_own.reshape(2, 2, 2, columns, part_rows).transpose(3, 2, 0, 1, 4)
-        (
-            residual,
-            residual_grad,
-            residual_low,
-            ffn_part,
-            grad_expert_gate,
-            grad_expert_up,
-            grad_expert_down,
-            grad_shared,
-            small,
-        ) = ffn_layer(
-            attn_part.reshape(columns, part_rows, model_width),
-            hidden_own,
-            grad_own,
-            ffn_gain[None, :],
-            kept_own.reshape(columns, 2, 4 * part_rows, 1),
-            out_all.reshape(2, 2, 2, columns, part_rows, model_width),
-            w_pre,
-            w_down,
-            layout,
-        )
-        spots = jnp.where(reachable[None, :], path[None, :], -1) == jnp.arange(devices)[:, None]
-        level_mask = jnp.repeat(jnp.where(reachable, 0.0, -jnp.inf), tok_rows)[None, :]
-        sign = jnp.where(jnp.arange(HEAD_DIM) < HEAD_DIM // 2, -1.0, 1.0)
-        (
-            hidden_out,
-            hidden_in_grad,
-            sum_query,
-            sum_key,
-            sum_value,
-            sum_out,
-            shared_grads,
-            small,
-            bias_sums,
-        ) = back_layer(
-            score_scale,
-            experts + 2,
-            (
-                residual,
-                residual_grad,
-                residual_low,
-                ffn_part,
-                grad_shared,
-                small,
-                query_rot,
-                key_path,
-                value_path,
-                level_mask,
-                spots.astype(f32).reshape(-1),
-                log_total,
-                attended_low,
-                attn_normed,
-                hidden_in,
-                attn_gain[None, :],
-                cosine[:, 0],
-                sine[:, 0] * sign[None, :],
-                w_out,
-                w_query,
-                w_key,
-                w_value,
-            ),
-        )
-        hidden_out = hidden_out.reshape(tok_rows, model_width)
-        hidden_in_grad = hidden_in_grad.reshape(tok_rows, model_width)
-        small = small.T
-        bias_sums = lax.dynamic_slice_in_dim(
-            bias_sums[: 3 * b_query.shape[0]].reshape(3, *b_query.shape),
-            place * (HEAD_DIM // devices),
-            HEAD_DIM // devices,
-            2,
-        )
-        return (
-            hidden_out,
-            hidden_in_grad,
-            small[:, experts + 2],
-            sum_query,
-            sum_key,
-            sum_value,
-            bias_sums[0],
-            bias_sums[1],
-            bias_sums[2],
-            sum_out,
-            small[:, experts + 1],
-            small[:, :experts],
-            small[:, experts],
-            shared_grads[0],
-            shared_grads[1],
-            shared_grads[2],
-            grad_expert_gate[None],
-            grad_expert_up[None],
-            grad_expert_down[None],
-        )
-
     (
         residual,
         residual_grad,
@@ -1693,6 +2030,187 @@
         grad_expert_up[None],
         grad_expert_down[None],
     )
+
+
+def on_cube(
+    hidden_in,
+    out_grad,
+    parents,
+    routes,
+    attn_gain,
+    w_query,
+    w_key,
+    w_value,
+    b_query,
+    b_key,
+    b_value,
+    w_out,
+    ffn_gain,
+    w_router,
+    shared_gate,
+    shared_w_gate,
+    shared_w_up,
+    shared_w_down,
+    expert_w_gate,
+    expert_w_up,
+    expert_w_down,
+):
+    tok_rows, model_width = hidden_in.shape
+    devices, columns = lax.axis_size("dp"), lax.axis_size("tensor")
+    place = lax.axis_index("dp")
+    experts, top_count = w_router.shape[1], routes.shape[1]
+    capacity = 5 * tok_rows * top_count // 4
+    score_scale = HEAD_DIM ** (-0.5)
+    bf16, f32 = jnp.bfloat16, jnp.float32
+    expert_units = expert_w_gate.shape[2]
+    shared_units = shared_w_gate.shape[1] // devices
+    shared_pad = -(-shared_units // 128) * 128
+    units = shared_pad + expert_units
+    units_pad = -(-(units + experts + 1) // 128) * 128
+    layout = (shared_units, shared_pad, expert_units, experts, units_pad)
+    part_rows = tok_rows // columns
+
+    side_first = units - (units_pad - 128)
+    side = jnp.pad(
+        jnp.concatenate([w_router, shared_gate[:, None]], 1),
+        ((0, 0), (side_first, 128 - side_first - experts - 1)),
+    )
+    hits = jnp.any(
+        routes.T[:, None, :] == jnp.arange(16, dtype=jnp.int32)[None, :, None], 0
+    ).astype(f32)
+    freqs = rope_base ** (-jnp.arange(0, HEAD_DIM, 2, dtype=f32) / HEAD_DIM)
+    biases = jnp.stack([b_query.reshape(-1), b_key.reshape(-1), b_value.reshape(-1)])
+    (
+        residual,
+        query_rot,
+        key_path,
+        value_path,
+        log_total,
+        attended,
+        attn_normed,
+        cosine,
+        sine,
+        hits_all,
+        grad_all,
+        w_pre,
+        w_down,
+    ) = front_layer(
+        score_scale,
+        layout,
+        (
+            parents,
+            hidden_in,
+            attn_gain[None, :],
+            biases,
+            jnp.concatenate([freqs, freqs])[None, :],
+            hits,
+            side,
+            out_grad.reshape(columns, part_rows, model_width),
+            w_query,
+            w_key,
+            w_value,
+            w_out,
+            expert_w_gate[0],
+            expert_w_up[0],
+            expert_w_down[0],
+            shared_w_gate,
+            shared_w_up,
+            shared_w_down,
+        ),
+    )
+    (
+        residual_grad,
+        residual_low,
+        ffn_part,
+        grad_expert_gate,
+        grad_expert_up,
+        grad_expert_down,
+        grad_shared,
+        small,
+    ) = ffn_layer(
+        residual,
+        ffn_gain[None, :],
+        hits_all,
+        grad_all.reshape(2, 2, 2, columns, part_rows, model_width),
+        w_pre,
+        w_down,
+        layout,
+        capacity,
+    )
+    (
+        hidden_out,
+        hidden_in_grad,
+        sum_query,
+        sum_key,
+        sum_value,
+        sum_out,
+        shared_grads,
+        small,
+        bias_sums,
+    ) = back_layer(
+        score_scale,
+        experts + 2,
+        (
+            residual,
+            residual_grad,
+            residual_low,
+            ffn_part,
+            grad_shared,
+            small,
+            query_rot,
+            key_path,
+            value_path,
+            parents,
+            log_total,
+            attended,
+            attn_normed,
+            hidden_in,
+            attn_gain[None, :],
+            cosine,
+            sine,
+            w_out,
+            w_query,
+            w_key,
+            w_value,
+        ),
+    )
+    small = small.T
+    bias_sums = lax.dynamic_slice_in_dim(
+        bias_sums[: 3 * b_query.shape[0]].reshape(3, *b_query.shape),
+        place * (HEAD_DIM // devices),
+        HEAD_DIM // devices,
+        2,
+    )
+    return (
+        hidden_out.reshape(tok_rows, model_width),
+        hidden_in_grad.reshape(tok_rows, model_width),
+        small[:, experts + 2],
+        sum_query,
+        sum_key,
+        sum_value,
+        bias_sums[0],
+        bias_sums[1],
+        bias_sums[2],
+        sum_out,
+        small[:, experts + 1],
+        small[:, :experts],
+        small[:, experts],
+        shared_grads[0],
+        shared_grads[1],
+        shared_grads[2],
+        grad_expert_gate[None],
+        grad_expert_up[None],
+        grad_expert_down[None],
+    )
+
+
+def on_device(*arrays):
+    devices, columns = lax.axis_size("dp"), lax.axis_size("tensor")
+    tok_rows, model_width = arrays[0].shape
+    cube = devices == 8 and columns == 4 and tok_rows == SEG
+    if cube and tok_rows * devices * model_width <= 2**22:
+        return on_cube(*arrays)
+    return on_slice(*arrays)
 
 
 def solution(mesh):

time: 449 us -> 397 us (0.88); the launches traced: 441 us -> 396 us
  Pallas kernels: 289 us -> 365 us
  waiting for transfers between devices: 36.3 us -> 0 us
  local copies, waits for them, and re-layouts: 59.3 us -> 28.2 us
  between operations: 17.6 us -> 0.79 us
  other arithmetic: 15.7 us -> 1.85 us
  matrix products: 12.7 us -> 0 us
  blocking collectives: 10.5 us -> 0 us
    pallas_call x0 -> x1, Pallas kernels: none -> 102 us  [front_layer(): pl.pallas_call(functools.partial(front_kernel, score_scale, layout), out_...]
    all_gather x2 -> x0, waiting for transfers between devices: 35.6 us -> none  [gather_dp(): return lax.all_gather(rows, 'dp', axis=0, tiled=True)]
    pallas_call x1, Pallas kernels: 132 us -> 107 us  [ffn_layer(): pl.pallas_call(functools.partial(ffn_kernel, (shared_units, shared_pad, e...]
    dynamic_slice x7 -> x0, local copies, waits for them, and re-layouts: 13.1 us -> none  [the longest x2 5.99 us: own_units(): lax.dynamic_slice_in_dim(matrix, place * shared_units, shared_units, 1)]
    dot_general x7 -> x0, matrix products: 12.7 us -> none  [the longest x1 4.22 us: attend_forward(): jnp.einsum('hqk,khd->qhd', weights, heads_of(value_path), preferred_eleme...]
    all_gather x1 -> x0, blocking collectives: 10.5 us -> none  [on_device(): routes_all = lax.all_gather(routes, 'dp', axis=0, tiled=True)]
    concatenate x6 -> x1, other arithmetic: 6.34 us -> 0.01 us  [on_cube(): jnp.concatenate([w_router, shared_gate[:, None]], 1)]
    unnamed x67 -> x46, local copies, waits for them, and re-layouts: 24.5 us -> 20.6 us
  transfers between devices with their start and end apart: 2 -> 0, of which waited for: 1 -> 0; matrix products, arithmetic and copies ran while one was open for 10% -> 0% of each run, Pallas kernels for 0% -> 0%
where the time goes in v4:
time: 397 us; the launch traced here: 396 us
  Pallas kernels  365 us (92%)
  local copies, waits for them, and re-layouts  28.2 us (7%)
    pallas_call x1, Pallas kernels, back_layer(): pl.pallas_call(functools.partial(back_kernel, score_scale, gain_row), out...  156 us
    pallas_call x1, Pallas kernels, ffn_layer(): pl.pallas_call(functools.partial(ffn_kernel, (shared_units, shared_pad, e...  107 us
    pallas_call x1, Pallas kernels, front_layer(): pl.pallas_call(functools.partial(front_kernel, score_scale, layout), out_...  102 us
    unnamed x46, local copies, waits for them, and re-layouts  20.6 us

profile of v4, /device:TPU:0, one launch (start us, length us, event | category | flops | bytes accessed | tf_op | source)
XLA Modules:
  0.0 396.3 jit_solution(8910235262602849827)
XLA Ops:
  0.7 0.0 copy-start.2
  0.7 2.7 copy.63
  3.3 0.0 copy-done.2
  3.3 1.6 copy.64
  4.9 0.0 copy-done.3
  4.9 0.0 copy-start.14
  4.9 0.0 copy-start.15
  4.9 0.0 copy-start.16
  4.9 1.6 copy.65
  6.5 0.0 copy-done.12
  6.5 0.0 copy-done.9
  6.5 0.3 copy.62
  6.8 1.0 pad.4.side_ref
  7.9 0.0 copy-done.13
  7.9 0.6 convert_element_type.5.hits_ref
  8.5 0.0 copy-done.14
  8.5 0.0 copy-done.15
  8.5 0.0 copy-done.16
  8.5 0.6 pad_maximum_fusion.1.bias_ref
  9.1 0.6 maximum_bitcast_fusion.freqs_ref
  9.7 102.3 %shard_map.348 = (f32[64,2048]{1,0:T(8,128)}, bf16[256,512]{1,0:T(8,128)(2,1)}, bf16[1024,512]{1,0:T(8,128)(2,1)}, bf16[1024,512]{1,0:T(8,128)(2,1)}, f32[4,256,...) custom-call(s32[8]{0:T(128)} %parents_ref.3, ...), custom_call_target="tpu_custom_call" | custom-call | flops 4294967296 | bytes 41943040 | tf_op jit(solution)/shard_map/pallas_call | solution.py:1176
  112.0 107.5 %shard_map.349 = (f32[64,2048]{1,0:T(8,128)}, bf16[64,2048]{1,0:T(8,128)(2,1)}, bf16[4,2,2,2,64,2048]{5,4,3,2,1,0:T(8,128)(2,1)}, f32[2048,352]{1,0:T(8,128)}, f...) custom-call(f32[64,2048]{1,0:T(8,128)} %get-tuple-element.49.residual_ref, ...), custom_call_target="tpu_custom_call" | custom-call | flops 51539607552 | bytes 62914560 | tf_op jit(solution)/shard_map/pallas_call | solution.py:746
  219.5 155.7 %shard_map.350 = (bf16[4,64,2048]{2,1,0:T(8,128)(2,1)}, bf16[4,64,2048]{2,1,0:T(8,128)(2,1)}, f32[256,512]{1,0:T(8,128)}, f32[256,512]{1,0:T(8,128)}, f32[256,51...) custom-call(f32[64,2048]{1,0:T(8,128)} %get-tuple-element.49.residual_ref, ...), custom_call_target="tpu_custom_call" | custom-call | flops 25769803776 | bytes 41943040 | tf_op jit(solution)/shard_map/pallas_call | solution.py:1767
  375.2 0.0 copy-start.10
  375.2 0.0 copy-start.11
  375.2 0.0 copy-start.1
  375.2 4.5 %slice_bitcast_fusion = (f32[256,1408]{1,0:T(8,128)}, f32[256,1408]{1,0:T(8,128)}, f32[256,1408]{1,0:T(8,128)}) fusion(f32[3,256,1408]{2,1,0:T(8,128)} %get-tuple-element.75), kind=kLoop, calls=%fused_computation | loop fusion | bytes 8650752 | tf_op jit(solution)/shard_map/squeeze | solution.py:2200
  379.7 0.0 copy-done.10
  379.8 0.7 dynamic-slice_bitcast_fusion
  380.4 0.0 copy-done.11
  380.4 0.6 slice.46
  381.0 0.6 fusion.1
  381.6 0.0 copy-done.1
  381.6 2.3 copy.66
  383.9 3.6 copy.67
  387.5 0.0 copy-done
  387.5 2.3 copy.68
  389.7 2.5 copy.75
  392.2 0.0 copy-done.4
  392.2 1.0 copy.76
  393.2 0.0 copy-done.8
  393.2 0.8 copy.77
  393.9 0.0 copy-done.7
  394.0 0.8 copy.78
  394.7 0.0 copy-done.6
  394.7 0.8 copy.79
  395.5 0.0 copy-done.5
  395.5 0.8 copy.80
  (15 shorter events, 0.1 us)
Async XLA Ops:
  0.7 2.7 copy-start.2
  3.3 1.6 copy-start.3
  4.9 1.6 copy-start.12
  4.9 1.6 copy-start.9
  4.9 3.0 copy-start.13
  4.9 3.6 copy-start.14
  4.9 3.6 copy-start.15
  4.9 3.6 copy-start.16
  375.2 4.6 %copy-start.10 = (f32[16,128]{1,0:T(8,128)S(1)}, f32[16,128]{1,0:T(8,128)}, u32[]{:S(2)}) copy-start(f32[16,128]{1,0:T(8,128)} %get-tuple-element.73) | copy-start | bytes 24580
  375.2 5.2 %copy-start.11 = (f32[16,256]{1,0:T(8,128)S(1)}, f32[16,256]{1,0:T(8,128)}, u32[]{:S(2)}) copy-start(f32[16,256]{1,0:T(8,128)} %get-tuple-element.69) | copy-start | bytes 49156
  375.2 6.4 %copy-start.1 = (f32[2048,352]{1,0:T(8,128)S(1)}, f32[2048,352]{1,0:T(8,128)}, u32[]{:S(2)}) copy-start(f32[2048,352]{1,0:T(8,128)} %get-tuple-element.76) | copy-start | bytes 8650756
  383.9 3.6 copy-start
  389.7 2.5 copy-start.4
  389.7 3.4 copy-start.8
  389.7 4.2 %copy-start.7 = (f32[256,512]{1,0:T(8,128)S(1)}, f32[256,512]{1,0:T(8,128)}, u32[]{:S(2)}) copy-start(f32[256,512]{1,0:T(8,128)} %get-tuple-element.187) | copy-start | bytes 1572868
  392.2 2.6 copy-start.6
  392.2 3.4 copy-start.5

commit v5 on v4

--- a/solution.py
+++ b/solution.py
@@ -266,8 +266,11 @@
     gain_ref,
     hits_ref,
     grad_all_ref,
-    w_pre_ref,
-    w_down_ref,
+    side_ref,
+    shared_w_ref,
+    e_gate_w_ref,
+    e_up_w_ref,
+    e_down_w_ref,
     res_grad_ref,
     res_low_ref,
     ffn_part_ref,
@@ -282,6 +285,7 @@
     w_down,
     both_all,
     scaled_all,
+    scaled_now,
     sums,
     got_core,
     got_x1,
@@ -329,14 +333,31 @@
             device_id_type=MESH,
         )
 
-    load_pre = pltpu.make_async_copy(w_pre_ref, w_pre, load_sems.at[0])
-    load_down = pltpu.make_async_copy(w_down_ref, w_down, load_sems.at[1])
-    load_pre.start()
-    load_down.start()
+    expert_first, side_first = shared_pad, shared_pad + expert_units
+    loads = []
+    for j, (target, first, ref) in enumerate(
+        ((w_pre, 0, e_gate_w_ref), (w_pre, unit_pad, e_up_w_ref), (w_down, 0, e_down_w_ref))
+    ):
+        own_rows = pl.ds(first + expert_first, expert_units)
+        shared_rows = pl.ds(first, shared_units)
+        loads += [
+            pltpu.make_async_copy(ref, target.at[own_rows], load_sems.at[8 + 2 * j]),
+            pltpu.make_async_copy(
+                shared_w_ref.at[j], target.at[shared_rows], load_sems.at[9 + 2 * j]
+            ),
+        ]
+    for copy in loads:
+        copy.start()
+    for target, first in ((w_pre, 0), (w_pre, unit_pad), (w_down, 0)):
+        gap = shared_pad - shared_units
+        target[first + shared_units : first + shared_pad, :] = jnp.zeros((gap, width), bf16)
+        rest = unit_pad - side_first
+        target[first + side_first : first + unit_pad, :] = jnp.zeros((rest, width), bf16)
+    w_pre[side_first : side_first + side_ref.shape[0], :] = side_ref[...]
 
     def load_grad(c, z):
         return pltpu.make_async_copy(
-            grad_all_ref.at[:, :, c, z], dy_all.at[z, c], load_sems.at[2 + c * 4 + z]
+            grad_all_ref.at[:, :, c, z], dy_all.at[z, c], load_sems.at[c * 4 + z]
         )
 
     for c in range(2):
@@ -518,8 +539,8 @@
                 z * rows : (z + 1) * rows, d : d + 1
             ]
 
-    load_pre.wait()
-    load_down.wait()
+    for copy in loads:
+        copy.wait()
     for c in range(2):
         for z in range(4):
             load_grad(c, z).wait()
@@ -545,15 +566,15 @@
         z = level_of(k)
         row_block = rows_all[z, c].reshape(4 * rows, width)
         dy_block = dy_all[z, c].reshape(4 * rows, width)
-        pre_gate = product(row_block, w_pre[:, :unit_pad])
-        pre_up = product(row_block, w_pre[:, unit_pad:])
-        down_back = product(dy_block, w_down[...])
+        pre_gate = product_nt(row_block, w_pre[:unit_pad])
+        pre_up = product_nt(row_block, w_pre[unit_pad:])
+        down_back = product_nt(dy_block, w_down[...])
         probs, shared_weight = routing(pre_gate[:, last:])
         kept = kept_ref[z, c]
         gate = (
             jnp.sum(jnp.where(lane == first_lane + place, probs, 0.0), 1, keepdims=True) * kept
         )
-        dots = []
+        dots, scaled, gate_rows, up_rows = [], [], [], []
         for begin, end, weight in (
             (0, shared_pad, shared_weight),
             (shared_pad, unit_pad, gate),
@@ -564,16 +585,20 @@
             silu = a * sig
             hidden = (silu * b).astype(bf16).astype(f32)
             dots.append(jnp.sum(hidden * back, 1, keepdims=True))
-            scaled_all[z, c, :, begin:end] = (hidden * weight).astype(bf16)
+            scaled.append((hidden * weight).astype(bf16))
             grad = back * weight
-            both_all[z, c, :, unit_pad + begin : unit_pad + end] = (grad * silu).astype(bf16)
-            both_all[z, c, :, begin:end] = (
-                grad * b * sig * (1.0 + a * (1.0 - sig))
-            ).astype(bf16)
+            up_rows.append((grad * silu).astype(bf16))
+            gate_rows.append((grad * b * sig * (1.0 + a * (1.0 - sig))).astype(bf16))
+        both = jnp.concatenate(gate_rows + up_rows, 1)
+        own_scaled = jnp.concatenate(scaled, 1)
+        first_token = pl.multiple_of((2 * z + c) * 4 * rows, 4 * rows)
+        both_all[:, pl.ds(first_token, 4 * rows)] = both.T
+        scaled_all[:, pl.ds(first_token, 4 * rows)] = own_scaled.T
+        scaled_now[c] = own_scaled
         dot_block = jnp.where(is_shared, dots[0], 0.0) + jnp.where(
             lane == first_lane + place, dots[1] * kept, 0.0
         )
-        normed_grad = product_nt(both_all[z, c], w_pre[...]).astype(bf16)
+        normed_grad = product(both, w_pre[...]).astype(bf16)
         sums[k, c, :, :, :, 0:width] = normed_grad.reshape(2, 2, rows, width)
         sums[k, c, :, :, :, width:wide] = dot_block.astype(bf16).reshape(2, 2, rows, wide - width)
 
@@ -615,7 +640,7 @@
             store_chunk(k - 1, 1).wait()
 
         def outputs(c, carry):
-            part = product_nt(scaled_all[level_of(k), c], w_down[...]).astype(bf16)
+            part = product(scaled_now[c], w_down[...]).astype(bf16)
 
             @pl.when(c == 1)
             def _():
@@ -642,15 +667,15 @@
     lax.fori_loop(0, 4, chunk, 0)
     store_chunk(3, 1).wait()
 
-    tile = tile_gate.shape[1]
+    tile = tile_gate.shape[2]
     tiles = width // tile
 
     def tile_copies(i, slot):
         window = pl.ds(pl.multiple_of(i * tile, tile), tile)
         return [
-            pltpu.make_async_copy(tile_gate.at[slot], e_gate_ref.at[window], tile_sems.at[slot, 0]),
-            pltpu.make_async_copy(tile_up.at[slot], e_up_ref.at[window], tile_sems.at[slot, 1]),
-            pltpu.make_async_copy(tile_down.at[slot], e_down_ref.at[window], tile_sems.at[slot, 2]),
+            pltpu.make_async_copy(tile_gate.at[slot], e_gate_ref.at[:, window], tile_sems.at[slot, 0]),
+            pltpu.make_async_copy(tile_up.at[slot], e_up_ref.at[:, window], tile_sems.at[slot, 1]),
+            pltpu.make_async_copy(tile_down.at[slot], e_down_ref.at[:, window], tile_sems.at[slot, 2]),
             pltpu.make_async_copy(
                 tile_shared.at[slot], shared_ref.at[i], tile_sems.at[slot, 3]
             ),
@@ -668,16 +693,15 @@
 
         window = pl.ds(pl.multiple_of(i * tile, tile), tile)
         expert = slice(shared_pad, shared_pad + expert_units)
-        lhs = rows_all[:, :, :, :, :, window].reshape(tokens, tile)
-        grad = product_tn(lhs, both_all[...].reshape(tokens, 2 * unit_pad))
-        tile_gate[slot] = grad[:, expert]
-        tile_shared[slot, 0] = grad[:, :shared_pad].T[:shared_units].astype(bf16)
-        tile_up[slot] = grad[:, unit_pad + shared_pad : unit_pad + shared_pad + expert_units]
-        tile_shared[slot, 1] = grad[:, unit_pad : unit_pad + shared_pad].T[:shared_units].astype(bf16)
-        lhs = dy_all[:, :, :, :, :, window].reshape(tokens, tile)
-        grad = product_tn(lhs, scaled_all[...].reshape(tokens, unit_pad))
-        tile_down[slot] = grad[:, expert]
-        tile_shared[slot, 2] = grad[:, :shared_pad].T[:shared_units].astype(bf16)
+        row_tile = rows_all[:, :, :, :, :, window].reshape(tokens, tile)
+        for j, (first, target) in enumerate(((0, tile_gate), (unit_pad, tile_up))):
+            grad = product(both_all[first : first + unit_pad], row_tile).astype(bf16)
+            target[slot] = grad[expert]
+            tile_shared[slot, j] = grad[:shared_units]
+        dy_tile = dy_all[:, :, :, :, :, window].reshape(tokens, tile)
+        grad = product(scaled_all[...], dy_tile).astype(bf16)
+        tile_down[slot] = grad[expert]
+        tile_shared[slot, 2] = grad[:shared_units]
         for copy in tile_copies(i, slot):
             copy.start()
 
@@ -703,15 +727,15 @@
     dots = total[:, width:]
     unit = residual_ref[...] * scale_rows
     own_normed = rows_all[column, core, north, east]
-    side_w = w_pre[:, last:unit_pad]
-    probs, shared_weight = routing(product(own_normed, side_w))
+    side_w = w_pre[last:unit_pad]
+    probs, shared_weight = routing(product_nt(own_normed, side_w))
     router_dots = jnp.where(in_router, dots, 0.0)
     center = jnp.sum(probs * router_dots, 1, keepdims=True)
     side = jnp.where(in_router, probs * (router_dots - center), 0.0) + jnp.where(
         is_shared, dots * shared_weight * (1.0 - shared_weight), 0.0
     )
     side = side.astype(bf16)
-    normed_grad = total[:, :width] + product_nt(side, side_w)
+    normed_grad = total[:, :width] + product(side, side_w)
     side_rows = product_tn(side, own_normed)
     small_ref[...] = side_rows[first_lane : first_lane + small_ref.shape[0]]
     small_ref[experts + 1 : experts + 2, :] = jnp.sum(normed_grad * unit, 0, keepdims=True)
@@ -730,7 +754,7 @@
             copy.wait_send()
 
 
-def ffn_layer(residual, ffn_gain, hits, grad_all, w_pre, w_down, layout, capacity):
+def ffn_layer(residual, ffn_gain, hits, grad_all, side, shared_w, expert_w, layout, capacity):
     shared_units, shared_pad, expert_units, experts, unit_pad = layout
     rows, width = residual.shape
     bf16, f32 = jnp.bfloat16, jnp.float32
@@ -752,21 +776,22 @@
             shape((rows, width), f32),
             shape((rows, width), bf16),
             shape((4, 2, 2, 2, rows, width), bf16),
-            shape((width, expert_units), f32),
-            shape((width, expert_units), f32),
-            shape((width, expert_units), f32),
+            shape((expert_units, width), bf16),
+            shape((expert_units, width), bf16),
+            shape((expert_units, width), bf16),
             shape((width // tile, 3, shared_units, tile), bf16),
             shape((16, width), f32),
         ],
-        in_specs=[vmem, vmem, vmem, anywhere, anywhere, anywhere],
+        in_specs=[vmem, vmem, vmem, anywhere, vmem] + [anywhere] * 4,
         out_specs=[vmem, vmem] + [anywhere] * 5 + [vmem],
         scratch_shapes=[
             pltpu.VMEM((4, 2, 2, 2, rows, width), bf16),
             pltpu.VMEM((4, 2, 2, 2, rows, width), bf16),
-            pltpu.VMEM(w_pre.shape, bf16),
-            pltpu.VMEM(w_down.shape, bf16),
-            pltpu.VMEM((4, 2, 4 * rows, 2 * unit_pad), bf16),
-            pltpu.VMEM((4, 2, 4 * rows, unit_pad), bf16),
+            pltpu.VMEM((2 * unit_pad, width), bf16),
+            pltpu.VMEM((unit_pad, width), bf16),
+            pltpu.VMEM((2 * unit_pad, 32 * rows), bf16),
+            pltpu.VMEM((unit_pad, 32 * rows), bf16),
+            pltpu.VMEM((2, 4 * rows, unit_pad), bf16),
             pltpu.VMEM((4, 2, 2, 2, rows, wide), bf16),
             pltpu.VMEM((4, 2, 2, rows, wide), bf16),
             pltpu.VMEM((4, 2, rows, half), bf16),
@@ -776,11 +801,11 @@
             pltpu.VMEM((4, rows, wide), bf16),
             pltpu.VMEM((4, 2, 4 * rows, 1), f32),
             pltpu.VMEM((2, 2, rows, width), bf16),
-            pltpu.VMEM((2, tile, expert_units), f32),
-            pltpu.VMEM((2, tile, expert_units), f32),
-            pltpu.VMEM((2, tile, expert_units), f32),
+            pltpu.VMEM((2, expert_units, tile), bf16),
+            pltpu.VMEM((2, expert_units, tile), bf16),
+            pltpu.VMEM((2, expert_units, tile), bf16),
             pltpu.VMEM((2, 3, shared_units, tile), bf16),
-            dma((10,)),
+            dma((14,)),
             dma((2,)),
             dma((2, 4)),
             dma((2, 4)),
@@ -794,7 +819,7 @@
             collective_id=0, has_side_effects=True, vmem_limit_bytes=63 * 2**20
         ),
         cost_estimate=cost,
-    )(residual, ffn_gain, hits, grad_all, w_pre, w_down)
+    )(residual, ffn_gain, hits, grad_all, side, shared_w, *expert_w)
 
 
 def path_scalars(parents_ref, segment):
@@ -804,6 +829,128 @@
         parent = parents_ref[jnp.maximum(last, 0)]
         path.append(jnp.where(last >= 0, parent, -1))
     return path
+
+
+class Line:
+    def __init__(self, sems):
+        self.sems = sems
+        self.column = lax.axis_index("tensor")
+        self.levels = [{"tensor": other(self.column, k)} for k in range(4)]
+        self.outer = (self.column % 3) == 0
+        self.inner = (self.column % 3) != 0
+
+    def remote(self, src, dst, send, receive, device):
+        return pltpu.make_async_remote_copy(
+            src_ref=src,
+            dst_ref=dst,
+            send_sem=self.sems.at[0, send],
+            recv_sem=self.sems.at[1, receive],
+            device_id=device,
+            device_id_type=MESH,
+        )
+
+
+class LineGather(Line):
+    def __init__(self, slot, sems):
+        super().__init__(sems)
+        self.slot = slot
+
+    def own(self, k):
+        ref = self.slot(self.column)
+        return self.remote(ref, ref, k, k, self.levels[k])
+
+    def passed(self):
+        ref = self.slot(other(self.column, 2))
+        return self.remote(ref, ref, 0, 3, self.levels[1])
+
+    def start(self):
+        self.own(2).start()
+        self.own(1).start()
+
+        @pl.when(self.inner)
+        def _():
+            self.own(3).start()
+
+    def forward(self):
+        self.own(2).wait_recv()
+
+        @pl.when(self.inner)
+        def _():
+            self.passed().start()
+
+    def finish(self):
+        self.own(1).wait_recv()
+        self.own(3).wait_recv()
+
+    def wait_sends(self):
+        self.own(1).wait_send()
+        self.own(2).wait_send()
+
+        @pl.when(self.inner)
+        def _():
+            self.own(3).wait_send()
+            self.passed().wait_send()
+
+
+class LineSum(Line):
+    def __init__(self, part, got, sems):
+        super().__init__(sems)
+        self.part, self.got = part, got
+
+    def own(self, k):
+        part = self.part(other(self.column, k))
+        return self.remote(part, self.got.at[k], k, k, self.levels[k])
+
+    def passed(self):
+        part = self.part(other(self.column, 3))
+        return self.remote(part, self.got.at[0], 0, 0, self.levels[1])
+
+    def start(self):
+        @pl.when(self.outer)
+        def _():
+            self.passed().start()
+            self.own(2).start()
+            self.got[3] = jnp.zeros(self.got.shape[1:], self.got.dtype)
+
+        @pl.when(self.inner)
+        def _():
+            self.own(3).start()
+
+        self.own(1).start()
+
+    def forward(self):
+        @pl.when(self.inner)
+        def _():
+            self.passed().wait_recv()
+            part = self.part(other(self.column, 2))
+            total = part[...].astype(jnp.float32) + self.got[0].astype(jnp.float32)
+            part[...] = total.astype(part.dtype)
+            self.own(2).start()
+
+    def finish(self):
+        self.own(1).wait_recv()
+        self.own(2).wait_recv()
+
+        @pl.when(self.inner)
+        def _():
+            self.own(3).wait_recv()
+
+        total = self.part(self.column)[...].astype(jnp.float32)
+        for k in (1, 2, 3):
+            total = total + self.got[k].astype(jnp.float32)
+        return total
+
+    def wait_sends(self):
+        self.own(1).wait_send()
+        self.own(2).wait_send()
+
+        @pl.when(self.outer)
+        def _():
+            self.passed().wait_send()
+
+        @pl.when(self.inner)
+        def _():
+            self.own(3).wait_send()
 
 
 class PlaneGather:
@@ -881,22 +1028,18 @@
 
 def front_kernel(
     score_scale,
-    layout,
+    shared_units,
     parents_ref,
     hidden_ref,
     gain_ref,
     bias_ref,
     freqs_ref,
     hits_ref,
-    side_ref,
     out_grad_ref,
     w_query_ref,
     w_key_ref,
     w_value_ref,
     w_out_ref,
-    e_gate_ref,
-    e_up_ref,
-    e_down_ref,
     s_gate_ref,
     s_up_ref,
     s_down_ref,
@@ -911,17 +1054,14 @@
     sine_ref,
     hits_all_ref,
     grad_all_ref,
-    w_pre_ref,
-    w_down_ref,
+    shared_ref,
     weights,
     kv_all,
     hits_all,
     part_send,
     part_z,
-    e_tiles,
     s_tiles,
-    pre_tiles,
-    down_tiles,
+    t_tiles,
     load_sems,
     tile_sems,
     store_sems,
@@ -934,7 +1074,6 @@
     tail_links,
     tail_cores,
 ):
-    shared_units, shared_pad, expert_units, experts, unit_pad = layout
     bf16, f32 = jnp.bfloat16, jnp.float32
     place, column = lax.axis_index("dp"), lax.axis_index("tensor")
     tok_rows, width = hidden_ref.shape
@@ -1011,42 +1150,32 @@
     query = product(normed_ref[...], weights[0]) + bias_ref[0:1, :]
     query_ref[...] = turn(query, cosine, sine).astype(bf16)
 
-    tile = e_tiles.shape[2]
+    tile, span = s_tiles.shape[2:]
     shared_first = place * shared_units
-    span = s_tiles.shape[3]
     shared_base = jnp.minimum(shared_first // 128 * 128, s_gate_ref.shape[1] - span)
-    shift = (span - (shared_first - shared_base)) % span
+    shared_skip = shared_first - shared_base
 
     def tile_loads(i, slot):
         window = pl.ds(pl.multiple_of(i * tile, tile), tile)
         columns = pl.ds(pl.multiple_of(shared_base, 128), span)
-        copies = []
-        for j, ref in enumerate((e_gate_ref, e_up_ref, e_down_ref)):
-            copies.append(
-                pltpu.make_async_copy(ref.at[window], e_tiles.at[slot, j], tile_sems.at[slot, j])
+        return [
+            pltpu.make_async_copy(
+                ref.at[window, columns], s_tiles.at[slot, j], tile_sems.at[slot, j]
             )
-        for j, ref in enumerate((s_gate_ref, s_up_ref, s_down_ref)):
-            copies.append(
-                pltpu.make_async_copy(
-                    ref.at[window, columns], s_tiles.at[slot, j], tile_sems.at[slot, 3 + j]
-                )
-            )
-        return copies
+            for j, ref in enumerate((s_gate_ref, s_up_ref, s_down_ref))
+        ]
 
     def tile_stores(i, slot):
         window = pl.ds(pl.multiple_of(i * tile, tile), tile)
+        units = pl.ds(pl.multiple_of(shared_skip, 16), shared_units)
         return [
-            pltpu.make_async_copy(pre_tiles.at[slot], w_pre_ref.at[window], store_sems.at[slot, 0]),
             pltpu.make_async_copy(
-                down_tiles.at[slot], w_down_ref.at[window], store_sems.at[slot, 1]
-            ),
+                t_tiles.at[slot, j, units], shared_ref.at[j, :, window], store_sems.at[slot, j]
+            )
+            for j in range(3)
         ]
 
     tiles = width // tile
-    whole = expert_units // 128 * 128
-    tail = expert_units - whole
-    shared_lane = lax.broadcasted_iota(jnp.int32, (tile, shared_pad), 1)
-    end_first = shared_pad + whole
 
     def pack(i, carry):
         slot = i % 2
@@ -1064,19 +1193,8 @@
             for copy in tile_stores(i - 2, slot):
                 copy.wait()
 
-        window = pl.ds(pl.multiple_of(i * tile, tile), tile)
-        for j, (target, first) in enumerate(
-            ((pre_tiles, 0), (pre_tiles, unit_pad), (down_tiles, 0))
-        ):
-            shared = pltpu.roll(s_tiles[slot, j].astype(f32), shift, 1)[:, :shared_pad]
-            shared = jnp.where(shared_lane < shared_units, shared, 0.0)
-            target[slot, :, first : first + shared_pad] = shared.astype(bf16)
-            target[slot, :, first + shared_pad : first + end_first] = e_tiles[slot, j, :, :whole]
-            end = e_tiles[slot, j, :, whole:].astype(f32)
-            end = jnp.concatenate([end, jnp.zeros((tile, 128 - tail), f32)], 1)
-            if j == 0:
-                end = end + side_ref[window, :].astype(f32)
-            target[slot, :, first + end_first : first + unit_pad] = end.astype(bf16)
+        for j in range(3):
+            t_tiles[slot, j] = s_tiles[slot, j].T
         for copy in tile_stores(i, slot):
             copy.start()
         return carry
@@ -1126,24 +1244,12 @@
         mine = slice(quarter * rows, (quarter + 1) * rows)
         part_send[quarter] = product_nt(attended_ref[mine, :], weights[3]).astype(bf16)
 
-    def part_copy(k):
-        return pltpu.make_async_remote_copy(
-            src_ref=part_send.at[other(column, k)],
-            dst_ref=part_z.at[k],
-            send_sem=part_sems.at[0, k],
-            recv_sem=part_sems.at[1, k],
-            device_id=levels[k],
-            device_id_type=MESH,
-        )
-
-    for k in (3, 2, 1):
-        part_copy(k).start()
+    line = LineSum(lambda z: part_send.at[z], part_z, part_sems)
+    line.start()
     head_gather.start_last()
+    line.forward()
     tail_gather.start_forward()
-    attn = part_send[column].astype(f32)
-    for k in (1, 2, 3):
-        part_copy(k).wait_recv()
-        attn = attn + part_z[k].astype(f32)
+    attn = line.finish()
     own_rows = pl.ds(pl.multiple_of(column * rows, rows), rows)
     residual_ref[...] = hidden_ref[own_rows, :].astype(f32) + attn
     tail_gather.start_last()
@@ -1157,13 +1263,11 @@
         gather.wait_sends()
     for j in range(1, 8):
         hit_copy(j).wait_send()
-    for k in (1, 2, 3):
-        part_copy(k).wait_send()
-
-
-def front_layer(score_scale, layout, operands):
-    shared_units, shared_pad, expert_units, experts, unit_pad = layout
-    hidden, w_query = operands[1], operands[8]
+    line.wait_sends()
+
+
+def front_layer(score_scale, shared_units, operands):
+    hidden, w_query = operands[1], operands[7]
     tok_rows, width = hidden.shape
     rows, local_width = tok_rows // 4, w_query.shape[1]
     heads = local_width // HEAD_DIM
@@ -1174,7 +1278,7 @@
     smem = pl.BlockSpec(memory_space=pltpu.SMEM)
     dma = pltpu.SemaphoreType.DMA
     return pl.pallas_call(
-        functools.partial(front_kernel, score_scale, layout),
+        functools.partial(front_kernel, score_scale, shared_units),
         out_shape=[
             shape((rows, width), f32),
             shape((tok_rows, local_width), bf16),
@@ -1187,24 +1291,21 @@
             shape((tok_rows, HEAD_DIM), f32),
             shape((8, 16, tok_rows), f32),
             shape((8, 4, rows, width), bf16),
-            shape((width, 2 * unit_pad), bf16),
-            shape((width, unit_pad), bf16),
+            shape((3, shared_units, width), bf16),
         ],
-        in_specs=[smem] + [vmem] * 6 + [anywhere] * 11,
-        out_specs=[vmem] * 10 + [anywhere] * 3,
+        in_specs=[smem] + [vmem] * 6 + [anywhere] * 7,
+        out_specs=[vmem] * 10 + [anywhere] * 2,
         scratch_shapes=[
             pltpu.VMEM((4, width, local_width), bf16),
             pltpu.VMEM((8, tok_rows, 2 * local_width), bf16),
             pltpu.VMEM((8, 16, tok_rows), f32),
             pltpu.VMEM((4, rows, width), bf16),
             pltpu.VMEM((4, rows, width), bf16),
-            pltpu.VMEM((2, 3, tile, expert_units), bf16),
             pltpu.VMEM((2, 3, tile, span), bf16),
-            pltpu.VMEM((2, tile, 2 * unit_pad), bf16),
-            pltpu.VMEM((2, tile, unit_pad), bf16),
+            pltpu.VMEM((2, 3, span, tile), bf16),
             dma((5,)),
-            dma((2, 6)),
-            dma((2, 2)),
+            dma((2, 3)),
+            dma((2, 3)),
             dma((2, 8)),
             dma((2, 4)),
         ]
@@ -1378,7 +1479,7 @@
     grad_key_ref,
     grad_value_ref,
     grad_out_ref,
-    grad_shared_ref,
+    shared_got,
     small_out_ref,
     bias_out_ref,
     low_all,
@@ -1395,7 +1496,6 @@
     part_send,
     part_z,
     hidden_stage,
-    shared_got,
     shared_stage,
     small_send,
     small_got,
@@ -1434,6 +1534,8 @@
         pltpu.make_async_copy(w_out_ref, w_qkv.at[2], load_sems.at[4]),
     ]
     load_value = pltpu.make_async_copy(w_value_ref, w_qkv.at[2], load_sems.at[7])
+    load_shared = pltpu.make_async_copy(shared_ref.at[place], shared_stage, load_sems.at[9])
+    load_shared.start()
     for z in range(4):
         load_out(z).start()
     for copy in loads:
@@ -1449,34 +1551,136 @@
         lambda k: out_mine.at[k], lambda k: ffn_part_ref.at[k, flip(core)], *out_scr
     )
     kv_sum = PlaneSum(
-        lambda k: kv_sums.at[core], lambda k: kv_sums.at[flip(core)], *kv_scr
+        lambda k: kv_sums.at[k, core], lambda k: kv_sums.at[k, flip(core)], *kv_scr
     )
     w_sum = PlaneSum(
         lambda k: w_sums.at[k, core], lambda k: w_sums.at[k, flip(core)], *w_scr
     )
     wkv_sum = PlaneSum(
-        lambda k: kv_sums.at[core], lambda k: kv_sums.at[flip(core)], *kv_scr[:5], *wkv_sems
+        lambda k: kv_sums.at[k, core],
+        lambda k: kv_sums.at[k, flip(core)],
+        *kv_scr[:5],
+        *wkv_sems,
     )
 
     low_all[column] = res_low_ref[...]
-    own_low = low_all.at[column]
-    low_copies = [remote(own_low, own_low, low_sems, (k,), levels[k]) for k in (3, 2, 1)]
-    for copy in low_copies:
-        copy.start()
-    for z in range(4):
+    low_line = LineGather(lambda z: low_all.at[z], low_sems)
+    low_line.start()
+    order = [other(column, k) for k in (1, 3, 2, 0)]
+    for z in order:
         out_sum.start(z)
+    kv_path[...] = jnp.zeros(kv_path.shape, f32)
     for z in range(4):
         load_out(z).wait()
+    for z in order:
         out_sum.after_core(z)
     for copy in loads:
         copy.wait()
-    for copy in low_copies:
-        copy.wait_recv()
-
-    low_rows = low_all[...].reshape(tok_rows, width)
-    attended_grad[...] = product(low_rows, w_qkv[2]).astype(bf16)
+
+    out_line = LineSum(lambda z: out_mine.at[z, north, east], out_z, out_sems)
+    low_line.forward()
+
+    half_rows = tok_rows // 2
+    key_rows = key_ref.shape[0]
+    row_id = lax.broadcasted_iota(jnp.int32, (half_rows, key_rows), 0)
+    col_id = lax.broadcasted_iota(jnp.int32, (half_rows, key_rows), 1)
+    path = path_scalars(parents_ref, place)
+    reached = col_id < 0
+    for level in range(1, LEVELS):
+        barred = jnp.where(path[level] >= 0, key_rows, 0)
+        inside = (col_id >= level * tok_rows) & (col_id < (level + 1) * tok_rows)
+        reached = reached | (inside & (col_id < barred))
+
+    def half(i, carry):
+        pair = (column // 2 + i) % 2
+        first = pl.multiple_of(pair * half_rows, half_rows)
+        window = pl.ds(first, half_rows)
+
+        @pl.when(i == 0)
+        def _():
+            low_line.own(1).wait_recv()
+
+        @pl.when(i == 1)
+        def _():
+            low_line.own(3).wait_recv()
+
+        low_rows = low_all[pl.ds(2 * pair, 2)].reshape(half_rows, width)
+        attended_grad[window, :] = product(low_rows, w_qkv[2]).astype(bf16)
+        allowed = (row_id + first >= col_id) | reached
+
+        def head(h, carry):
+            cols = pl.ds(pl.multiple_of(h * HEAD_DIM, HEAD_DIM), HEAD_DIM)
+            value_cols = pl.ds(pl.multiple_of(local_width + h * HEAD_DIM, HEAD_DIM), HEAD_DIM)
+            query, key, value = query_ref[window, cols], key_ref[:, cols], value_ref[:, cols]
+            grad = attended_grad[window, cols]
+            scores = jnp.where(allowed, product_nt(query, key) * score_scale, -jnp.inf)
+            weights = jnp.exp(scores - log_total_ref[h, window])
+            weight_grad = product_nt(grad, value)
+            center = jnp.sum(weights * weight_grad, 1, keepdims=True)
+            score_grad = (weights * (weight_grad - center)).astype(bf16)
+            query_grad[window, cols] = product(score_grad, key) * score_scale
+            kv_path[:, cols] += product_tn(score_grad, query) * score_scale
+            kv_path[:, value_cols] += product_tn(weights.astype(bf16), grad)
+            return carry
+
+        lax.fori_loop(0, local_width // HEAD_DIM, head, 0)
+
+        @pl.when(i == 0)
+        def _():
+            out_sum.after_first(order[0])
+
+        return carry
+
+    lax.fori_loop(0, 2, half, 0)
+    for z in order[1:]:
+        out_sum.after_first(z)
     load_value.start()
 
+    part_rows = rows // 2
+
+    def kv_blocks(i, c):
+        which, y, x = i // 4, (i // 2) % 2, i % 2
+        segment = 4 * y + 2 * x + c
+        total = jnp.zeros((4, part_rows, 2 * local_width), f32)
+        for level in range(1, LEVELS):
+            spot = jnp.where(path[level] == segment, 1.0, 0.0)
+            total = total + spot * kv_rows(level, which)
+        kv_sums[which, c, y, x] = total.reshape(4 * part_rows, 2 * local_width).astype(bf16)
+        return c
+
+    def kv_rows(level, which):
+        rows_view = kv_path.at[level * tok_rows : (level + 1) * tok_rows]
+        pieces = []
+        for z in range(4):
+            start = pl.multiple_of(z * rows + which * part_rows, part_rows)
+            pieces.append(rows_view[pl.ds(start, part_rows), :])
+        return jnp.stack(pieces)
+
+    lax.fori_loop(0, 4, kv_blocks, flip(core))
+    kv_sum.start(0)
+    lax.fori_loop(4, 8, kv_blocks, flip(core))
+    kv_sum.start(1)
+    lax.fori_loop(0, 8, kv_blocks, core)
+    for which in range(2):
+        own_kv = kv_sums.at[which, core, north, east]
+        added = own_kv[...].astype(f32) + kv_rows(0, which).reshape(4 * part_rows, -1)
+        own_kv[...] = added.astype(bf16)
+        kv_sum.after_core(which)
+
+    def bias_of(which, grad, begin):
+        bias = jnp.sum(grad.astype(f32), 0, keepdims=True)
+        for h in range(local_width // HEAD_DIM):
+            spot = slice(4 * which + h, 4 * which + h + 1)
+            added = bias[:, h * HEAD_DIM : (h + 1) * HEAD_DIM]
+            if not begin:
+                added = added + small_send[0, spot, 2 * HEAD_DIM :]
+            small_send[0, spot, 2 * HEAD_DIM :] = added
+
+    small_send[0, :, 2 * HEAD_DIM :] = jnp.zeros((16, HEAD_DIM), f32)
+    query_pre = unturn(query_grad[...], cosine_ref[...], sine_ref[...]).astype(bf16)
+    pre_grads[0] = query_pre.reshape(4, 2, part_rows, local_width)
+    bias_of(0, query_pre, True)
+    part[...] = product_nt(query_pre, w_qkv[0]).reshape(4, 2, part_rows, width)
     def block_index(place_of):
         return place_of % 2, place_of // 4, (place_of // 2) % 2
 
@@ -1487,126 +1691,88 @@
         w_sums[0, c, y, x] = product_tn(lhs, attended_ref[...]).astype(bf16)
         return carry
 
-    lax.fori_loop(0, 8, out_weights, 0)
-    w_sum.start(0)
-
-    key_rows = key_ref.shape[0]
-    row_id = lax.broadcasted_iota(jnp.int32, (tok_rows, key_rows), 0)
-    col_id = lax.broadcasted_iota(jnp.int32, (tok_rows, key_rows), 1)
-    path = path_scalars(parents_ref, place)
-    allowed = row_id >= col_id
-    for level in range(1, LEVELS):
-        barred = jnp.where(path[level] >= 0, key_rows, 0)
-        inside = (col_id >= level * tok_rows) & (col_id < (level + 1) * tok_rows)
-        allowed = allowed | (inside & (col_id < barred))
-
-    def head(h, carry):
-        cols = pl.ds(pl.multiple_of(h * HEAD_DIM, HEAD_DIM), HEAD_DIM)
-        value_cols = pl.ds(pl.multiple_of(local_width + h * HEAD_DIM, HEAD_DIM), HEAD_DIM)
-        query, key, value = query_ref[:, cols], key_ref[:, cols], value_ref[:, cols]
-        grad = attended_grad[:, cols]
-        scores = jnp.where(allowed, product_nt(query, key) * score_scale, -jnp.inf)
-        weights = jnp.exp(scores - log_total_ref[h])
-        weight_grad = product_nt(grad, value)
-        center = jnp.sum(weights * weight_grad, 1, keepdims=True)
-        score_grad = (weights * (weight_grad - center)).astype(bf16)
-        query_grad[:, cols] = product(score_grad, key) * score_scale
-        kv_path[:, cols] = (product_tn(score_grad, query) * score_scale).astype(bf16)
-        kv_path[:, value_cols] = product_tn(weights.astype(bf16), grad).astype(bf16)
-        return carry
-
-    lax.fori_loop(0, 2, head, 0)
-    for z in range(4):
-        out_sum.after_first(z)
-    w_sum.after_core(0)
-    lax.fori_loop(2, 4, head, 0)
-
-    def kv_blocks(q, c):
-        y, x = q // 2, q % 2
-        segment = 4 * y + 2 * x + c
-        total = jnp.zeros((tok_rows, 2 * local_width), f32)
-        for level in range(1, LEVELS):
-            spot = jnp.where(path[level] == segment, 1.0, 0.0)
-            total = total + spot * kv_path[level * tok_rows : (level + 1) * tok_rows].astype(f32)
-        kv_sums[c, y, x] = total.astype(bf16)
-        return c
-
-    lax.fori_loop(0, 4, kv_blocks, flip(core))
-    kv_sum.start(0)
-    lax.fori_loop(0, 4, kv_blocks, core)
-    own_kv = kv_sums.at[core, north, east]
-    own_kv[...] = (own_kv[...].astype(f32) + kv_path[0:tok_rows].astype(f32)).astype(bf16)
-    kv_sum.after_core(0)
-
-    def cast_pre(which, grad):
-        low = grad.astype(bf16)
-        pre_grads[which] = low
-        bias = jnp.sum(low.astype(f32), 0, keepdims=True)
-        for h in range(local_width // HEAD_DIM):
-            small_send[0, 4 * which + h : 4 * which + h + 1, 2 * HEAD_DIM :] = bias[
-                :, h * HEAD_DIM : (h + 1) * HEAD_DIM
-            ]
-
-    small_send[0, :, 2 * HEAD_DIM :] = jnp.zeros((16, HEAD_DIM), f32)
-    cast_pre(0, unturn(query_grad[...], cosine_ref[...], sine_ref[...]))
-
     def query_weights(i, carry):
         c, y, x = block_index(i)
         window = pl.ds(pl.multiple_of(i * tok_rows, tok_rows), tok_rows)
-        w_sums[1, c, y, x] = product_tn(normed_ref[:, window], pre_grads[0]).astype(bf16)
+        rows_pre = pre_grads[0].reshape(tok_rows, local_width)
+        w_sums[1, c, y, x] = product_tn(normed_ref[:, window], rows_pre).astype(bf16)
         return carry
 
+    lax.fori_loop(0, 8, out_weights, 0)
+    w_sum.start(0)
     lax.fori_loop(0, 8, query_weights, 0)
     w_sum.start(1)
-    part[...] = product_nt(pre_grads[0], w_qkv[0])
     kv_sum.after_first(0)
-
-    def out_level(k):
-        return remote(
-            out_mine.at[other(column, k), north, east],
-            out_z.at[k],
-            out_sems,
-            (0, k),
-            levels[k],
-        )
-
-    w_sum.after_first(0)
-    for z in range(4):
+    kv_sum.after_first(1)
+    for z in order:
         out_sum.after_second(z)
-    for k in (3, 2, 1):
-        out_level(k).start()
-    w_sum.after_core(1)
-
-    own_kv = kv_sum.after_second(0)
-    cast_pre(1, unturn(own_kv[:, :local_width].astype(f32), cosine_ref[...], sine_ref[...]))
-    cast_pre(2, own_kv[:, local_width:].astype(f32))
+    out_line.start()
+
     load_value.wait()
-    for which in (1, 2):
-        part[...] += product_nt(pre_grads[which], w_qkv[which])
-
     hidden_f = hidden_ref[...].astype(f32)
     unit_scale = lax.rsqrt(jnp.mean(hidden_f * hidden_f, 1, keepdims=True) + epsilon)
-    part_send[...] = part[...].astype(bf16).reshape(4, rows, width)
-
-    def part_copy(k):
-        return remote(part_send.at[other(column, k)], part_z.at[k], part_sems, (k,), levels[k])
-
-    for k in (3, 2, 1):
-        part_copy(k).start()
-    attn_gain_row = jnp.sum(part[...] * (hidden_f * unit_scale), 0, keepdims=True)
-
-    kv_sum.wait_sends(0)
-
+
+    part_lines = [
+        LineSum(
+            lambda z, which=which: part_send.at[which, z],
+            part_z.at[which],
+            part_sems.at[which],
+        )
+        for which in range(2)
+    ]
+
+    for which in range(2):
+        own_kv = kv_sum.after_second(which)
+        cos_rows = cosine_ref[...].reshape(4, 2, part_rows, HEAD_DIM)[:, which]
+        sin_rows = sine_ref[...].reshape(4, 2, part_rows, HEAD_DIM)[:, which]
+        key_pre = unturn(
+            own_kv[:, :local_width].astype(f32),
+            cos_rows.reshape(4 * part_rows, HEAD_DIM),
+            sin_rows.reshape(4 * part_rows, HEAD_DIM),
+        ).astype(bf16)
+        value_pre = own_kv[:, local_width:]
+        pre_grads[1, :, which] = key_pre.reshape(4, part_rows, local_width)
+        pre_grads[2, :, which] = value_pre.reshape(4, part_rows, local_width)
+        bias_of(1, key_pre, which == 0)
+        bias_of(2, value_pre, which == 0)
+        added = product_nt(key_pre, w_qkv[1]) + product_nt(value_pre, w_qkv[2])
+        whole = part[:, which] + added.reshape(4, part_rows, width)
+        part[:, which] = whole
+        part_send[which] = whole.astype(bf16)
+        part_lines[which].start()
+        if which == 0:
+            out_line.forward()
+
+
+    def shared_copy(j):
+        return remote(
+            shared_ref.at[other(place, j)], shared_got.at[place], shared_sems, (j,), peers[j]
+        )
+
+    for k in range(2):
+        w_sum.after_core(k)
+    part_lines[0].forward()
+    attn_gain_row = jnp.sum(
+        part[...].reshape(tok_rows, width) * (hidden_f * unit_scale), 0, keepdims=True
+    )
     def key_value_weights(i, carry):
         c, y, x = block_index(i)
         window = pl.ds(pl.multiple_of(i * tok_rows, tok_rows), tok_rows)
         lhs = normed_ref[:, window]
-        kv_sums[c, y, x, :, :local_width] = product_tn(lhs, pre_grads[1]).astype(bf16)
-        kv_sums[c, y, x, :, local_width:] = product_tn(lhs, pre_grads[2]).astype(bf16)
+        for which, cols in ((1, slice(0, local_width)), (2, slice(local_width, None))):
+            rows_pre = pre_grads[which].reshape(tok_rows, local_width)
+            grad = product_tn(lhs, rows_pre).astype(bf16)
+            for k in range(2):
+                piece = slice(k * half_rows, (k + 1) * half_rows)
+                kv_sums[k, c, y, x, :, cols] = grad[piece]
         return carry
 
+    for k in range(2):
+        kv_sum.wait_sends(k)
     lax.fori_loop(0, 8, key_value_weights, 0)
-    wkv_sum.start(0)
+    for k in range(2):
+        wkv_sum.start(k)
+    part_lines[1].forward()
 
     bias_rows = small_send[0, :, 2 * HEAD_DIM :]
     for d in range(8):
@@ -1624,17 +1790,12 @@
     for j in range(1, 8):
         small_copy(j).start()
 
-    def shared_copy(j):
-        return remote(
-            shared_ref.at[other(place, j)], shared_got.at[place], shared_sems, (j,), peers[j]
-        )
-
+    w_sum.after_first(0)
+    for k in range(2):
+        wkv_sum.after_core(k)
     w_sum.after_first(1)
-    wkv_sum.after_core(0)
-    grad_out_ref[...] = w_sum.after_second(0)[...].astype(f32)
-    for j in (6, 7, 2, 3, 4, 5, 1):
-        shared_copy(j).start()
-    own_shared = pltpu.make_async_copy(shared_ref.at[place], shared_got.at[place], load_sems.at[8])
+    own_shared = pltpu.make_async_copy(shared_stage, shared_got.at[place], load_sems.at[8])
+    load_shared.wait()
     own_shared.start()
 
     total = small_send[place]
@@ -1650,83 +1811,74 @@
     for copy in small_levels:
         copy.start()
 
-    mine = pl.ds(pl.multiple_of(column * rows, rows), rows)
-    attn_grad = part_send[column].astype(f32)
-    for k in (1, 2, 3):
-        part_copy(k).wait_recv()
-        attn_grad = attn_grad + part_z[k].astype(f32)
-    own_hidden = hidden_ref[mine, :].astype(f32)
-    own_scale = lax.rsqrt(jnp.mean(own_hidden * own_hidden, 1, keepdims=True) + epsilon)
-    hidden_stage[0, column] = (
-        res_grad_ref[...] + norm_back(attn_grad, own_hidden * own_scale, own_scale, gain_ref[...])
-    ).astype(bf16)
-
-    def end_copy(which, k):
-        own = hidden_stage.at[which, column]
-        return remote(own, own, end_sems, (which, k), levels[k])
-
-    for k in (3, 2, 1):
-        end_copy(0, k).start()
-
-    out = residual_ref[...] + out_mine[column, north, east].astype(f32)
-    for k in (1, 2, 3):
-        out_level(k).wait_recv()
-        out = out + out_z[k].astype(f32)
-    hidden_stage[1, column] = out.astype(bf16)
-    for k in (3, 2, 1):
-        end_copy(1, k).start()
-
-    wkv_sum.after_first(0)
-    grad_query_ref[...] = w_sum.after_second(1)[...].astype(f32)
+    end_lines = [
+        LineGather(
+            lambda z, which=which, piece=piece: hidden_stage.at[which, z, piece],
+            end_sems.at[which, piece],
+        )
+        for which in range(2)
+        for piece in range(2)
+    ]
+
+    for which in range(2):
+        attn_grad = part_lines[which].finish()
+        start = pl.multiple_of(column * rows + which * part_rows, part_rows)
+        own_hidden = hidden_ref[pl.ds(start, part_rows), :].astype(f32)
+        own_scale = lax.rsqrt(jnp.mean(own_hidden * own_hidden, 1, keepdims=True) + epsilon)
+        own_grad = res_grad_ref[which * part_rows : (which + 1) * part_rows, :]
+        hidden_stage[0, column, which] = (
+            own_grad + norm_back(attn_grad, own_hidden * own_scale, own_scale, gain_ref[...])
+        ).astype(bf16)
+        end_lines[which].start()
+        if which == 0:
+            grad_out_ref[...] = w_sum.after_second(0)[...]
+            for k in range(2):
+                wkv_sum.after_first(k)
+            for j in (6, 7, 2, 3, 4, 5, 1):
+                shared_copy(j).start()
+
+    end_lines[0].forward()
+    out = residual_ref[...] + out_line.finish()
+    hidden_stage[1, column] = out.astype(bf16).reshape(2, part_rows, width)
+    end_lines[1].forward()
+    end_lines[2].start()
+    end_lines[3].start()
+
+    grad_query_ref[...] = w_sum.after_second(1)[...]
     for copy in small_levels:
         copy.wait_recv()
     small_out_ref[...] = (small_z[0] + small_z[1]) + (small_z[2] + small_z[3])
-    own_wkv = wkv_sum.after_second(0)
-    grad_key_ref[...] = own_wkv[:, :local_width].astype(f32)
-    grad_value_ref[...] = own_wkv[:, local_width:].astype(f32)
-
+    for k in range(2):
+        own_wkv = wkv_sum.after_second(k)
+        piece = slice(k * half_rows, (k + 1) * half_rows)
+        grad_key_ref[piece, :] = own_wkv[:, :local_width]
+        grad_value_ref[piece, :] = own_wkv[:, local_width:]
+
+    end_lines[2].forward()
+    end_lines[3].forward()
     own_shared.wait()
     for j in range(1, 8):
         shared_copy(j).wait_recv()
-
-    def store_shared(which):
-        return pltpu.make_async_copy(
-            shared_stage, grad_shared_ref.at[which], load_sems.at[9]
-        )
-
-    for which in range(3):
-        units = shared_got[:, which].astype(f32)
-        turned = units.reshape(-1, units.shape[-1]).T
-        if which:
-            store_shared(which - 1).wait()
-        shared_stage[...] = turned
-        store_shared(which).start()
-
-    for k in (1, 2, 3):
-        end_copy(0, k).wait_recv()
-        end_copy(1, k).wait_recv()
+    for line in end_lines:
+        line.finish()
     ends = [
         pltpu.make_async_copy(hidden_stage.at[0], hidden_grad_ref, load_sems.at[10]),
         pltpu.make_async_copy(hidden_stage.at[1], hidden_out_ref, load_sems.at[11]),
     ]
     for copy in ends:
         copy.start()
-    store_shared(2).wait()
     for copy in ends:
         copy.wait()
 
-    for copy in low_copies + small_levels:
+    for copy in small_levels:
         copy.wait_send()
+    for line in [low_line, out_line] + part_lines + end_lines:
+        line.wait_sends()
     for z in range(4):
         out_sum.wait_sends(z)
-    for k in (1, 2, 3):
-        out_level(k).wait_send()
-        part_copy(k).wait_send()
-        end_copy(0, k).wait_send()
-        end_copy(1, k).wait_send()
     for k in range(2):
         w_sum.wait_sends(k)
-    wkv_sum.wait_sends(0)
+        wkv_sum.wait_sends(k)
     for j in range(1, 8):
         small_copy(j).wait_send()
         shared_copy(j).wait_send()
@@ -1767,13 +1919,13 @@
     return pl.pallas_call(
         functools.partial(back_kernel, score_scale, gain_row),
         out_shape=[
-            shape((4, rows, width), bf16),
-            shape((4, rows, width), bf16),
-            shape((tok_rows, local_width), f32),
-            shape((tok_rows, local_width), f32),
-            shape((tok_rows, local_width), f32),
-            shape((tok_rows, local_width), f32),
-            shape((3, tok_rows, 8 * units), f32),
+            shape((4, 2, rows // 2, width), bf16),
+            shape((4, 2, rows // 2, width), bf16),
+            shape((tok_rows, local_width), bf16),
+            shape((tok_rows, local_width), bf16),
+            shape((tok_rows, local_width), bf16),
+            shape((tok_rows, local_width), bf16),
+            shape((8, 3, units, tok_rows), bf16),
             shape((16, tok_rows), f32),
             shape((16, HEAD_DIM), f32),
         ],
@@ -1782,38 +1934,37 @@
         + [smem]
         + [vmem] * 7
         + [anywhere] * 4,
-        out_specs=[anywhere] * 2 + [vmem] * 4 + [anywhere, vmem, vmem],
+        out_specs=[anywhere] * 2 + [vmem] * 4 + [anywhere] + [vmem] * 2,
         scratch_shapes=[
             pltpu.VMEM((4, rows, width), bf16),
             pltpu.VMEM((3, width, local_width), bf16),
             pltpu.VMEM((4, 2, 2, rows, width), bf16),
             pltpu.VMEM((4, rows, width), bf16),
-            pltpu.VMEM((2, 2, 2, tok_rows, 2 * local_width), bf16),
+            pltpu.VMEM((2, 2, 2, 2, tok_rows // 2, 2 * local_width), bf16),
             pltpu.VMEM((2, 2, 2, 2, tok_rows, local_width), bf16),
-            pltpu.VMEM((LEVELS * tok_rows, 2 * local_width), bf16),
+            pltpu.VMEM((LEVELS * tok_rows, 2 * local_width), f32),
             pltpu.VMEM((tok_rows, local_width), bf16),
             pltpu.VMEM((tok_rows, local_width), f32),
-            pltpu.VMEM((3, tok_rows, local_width), bf16),
-            pltpu.VMEM((tok_rows, width), f32),
-            pltpu.VMEM((4, rows, width), bf16),
-            pltpu.VMEM((4, rows, width), bf16),
-            pltpu.VMEM((2, 4, rows, width), bf16),
-            pltpu.VMEM((8, 3, units, tok_rows), bf16),
-            pltpu.VMEM((tok_rows, 8 * units), f32),
+            pltpu.VMEM((3, 4, 2, rows // 2, local_width), bf16),
+            pltpu.VMEM((4, 2, rows // 2, width), f32),
+            pltpu.VMEM((2, 4, rows // 2, width), bf16),
+            pltpu.VMEM((2, 4, rows // 2, width), bf16),
+            pltpu.VMEM((2, 4, 2, rows // 2, width), bf16),
+            pltpu.VMEM((3, units, tok_rows), bf16),
             pltpu.VMEM((8, 16, 2 * HEAD_DIM + HEAD_DIM), f32),
             pltpu.VMEM((8, 16, 2 * HEAD_DIM + HEAD_DIM), f32),
             pltpu.VMEM((4, 16, 2 * HEAD_DIM), f32),
         ]
         + plane_scratch(4, rows, width)
-        + plane_scratch(1, tok_rows, 2 * local_width)
+        + plane_scratch(2, tok_rows // 2, 2 * local_width)
         + plane_scratch(2, tok_rows, local_width)
-        + plane_scratch(1, tok_rows, 2 * local_width)[5:]
+        + plane_scratch(2, tok_rows // 2, 2 * local_width)[5:]
         + [
             dma((12,)),
             dma((2, 4)),
-            dma((2, 1, 4)),
             dma((2, 4)),
             dma((2, 2, 4)),
+            dma((2, 2, 2, 4)),
             dma((2, 8)),
             dma((2, 8)),
             dma((2, 4)),
@@ -2030,6 +2181,98 @@
         grad_expert_up[None],
         grad_expert_down[None],
     )
+
+
+def finish_kernel(
+    hidden_out_in,
+    hidden_grad_in,
+    query_in,
+    key_in,
+    value_in,
+    out_in,
+    shared_in,
+    gate_in,
+    up_in,
+    down_in,
+    small_in,
+    hidden_out,
+    hidden_grad,
+    query_out,
+    key_out,
+    value_out,
+    out_out,
+    s_gate_out,
+    s_up_out,
+    s_down_out,
+    gate_out,
+    up_out,
+    down_out,
+    router_out,
+    shared_gate_out,
+    ffn_gain_out,
+    attn_gain_out,
+):
+    f32 = jnp.float32
+    experts = router_out.shape[0]
+    hidden_out[...] = hidden_out_in[...]
+    hidden_grad[...] = hidden_grad_in[...]
+    for source, target in (
+        (query_in, query_out),
+        (key_in, key_out),
+        (value_in, value_out),
+        (out_in, out_out),
+        (gate_in, gate_out),
+        (up_in, up_out),
+        (down_in, down_out),
+    ):
+        target[...] = source[...].astype(f32)
+
+    @pl.when(pl.program_id(0) % 4 == 0)
+    def _():
+        for which, target in enumerate((s_gate_out, s_up_out, s_down_out)):
+            units = shared_in[:, which]
+            target[...] = units.reshape(-1, units.shape[-1]).T.astype(f32)
+
+    router_out[...] = small_in[0:experts]
+    shared_gate_out[...] = small_in[experts : experts + 1]
+    ffn_gain_out[...] = small_in[experts + 1 : experts + 2]
+    attn_gain_out[...] = small_in[experts + 2 : experts + 3]
+
+
+def finish_layer(hidden_out, hidden_grad, grads, shared, expert_grads, small, experts):
+    steps = 8
+    tok_rows, width = hidden_out.shape
+    local_width = grads[0].shape[1]
+    units = shared.shape[2]
+    expert_units = expert_grads[0].shape[0]
+    f32, bf16 = jnp.float32, jnp.bfloat16
+    shape = jax.ShapeDtypeStruct
+    row = lambda wide: pl.BlockSpec((tok_rows // steps, wide), lambda i: (i, 0))
+    column = pl.BlockSpec((expert_units, width // steps), lambda i: (0, i))
+    whole = lambda *dims: pl.BlockSpec(dims, lambda i: (0,) * len(dims))
+    return pl.pallas_call(
+        finish_kernel,
+        grid=(steps,),
+        in_specs=[row(width)] * 2
+        + [row(local_width)] * 4
+        + [pl.BlockSpec((8, 3, units, tok_rows // 2), lambda i: (0, 0, 0, i // 4))]
+        + [column] * 3
+        + [whole(16, tok_rows)],
+        out_specs=[row(width)] * 2
+        + [row(local_width)] * 4
+        + [pl.BlockSpec((tok_rows // 2, 8 * units), lambda i: (i // 4, 0))] * 3
+        + [column] * 3
+        + [whole(experts, tok_rows)]
+        + [whole(1, tok_rows)] * 3,
+        out_shape=[shape((tok_rows, width), bf16)] * 2
+        + [shape((tok_rows, local_width), f32)] * 4
+        + [shape((tok_rows, 8 * units), f32)] * 3
+        + [shape((expert_units, width), f32)] * 3
+        + [shape((experts, tok_rows), f32)]
+        + [shape((1, tok_rows), f32)] * 3,
+        compiler_params=pltpu.CompilerParams(vmem_limit_bytes=63 * 2**20),
+        cost_estimate=pl.CostEstimate(flops=0, bytes_accessed=26 * 2**20, transcendentals=0),
+    )(hidden_out, hidden_grad, *grads, shared, *expert_grads, small)
 
 
 def on_cube(
@@ -2070,10 +2313,8 @@
     layout = (shared_units, shared_pad, expert_units, experts, units_pad)
     part_rows = tok_rows // columns
 
-    side_first = units - (units_pad - 128)
     side = jnp.pad(
-        jnp.concatenate([w_router, shared_gate[:, None]], 1),
-        ((0, 0), (side_first, 128 - side_first - experts - 1)),
+        jnp.concatenate([w_router.T, shared_gate[None, :]], 0), ((0, 16 - experts - 1), (0, 0))
     )
     hits = jnp.any(
         routes.T[:, None, :] == jnp.arange(16, dtype=jnp.int32)[None, :, None], 0
@@ -2092,11 +2333,10 @@
         sine,
         hits_all,
         grad_all,
-        w_pre,
-        w_down,
+        shared_w,
     ) = front_layer(
         score_scale,
-        layout,
+        shared_units,
         (
             parents,
             hidden_in,
@@ -2104,15 +2344,11 @@
             biases,
             jnp.concatenate([freqs, freqs])[None, :],
             hits,
-            side,
             out_grad.reshape(columns, part_rows, model_width),
             w_query,
             w_key,
             w_value,
             w_out,
-            expert_w_gate[0],
-            expert_w_up[0],
-            expert_w_down[0],
             shared_w_gate,
             shared_w_up,
             shared_w_down,
@@ -2132,8 +2368,9 @@
         ffn_gain[None, :],
         hits_all,
         grad_all.reshape(2, 2, 2, columns, part_rows, model_width),
-        w_pre,
-        w_down,
+        side,
+        shared_w,
+        (expert_w_gate[0].T, expert_w_up[0].T, expert_w_down[0].T),
         layout,
         capacity,
     )
@@ -2144,7 +2381,7 @@
         sum_key,
         sum_value,
         sum_out,
-        shared_grads,
+        grad_shared,
         small,
         bias_sums,
     ) = back_layer(
@@ -2174,17 +2411,42 @@
             w_value,
         ),
     )
-    small = small.T
     bias_sums = lax.dynamic_slice_in_dim(
         bias_sums[: 3 * b_query.shape[0]].reshape(3, *b_query.shape),
         place * (HEAD_DIM // devices),
         HEAD_DIM // devices,
         2,
     )
-    return (
+    (
+        hidden_out,
+        hidden_in_grad,
+        sum_query,
+        sum_key,
+        sum_value,
+        sum_out,
+        sum_s_gate,
+        sum_s_up,
+        sum_s_down,
+        grad_expert_gate,
+        grad_expert_up,
+        grad_expert_down,
+        sum_router,
+        sum_shared_gate,
+        sum_ffn_gain,
+        sum_attn_gain,
+    ) = finish_layer(
         hidden_out.reshape(tok_rows, model_width),
         hidden_in_grad.reshape(tok_rows, model_width),
-        small[:, experts + 2],
+        (sum_query, sum_key, sum_value, sum_out),
+        grad_shared,
+        (grad_expert_gate, grad_expert_up, grad_expert_down),
+        small,
+        experts,
+    )
+    return (
+        hidden_out,
+        hidden_in_grad,
+        sum_attn_gain[0],
         sum_query,
         sum_key,
         sum_value,
@@ -2192,15 +2454,15 @@
         bias_sums[1],
         bias_sums[2],
         sum_out,
-        small[:, experts + 1],
-        small[:, :experts],
-        small[:, experts],
-        shared_grads[0],
-        shared_grads[1],
-        shared_grads[2],
-        grad_expert_gate[None],
-        grad_expert_up[None],
-        grad_expert_down[None],
+        sum_ffn_gain[0],
+        sum_router.T,
+        sum_shared_gate[0],
+        sum_s_gate,
+        sum_s_up,
+        sum_s_down,
+        grad_expert_gate.T[None],
+        grad_expert_up.T[None],
+        grad_expert_down.T[None],
     )
 
 

time: 397 us -> 336 us (0.85)
  Pallas kernels: 365 us -> 328 us
  local copies, waits for them, and re-layouts: 28.2 us -> 0.69 us
    pallas_call x1, Pallas kernels: 156 us -> 134 us  [back_layer(): pl.pallas_call(functools.partial(back_kernel, score_scale, gain_row), out...]
    unnamed x46 -> x6, local copies, waits for them, and re-layouts: 20.6 us -> 0.01 us
    pallas_call x1 -> x2, Pallas kernels: 102 us -> 84.2 us  [the longest x1 71.2 us: front_layer(): pl.pallas_call(functools.partial(front_kernel, score_scale, shared_units)...]
    squeeze x1 -> x0, local copies, waits for them, and re-layouts: 4.52 us -> none  [on_cube(): shared_grads[2]]
where the time goes in v5:
time: 336 us; the launch traced here: 334 us
  Pallas kernels  328 us (98%)
  other arithmetic  3.89 us (1%)
    pallas_call x1, Pallas kernels, back_layer(): pl.pallas_call(functools.partial(back_kernel, score_scale, gain_row), out...  134 us
    pallas_call x1, Pallas kernels, ffn_layer(): pl.pallas_call(functools.partial(ffn_kernel, (shared_units, shared_pad, e...  110 us
    pallas_call x1, Pallas kernels, front_layer(): pl.pallas_call(functools.partial(front_kernel, score_scale, shared_units)...  71.2 us
    pallas_call x1, Pallas kernels, finish_layer(): pl.pallas_call(finish_kernel, grid=(steps,), in_specs=[row(width)] * 2 +...  13 us

profile of v5, /device:TPU:0, one launch (start us, length us, event | category | flops | bytes accessed | tf_op | source)
XLA Modules:
  0.0 333.8 jit_solution(478022402548350563)
XLA Ops:
  0.7 0.7 fusion.3
  1.4 0.6 convert_element_type.5.hits_ref
  2.0 1.3 pad_maximum_fusion.bias_ref
  3.3 0.6 maximum_bitcast_fusion.freqs_ref
  3.9 0.0 copy-start.2
  3.9 0.0 copy-start
  3.9 71.2 %shard_map.348 = (f32[64,2048]{1,0:T(8,128)}, bf16[256,512]{1,0:T(8,128)(2,1)}, bf16[1024,512]{1,0:T(8,128)(2,1)}, bf16[1024,512]{1,0:T(8,128)(2,1)}, f32[4,256,...) custom-call(s32[8]{0:T(128)} %parents_ref.3, ...), custom_call_target="tpu_custom_call" | custom-call | flops 4294967296 | bytes 41943040 | tf_op jit(solution)/shard_map/pallas_call | solution.py:1280
  75.1 0.0 copy-done.2
  75.2 0.0 copy-done
  75.2 0.6 fusion.2.side_ref
  75.8 110.4 %shard_map.349 = (f32[64,2048]{1,0:T(8,128)}, bf16[64,2048]{1,0:T(8,128)(2,1)}, bf16[4,2,2,2,64,2048]{5,4,3,2,1,0:T(8,128)(2,1)}, bf16[352,2048]{1,0:T(8,128)(2,...) custom-call(f32[64,2048]{1,0:T(8,128)} %get-tuple-element.64.residua, ...), custom_call_target="tpu_custom_call" | custom-call | flops 51539607552 | bytes 62914560 | tf_op jit(solution)/shard_map/pallas_call | solution.py:770
  186.2 133.9 %shard_map.350 = (bf16[4,2,32,2048]{3,2,1,0:T(8,128)(2,1)}, bf16[4,2,32,2048]{3,2,1,0:T(8,128)(2,1)}, bf16[256,512]{1,0:T(8,128)(2,1)}, bf16[256,512]{1,0:T(8,12...) custom-call(f32[64,2048]{1,0:T(8,128)} %get-tuple-element.64.residua, ...), custom_call_target="tpu_custom_call" | custom-call | flops 25769803776 | bytes 41943040 | tf_op jit(solution)/shard_map/pallas_call | solution.py:1919
  320.1 0.0 copy-start.1
  320.1 13.0 %shard_map.351 = (bf16[256,2048]{1,0:T(8,128)(2,1)}, bf16[256,2048]{1,0:T(8,128)(2,1)}, f32[256,512]{1,0:T(8,128)}, f32[256,512]{1,0:T(8,128)}, f32[256,512]{1,0...) custom-call(bf16[256,2048]{1,0:T(8,128)(2,1)} %bitcast.43, ...), custom_call_target="tpu_custom_call" | custom-call | bytes 27262976 | tf_op jit(solution)/shard_map/pallas_call | solution.py:2253
  333.1 0.0 copy-done.1
  333.1 0.7 dynamic-slice_bitcast_fusion
  (3 shorter events, 0.0 us)
Async XLA Ops:
  3.9 71.2 %copy-start.2 = (bf16[2048]{0:T(1024)(128)(2,1)S(1)}, bf16[2048]{0:T(1024)(128)(2,1)}, u32[]{:S(2)}) copy-start(bf16[2048]{0:T(1024)(128)(2,1)} %param.35) | copy-start | bytes 12292
  3.9 71.3 %copy-start = (bf16[2048,8]{0,1:T(8,128)(2,1)S(1)}, bf16[2048,8]{0,1:T(8,128)(2,1)}, u32[]{:S(2)}) copy-start(bf16[2048,8]{0,1:T(8,128)(2,1)} %param.34) | copy-start | bytes 98308
  320.1 13.0 %copy-start.1 = (f32[16,128]{1,0:T(8,128)S(1)}, f32[16,128]{1,0:T(8,128)}, u32[]{:S(2)}) copy-start(f32[16,128]{1,0:T(8,128)} %get-tuple-element.98) | copy-start | bytes 24580

commit v6 on v5

--- a/solution.py
+++ b/solution.py
@@ -286,6 +286,7 @@
     both_all,
     scaled_all,
     scaled_now,
+    down_back_all,
     sums,
     got_core,
     got_x1,
@@ -294,7 +295,9 @@
     got_x2,
     got_z,
     kept_ref,
-    ffn_chunk,
+    out_send,
+    out_own,
+    got_out,
     tile_gate,
     tile_up,
     tile_down,
@@ -308,6 +311,7 @@
     rs_core,
     rs_links,
     rs_z,
+    rs_out,
 ):
     shared_units, shared_pad, expert_units, experts, unit_pad, half, wide, capacity = units
     bf16, f32 = jnp.bfloat16, jnp.float32
@@ -431,7 +435,7 @@
         corner_copy(k).wait_recv()
 
     def core_copy(k):
-        return remote(sums.at[k, flip(core)], got_core.at[k], rs_core, (k,), sibling)
+        return remote(sums.at[k, flip(core)], got_core.at[k % 2], rs_core, (k,), sibling)
 
     left, right = pl.ds(0, half), pl.ds(half, wide - half)
 
@@ -439,13 +443,13 @@
         return [
             remote(
                 sums.at[k, core, :, flip(east), :, left],
-                got_x1.at[k],
+                got_x1.at[k % 2],
                 rs_links, (0, k),
                 x_side,
             ),
             remote(
                 sums.at[k, core, flip(north), :, :, right],
-                got_y1.at[k],
+                got_y1.at[k % 2],
                 rs_links, (1, k),
                 y_side,
             ),
@@ -455,13 +459,13 @@
         return [
             remote(
                 sums.at[k, core, flip(north), east, :, left],
-                got_y2.at[k],
+                got_y2.at[k % 2],
                 rs_links, (2, k),
                 y_side,
             ),
             remote(
                 sums.at[k, core, north, flip(east), :, right],
-                got_x2.at[k],
+                got_x2.at[k % 2],
                 rs_links, (3, k),
                 x_side,
             ),
@@ -477,7 +481,7 @@
         core_copy(k).wait_recv()
         for y in range(2):
             for x in range(2):
-                add(sums.at[k, core, y, x], got_core[k, y, x])
+                add(sums.at[k, core, y, x], got_core[k % 2, y, x])
         for copy in first_copies(k):
             copy.start()
 
@@ -485,19 +489,19 @@
         x_copy, y_copy = first_copies(k)
         x_copy.wait_recv()
         for y in range(2):
-            add(sums.at[k, core, y, east, :, left], got_x1[k, y])
+            add(sums.at[k, core, y, east, :, left], got_x1[k % 2, y])
         y_copy.wait_recv()
         for x in range(2):
-            add(sums.at[k, core, north, x, :, right], got_y1[k, x])
+            add(sums.at[k, core, north, x, :, right], got_y1[k % 2, x])
         for copy in second_copies(k):
             copy.start()
 
     def after_second(k):
         y_copy, x_copy = second_copies(k)
         y_copy.wait_recv()
-        add(sums.at[k, core, north, east, :, left], got_y2[k])
+        add(sums.at[k, core, north, east, :, left], got_y2[k % 2])
         x_copy.wait_recv()
-        add(sums.at[k, core, north, east, :, right], got_x2[k])
+        add(sums.at[k, core, north, east, :, right], got_x2[k % 2])
         for level in range(1, 4):
 
             @pl.when(k == level)
@@ -544,10 +548,20 @@
     for c in range(2):
         for z in range(4):
             load_grad(c, z).wait()
+
+    def back_down(i, carry):
+        z, c = i // 2, i % 2
+        dy_block = dy_all[z, c].reshape(4 * rows, width)
+        down_back_all[z, c] = product_nt(dy_block, w_down[...]).astype(bf16)
+        return carry
+
+    lax.fori_loop(0, 3, back_down, 0)
     start_forward(0)
     z_copy(1).wait_recv()
     start_direct(1)
+    lax.fori_loop(3, 5, back_down, 0)
     start_corner(0)
+    lax.fori_loop(5, 8, back_down, 0)
 
     last = unit_pad - 128
     lane = lax.broadcasted_iota(jnp.int32, (1, 128), 1)
@@ -565,10 +579,9 @@
     def compute(k, c):
         z = level_of(k)
         row_block = rows_all[z, c].reshape(4 * rows, width)
-        dy_block = dy_all[z, c].reshape(4 * rows, width)
         pre_gate = product_nt(row_block, w_pre[:unit_pad])
         pre_up = product_nt(row_block, w_pre[unit_pad:])
-        down_back = product_nt(dy_block, w_down[...])
+        down_back = down_back_all[z, c].astype(f32)
         probs, shared_weight = routing(pre_gate[:, last:])
         kept = kept_ref[z, c]
         gate = (
@@ -602,10 +615,11 @@
         sums[k, c, :, :, :, 0:width] = normed_grad.reshape(2, 2, rows, width)
         sums[k, c, :, :, :, width:wide] = dot_block.astype(bf16).reshape(2, 2, rows, wide - width)
 
-    def store_chunk(k, c):
-        return pltpu.make_async_copy(
-            ffn_chunk, ffn_part_ref.at[level_of(k), c], store_sems.at[c]
-        )
+    def store_chunk(k):
+        return pltpu.make_async_copy(out_own, ffn_part_ref.at[level_of(k)], store_sems.at[0])
+
+    def out_core_copy(k):
+        return remote(out_send, got_out.at[k % 2], rs_out, (k,), sibling)
 
     def chunk(k, carry):
         @pl.when(k < 3)
@@ -637,17 +651,21 @@
         @pl.when(k >= 1)
         def _():
             after_first(k - 1)
-            store_chunk(k - 1, 1).wait()
-
-        def outputs(c, carry):
-            part = product(scaled_now[c], w_down[...]).astype(bf16)
-
-            @pl.when(c == 1)
+            store_chunk(k - 1).wait()
+            out_core_copy(k - 1).wait_send()
+
+        def outputs(i, carry):
+            part = product(scaled_now[(i + 1 + core) % 2], w_down[...]).astype(bf16)
+
+            @pl.when(i == 0)
             def _():
-                store_chunk(k, 0).wait()
-
-            ffn_chunk[...] = part.reshape(2, 2, rows, width)
-            store_chunk(k, c).start()
+                out_send[...] = part.reshape(2, 2, rows, width)
+                out_core_copy(k).start()
+
+            @pl.when(i == 1)
+            def _():
+                out_own[...] = part.reshape(2, 2, rows, width)
+
             return carry
 
         lax.fori_loop(0, 2, outputs, 0)
@@ -657,6 +675,11 @@
             start_corner(k + 1)
 
         after_core(k)
+        out_core_copy(k).wait_recv()
+        for y in range(2):
+            for x in range(2):
+                add(out_own.at[y, x], got_out[k % 2, y, x])
+        store_chunk(k).start()
 
         @pl.when(k >= 1)
         def _():
@@ -665,7 +688,8 @@
         return carry
 
     lax.fori_loop(0, 4, chunk, 0)
-    store_chunk(3, 1).wait()
+    store_chunk(3).wait()
+    out_core_copy(3).wait_send()
 
     tile = tile_gate.shape[2]
     tiles = width // tile
@@ -775,7 +799,7 @@
         out_shape=[
             shape((rows, width), f32),
             shape((rows, width), bf16),
-            shape((4, 2, 2, 2, rows, width), bf16),
+            shape((4, 2, 2, rows, width), bf16),
             shape((expert_units, width), bf16),
             shape((expert_units, width), bf16),
             shape((expert_units, width), bf16),
@@ -792,15 +816,18 @@
             pltpu.VMEM((2 * unit_pad, 32 * rows), bf16),
             pltpu.VMEM((unit_pad, 32 * rows), bf16),
             pltpu.VMEM((2, 4 * rows, unit_pad), bf16),
+            pltpu.VMEM((4, 2, 4 * rows, unit_pad), bf16),
             pltpu.VMEM((4, 2, 2, 2, rows, wide), bf16),
-            pltpu.VMEM((4, 2, 2, rows, wide), bf16),
-            pltpu.VMEM((4, 2, rows, half), bf16),
-            pltpu.VMEM((4, 2, rows, wide - half), bf16),
-            pltpu.VMEM((4, rows, half), bf16),
-            pltpu.VMEM((4, rows, wide - half), bf16),
+            pltpu.VMEM((2, 2, 2, rows, wide), bf16),
+            pltpu.VMEM((2, 2, rows, half), bf16),
+            pltpu.VMEM((2, 2, rows, wide - half), bf16),
+            pltpu.VMEM((2, rows, half), bf16),
+            pltpu.VMEM((2, rows, wide - half), bf16),
             pltpu.VMEM((4, rows, wide), bf16),
             pltpu.VMEM((4, 2, 4 * rows, 1), f32),
             pltpu.VMEM((2, 2, rows, width), bf16),
+            pltpu.VMEM((2, 2, rows, width), bf16),
+            pltpu.VMEM((2, 2, 2, rows, width), bf16),
             pltpu.VMEM((2, expert_units, tile), bf16),
             pltpu.VMEM((2, expert_units, tile), bf16),
             pltpu.VMEM((2, expert_units, tile), bf16),
@@ -813,6 +840,7 @@
             dma((2, 4, 4)),
             dma((2, 4)),
             dma((2, 4, 4)),
+            dma((2, 4)),
             dma((2, 4)),
         ],
         compiler_params=pltpu.CompilerParams(
@@ -1205,12 +1233,12 @@
     kv_gather.start_forward()
     lax.fori_loop(tiles // 2, tiles, pack, 0)
     kv_gather.start_last()
+    tail_gather.start()
     head_gather.start_forward()
     for i in (tiles - 2, tiles - 1):
         for copy in tile_stores(i, i % 2):
             copy.wait()
     kv_gather.finish()
-    tail_gather.start()
 
     for level, segment in enumerate(path):
         block = kv_all[jnp.maximum(segment, 0)]
@@ -1247,8 +1275,8 @@
     line = LineSum(lambda z: part_send.at[z], part_z, part_sems)
     line.start()
     head_gather.start_last()
+    tail_gather.start_forward()
     line.forward()
-    tail_gather.start_forward()
     attn = line.finish()
     own_rows = pl.ds(pl.multiple_of(column * rows, rows), rows)
     residual_ref[...] = hidden_ref[own_rows, :].astype(f32) + attn
@@ -1324,8 +1352,8 @@
         self.mine, self.theirs = mine, theirs
         self.got = (got_core, got_x1, got_y1, got_y2, got_x2)
         self.core_sems, self.sems = core_sems, sems
-        self.wide = got_core.shape[-1]
         self.half = got_x1.shape[-1]
+        self.wide = self.half + got_y1.shape[-1]
         self.left, self.right = pl.ds(0, self.half), pl.ds(self.half, self.wide - self.half)
         place = lax.axis_index("dp")
         self.core, self.east, self.north = place % 2, (place // 2) % 2, place // 4
@@ -1397,6 +1425,9 @@
         for y in range(2):
             for x in range(2):
                 self.add(mine.at[y, x], self.got[0][k, y, x])
+        self.start_first(k)
+
+    def start_first(self, k):
         for copy in self.first_copies(k):
             copy.start()
 
@@ -1422,7 +1453,8 @@
         return own
 
     def wait_sends(self, k):
-        self.core_copy(k).wait_send()
+        if self.theirs is not None:
+            self.core_copy(k).wait_send()
         for copy in self.first_copies(k) + self.second_copies(k):
             copy.wait_send()
 
@@ -1503,7 +1535,7 @@
     *rest,
 ):
     bf16, f32 = jnp.bfloat16, jnp.float32
-    out_scr, rest = rest[:7], rest[7:]
+    out_scr, rest = rest[:5], rest[5:]
     kv_scr, rest = rest[:7], rest[7:]
     w_scr, rest = rest[:7], rest[7:]
     wkv_sems, rest = rest[:2], rest[2:]
@@ -1526,7 +1558,7 @@
         )
 
     def load_out(z):
-        return pltpu.make_async_copy(ffn_part_ref.at[z, core], out_mine.at[z], load_sems.at[z])
+        return pltpu.make_async_copy(ffn_part_ref.at[z], out_mine.at[z], load_sems.at[z])
 
     loads = [
         pltpu.make_async_copy(w_query_ref, w_qkv.at[0], load_sems.at[5]),
@@ -1547,9 +1579,7 @@
         pl.semaphore_signal(barrier, inc=1, device_id=partner, device_id_type=MESH)
     pl.semaphore_wait(barrier, len(partners))
 
-    out_sum = PlaneSum(
-        lambda k: out_mine.at[k], lambda k: ffn_part_ref.at[k, flip(core)], *out_scr
-    )
+    out_sum = PlaneSum(lambda k: out_mine.at[k], None, None, *out_scr[:4], None, out_scr[4])
     kv_sum = PlaneSum(
         lambda k: kv_sums.at[k, core], lambda k: kv_sums.at[k, flip(core)], *kv_scr
     )
@@ -1567,13 +1597,11 @@
     low_line = LineGather(lambda z: low_all.at[z], low_sems)
     low_line.start()
     order = [other(column, k) for k in (1, 3, 2, 0)]
-    for z in order:
-        out_sum.start(z)
-    kv_path[...] = jnp.zeros(kv_path.shape, f32)
     for z in range(4):
         load_out(z).wait()
     for z in order:
-        out_sum.after_core(z)
+        out_sum.start_first(z)
+    kv_path[...] = jnp.zeros(kv_path.shape, f32)
     for copy in loads:
         copy.wait()
 
@@ -1628,11 +1656,12 @@
         @pl.when(i == 0)
         def _():
             out_sum.after_first(order[0])
+            out_sum.after_first(order[1])
 
         return carry
 
     lax.fori_loop(0, 2, half, 0)
-    for z in order[1:]:
+    for z in order[2:]:
         out_sum.after_first(z)
     load_value.start()
 
@@ -1666,6 +1695,9 @@
         added = own_kv[...].astype(f32) + kv_rows(0, which).reshape(4 * part_rows, -1)
         own_kv[...] = added.astype(bf16)
         kv_sum.after_core(which)
+    for z in order:
+        out_sum.after_second(z)
+    out_line.start()
 
     def bias_of(which, grad, begin):
         bias = jnp.sum(grad.astype(f32), 0, keepdims=True)
@@ -1704,9 +1736,6 @@
     w_sum.start(1)
     kv_sum.after_first(0)
     kv_sum.after_first(1)
-    for z in order:
-        out_sum.after_second(z)
-    out_line.start()
 
     load_value.wait()
     hidden_f = hidden_ref[...].astype(f32)
@@ -1955,7 +1984,8 @@
             pltpu.VMEM((8, 16, 2 * HEAD_DIM + HEAD_DIM), f32),
             pltpu.VMEM((4, 16, 2 * HEAD_DIM), f32),
         ]
-        + plane_scratch(4, rows, width)
+        + plane_scratch(4, rows, width)[1:5]
+        + plane_scratch(4, rows, width)[6:]
         + plane_scratch(2, tok_rows // 2, 2 * local_width)
         + plane_scratch(2, tok_rows, local_width)
         + plane_scratch(2, tok_rows // 2, 2 * local_width)[5:]
@@ -2227,11 +2257,9 @@
     ):
         target[...] = source[...].astype(f32)
 
-    @pl.when(pl.program_id(0) % 4 == 0)
-    def _():
-        for which, target in enumerate((s_gate_out, s_up_out, s_down_out)):
-            units = shared_in[:, which]
-            target[...] = units.reshape(-1, units.shape[-1]).T.astype(f32)
+    for which, target in enumerate((s_gate_out, s_up_out, s_down_out)):
+        units = shared_in[:, which]
+        target[...] = units.reshape(-1, units.shape[-1]).T.astype(f32)
 
     router_out[...] = small_in[0:experts]
     shared_gate_out[...] = small_in[experts : experts + 1]
@@ -2240,7 +2268,7 @@
 
 
 def finish_layer(hidden_out, hidden_grad, grads, shared, expert_grads, small, experts):
-    steps = 8
+    steps = 2
     tok_rows, width = hidden_out.shape
     local_width = grads[0].shape[1]
     units = shared.shape[2]
@@ -2255,12 +2283,12 @@
         grid=(steps,),
         in_specs=[row(width)] * 2
         + [row(local_width)] * 4
-        + [pl.BlockSpec((8, 3, units, tok_rows // 2), lambda i: (0, 0, 0, i // 4))]
+        + [pl.BlockSpec((8, 3, units, tok_rows // steps), lambda i: (0, 0, 0, i))]
         + [column] * 3
         + [whole(16, tok_rows)],
         out_specs=[row(width)] * 2
         + [row(local_width)] * 4
-        + [pl.BlockSpec((tok_rows // 2, 8 * units), lambda i: (i // 4, 0))] * 3
+        + [pl.BlockSpec((tok_rows // steps, 8 * units), lambda i: (i, 0))] * 3
         + [column] * 3
         + [whole(experts, tok_rows)]
         + [whole(1, tok_rows)] * 3,

time: 336 us -> 309 us (0.920)
  Pallas kernels: 328 us -> 303 us
    pallas_call x1, Pallas kernels: 134 us -> 122 us  [back_layer(): pl.pallas_call(functools.partial(back_kernel, score_scale, gain_row), out...]
    pallas_call x1, Pallas kernels: 110 us -> 104 us  [ffn_layer(): pl.pallas_call(functools.partial(ffn_kernel, (shared_units, shared_pad, e...]
    pallas_call x1, Pallas kernels: 13 us -> 9.2 us  [finish_layer(): pl.pallas_call(finish_kernel, grid=(steps,), in_specs=[row(width)] * 2 +...]
where the time goes in v6:
time: 309 us
  Pallas kernels  303 us (98%)
  other arithmetic  3.88 us (1%)
    pallas_call x1, Pallas kernels, back_layer(): pl.pallas_call(functools.partial(back_kernel, score_scale, gain_row), out...  122 us
    pallas_call x1, Pallas kernels, ffn_layer(): pl.pallas_call(functools.partial(ffn_kernel, (shared_units, shared_pad, e...  104 us
    pallas_call x1, Pallas kernels, front_layer(): pl.pallas_call(functools.partial(front_kernel, score_scale, shared_units)...  68 us
    pallas_call x1, Pallas kernels, finish_layer(): pl.pallas_call(finish_kernel, grid=(steps,), in_specs=[row(width)] * 2 +...  9.2 us

profile of v6, /device:TPU:0, one launch (start us, length us, event | category | flops | bytes accessed | tf_op | source)
XLA Modules:
  0.0 308.7 jit_solution(15038911098503629859)
XLA Ops:
  0.7 0.7 fusion.3
  1.4 0.6 convert_element_type.5.hits_ref
  2.0 1.3 pad_maximum_fusion.bias_ref
  3.3 0.6 maximum_bitcast_fusion.freqs_ref
  3.9 0.0 copy-start.2
  3.9 0.0 copy-start
  3.9 68.0 %shard_map.348 = (f32[64,2048]{1,0:T(8,128)}, bf16[256,512]{1,0:T(8,128)(2,1)}, bf16[1024,512]{1,0:T(8,128)(2,1)}, bf16[1024,512]{1,0:T(8,128)(2,1)}, f32[4,256,...) custom-call(s32[8]{0:T(128)} %parents_ref.3, ...), custom_call_target="tpu_custom_call" | custom-call | flops 4294967296 | bytes 41943040 | tf_op jit(solution)/shard_map/pallas_call | solution.py:1308
  71.9 0.0 copy-done.2
  71.9 0.0 copy-done
  71.9 0.6 fusion.2.side_ref
  72.6 104.1 %shard_map.349 = (f32[64,2048]{1,0:T(8,128)}, bf16[64,2048]{1,0:T(8,128)(2,1)}, bf16[4,2,2,64,2048]{4,3,2,1,0:T(8,128)(2,1)}, bf16[352,2048]{1,0:T(8,128)(2,1)},...) custom-call(f32[64,2048]{1,0:T(8,128)} %get-tuple-element.64.residua, ...), custom_call_target="tpu_custom_call" | custom-call | flops 51539607552 | bytes 62914560 | tf_op jit(solution)/shard_map/pallas_call | solution.py:794
  176.7 122.1 %shard_map.350 = (bf16[4,2,32,2048]{3,2,1,0:T(8,128)(2,1)}, bf16[4,2,32,2048]{3,2,1,0:T(8,128)(2,1)}, bf16[256,512]{1,0:T(8,128)(2,1)}, bf16[256,512]{1,0:T(8,12...) custom-call(f32[64,2048]{1,0:T(8,128)} %get-tuple-element.64.residua, ...), custom_call_target="tpu_custom_call" | custom-call | flops 25769803776 | bytes 41943040 | tf_op jit(solution)/shard_map/pallas_call | solution.py:1948
  298.8 0.0 copy-start.1
  298.8 9.2 %shard_map.351 = (bf16[256,2048]{1,0:T(8,128)(2,1)}, bf16[256,2048]{1,0:T(8,128)(2,1)}, f32[256,512]{1,0:T(8,128)}, f32[256,512]{1,0:T(8,128)}, f32[256,512]{1,0...) custom-call(bf16[256,2048]{1,0:T(8,128)(2,1)} %bitcast.43, ...), custom_call_target="tpu_custom_call" | custom-call | bytes 27262976 | tf_op jit(solution)/shard_map/pallas_call | solution.py:2281
  308.0 0.0 copy-done.1
  308.1 0.7 dynamic-slice_bitcast_fusion
  (3 shorter events, 0.0 us)
Async XLA Ops:
  3.9 68.0 %copy-start.2 = (bf16[2048]{0:T(1024)(128)(2,1)S(1)}, bf16[2048]{0:T(1024)(128)(2,1)}, u32[]{:S(2)}) copy-start(bf16[2048]{0:T(1024)(128)(2,1)} %param.35) | copy-start | bytes 12292
  3.9 68.0 %copy-start = (bf16[2048,8]{0,1:T(8,128)(2,1)S(1)}, bf16[2048,8]{0,1:T(8,128)(2,1)}, u32[]{:S(2)}) copy-start(bf16[2048,8]{0,1:T(8,128)(2,1)} %param.34) | copy-start | bytes 98308
  298.8 9.2 %copy-start.1 = (f32[16,128]{1,0:T(8,128)S(1)}, f32[16,128]{1,0:T(8,128)}, u32[]{:S(2)}) copy-start(f32[16,128]{1,0:T(8,128)} %get-tuple-element.98) | copy-start | bytes 24580

commit v7 on v6

--- a/solution.py
+++ b/solution.py
@@ -2,6 +2,7 @@
 
 import jax
 import jax.numpy as jnp
+import numpy as np
 from jax import lax
 from jax.experimental import pallas as pl
 from jax.experimental.pallas import tpu as pltpu
@@ -266,7 +267,8 @@
     gain_ref,
     hits_ref,
     grad_all_ref,
-    side_ref,
+    router_ref,
+    shared_gate_ref,
     shared_w_ref,
     e_gate_w_ref,
     e_up_w_ref,
@@ -357,7 +359,9 @@
         target[first + shared_units : first + shared_pad, :] = jnp.zeros((gap, width), bf16)
         rest = unit_pad - side_first
         target[first + side_first : first + unit_pad, :] = jnp.zeros((rest, width), bf16)
-    w_pre[side_first : side_first + side_ref.shape[0], :] = side_ref[...]
+    side_rows = [router_ref[...].astype(f32), shared_gate_ref[...].astype(f32)]
+    side_rows.append(jnp.zeros((16 - experts - 1, width), f32))
+    w_pre[side_first : side_first + 16, :] = jnp.concatenate(side_rows, 0).astype(bf16)
 
     def load_grad(c, z):
         return pltpu.make_async_copy(
@@ -778,7 +782,9 @@
             copy.wait_send()
 
 
-def ffn_layer(residual, ffn_gain, hits, grad_all, side, shared_w, expert_w, layout, capacity):
+def ffn_layer(
+    residual, ffn_gain, hits, grad_all, router, shared_gate, shared_w, expert_w, layout, capacity
+):
     shared_units, shared_pad, expert_units, experts, unit_pad = layout
     rows, width = residual.shape
     bf16, f32 = jnp.bfloat16, jnp.float32
@@ -806,7 +812,7 @@
             shape((width // tile, 3, shared_units, tile), bf16),
             shape((16, width), f32),
         ],
-        in_specs=[vmem, vmem, vmem, anywhere, vmem] + [anywhere] * 4,
+        in_specs=[vmem, vmem, vmem, anywhere, vmem, vmem] + [anywhere] * 4,
         out_specs=[vmem, vmem] + [anywhere] * 5 + [vmem],
         scratch_shapes=[
             pltpu.VMEM((4, 2, 2, 2, rows, width), bf16),
@@ -847,7 +853,7 @@
             collective_id=0, has_side_effects=True, vmem_limit_bytes=63 * 2**20
         ),
         cost_estimate=cost,
-    )(residual, ffn_gain, hits, grad_all, side, shared_w, *expert_w)
+    )(residual, ffn_gain, hits, grad_all, router, shared_gate, shared_w, *expert_w)
 
 
 def path_scalars(parents_ref, segment):
@@ -1060,9 +1066,11 @@
     parents_ref,
     hidden_ref,
     gain_ref,
-    bias_ref,
+    b_query_ref,
+    b_key_ref,
+    b_value_ref,
     freqs_ref,
-    hits_ref,
+    routes_ref,
     out_grad_ref,
     w_query_ref,
     w_key_ref,
@@ -1073,11 +1081,11 @@
     s_down_ref,
     residual_ref,
     query_ref,
-    key_ref,
-    value_ref,
+    key_out,
+    value_out,
     log_total_ref,
     attended_ref,
-    normed_ref,
+    normed_out,
     cosine_ref,
     sine_ref,
     hits_all_ref,
@@ -1090,6 +1098,9 @@
     part_z,
     s_tiles,
     t_tiles,
+    key_ref,
+    value_ref,
+    normed_ref,
     load_sems,
     tile_sems,
     store_sems,
@@ -1118,7 +1129,11 @@
     for copy in loads:
         copy.start()
     own_grad.start()
-    hits_all[place] = hits_ref[...]
+    expert_id = lax.broadcasted_iota(jnp.int32, hits_all.shape[1:], 0)
+    hits = jnp.zeros(hits_all.shape[1:], f32)
+    for choice in range(routes_ref.shape[0]):
+        hits = hits + jnp.where(expert_id == routes_ref[choice : choice + 1, :], 1.0, 0.0)
+    hits_all[place] = hits
 
     barrier = pltpu.get_barrier_semaphore()
     partners = peers[1:] + levels[1:]
@@ -1152,6 +1167,9 @@
 
     for j in range(1, 8):
         hit_copy(j).start()
+
+    def row_of(ref):
+        return jnp.concatenate([ref[h : h + 1, :] for h in range(ref.shape[0])], 1)
 
     path = path_scalars(parents_ref, place)
     depth = jnp.float32(-1.0)
@@ -1167,15 +1185,22 @@
     hidden_f = hidden_ref[...].astype(f32)
     scale_rows = lax.rsqrt(jnp.mean(hidden_f * hidden_f, 1, keepdims=True) + epsilon)
     normed_ref[...] = (hidden_f * scale_rows * gain_ref[...]).astype(bf16)
+    results = [
+        pltpu.make_async_copy(source, target, load_sems.at[5 + i])
+        for i, (source, target) in enumerate(
+            ((normed_ref, normed_out), (key_ref, key_out), (value_ref, value_out))
+        )
+    ]
+    results[0].start()
     for copy in loads[1:3]:
         copy.wait()
-    key = product(normed_ref[...], weights[1]) + bias_ref[1:2, :]
+    key = product(normed_ref[...], weights[1]) + row_of(b_key_ref)
     kv_all[place, :, :local_width] = turn(key, cosine, sine).astype(bf16)
-    value = product(normed_ref[...], weights[2]) + bias_ref[2:3, :]
+    value = product(normed_ref[...], weights[2]) + row_of(b_value_ref)
     kv_all[place, :, local_width:] = value.astype(bf16)
     kv_gather.start()
     loads[0].wait()
-    query = product(normed_ref[...], weights[0]) + bias_ref[0:1, :]
+    query = product(normed_ref[...], weights[0]) + row_of(b_query_ref)
     query_ref[...] = turn(query, cosine, sine).astype(bf16)
 
     tile, span = s_tiles.shape[2:]
@@ -1244,6 +1269,8 @@
         block = kv_all[jnp.maximum(segment, 0)]
         key_ref[level * tok_rows : (level + 1) * tok_rows, :] = block[:, :local_width]
         value_ref[level * tok_rows : (level + 1) * tok_rows, :] = block[:, local_width:]
+    for copy in results[1:]:
+        copy.start()
     key_rows = key_ref.shape[0]
     row_id = lax.broadcasted_iota(jnp.int32, (tok_rows, key_rows), 0)
     col_id = lax.broadcasted_iota(jnp.int32, (tok_rows, key_rows), 1)
@@ -1287,6 +1314,9 @@
     hits_all_ref[...] = hits_all[...]
     tail_gather.finish()
 
+    for copy in results:
+        copy.wait()
+
     for gather in (kv_gather, head_gather, tail_gather):
         gather.wait_sends()
     for j in range(1, 8):
@@ -1295,7 +1325,7 @@
 
 
 def front_layer(score_scale, shared_units, operands):
-    hidden, w_query = operands[1], operands[7]
+    hidden, w_query = operands[1], operands[9]
     tok_rows, width = hidden.shape
     rows, local_width = tok_rows // 4, w_query.shape[1]
     heads = local_width // HEAD_DIM
@@ -1321,8 +1351,10 @@
             shape((8, 4, rows, width), bf16),
             shape((3, shared_units, width), bf16),
         ],
-        in_specs=[smem] + [vmem] * 6 + [anywhere] * 7,
-        out_specs=[vmem] * 10 + [anywhere] * 2,
+        in_specs=[smem] + [vmem] * 8 + [anywhere] * 7,
+        out_specs=[vmem, vmem, anywhere, anywhere, vmem, vmem, anywhere]
+        + [vmem] * 3
+        + [anywhere] * 2,
         scratch_shapes=[
             pltpu.VMEM((4, width, local_width), bf16),
             pltpu.VMEM((8, tok_rows, 2 * local_width), bf16),
@@ -1331,7 +1363,10 @@
             pltpu.VMEM((4, rows, width), bf16),
             pltpu.VMEM((2, 3, tile, span), bf16),
             pltpu.VMEM((2, 3, span, tile), bf16),
-            dma((5,)),
+            pltpu.VMEM((LEVELS * tok_rows, local_width), bf16),
+            pltpu.VMEM((LEVELS * tok_rows, local_width), bf16),
+            pltpu.VMEM((tok_rows, width), bf16),
+            dma((8,)),
             dma((2, 3)),
             dma((2, 3)),
             dma((2, 8)),
@@ -1484,20 +1519,20 @@
 def back_kernel(
     score_scale,
     gain_row,
-    residual_ref,
-    res_grad_ref,
+    residual_in,
+    res_grad_in,
     res_low_ref,
     ffn_part_ref,
     shared_ref,
     small_ref,
     query_ref,
-    key_ref,
-    value_ref,
+    key_in,
+    value_in,
     parents_ref,
     log_total_ref,
     attended_ref,
-    normed_ref,
-    hidden_ref,
+    normed_in,
+    hidden_in,
     gain_ref,
     cosine_ref,
     sine_ref,
@@ -1532,6 +1567,12 @@
     small_send,
     small_got,
     small_z,
+    residual_ref,
+    res_grad_ref,
+    key_ref,
+    value_ref,
+    normed_ref,
+    hidden_ref,
     *rest,
 ):
     bf16, f32 = jnp.bfloat16, jnp.float32
@@ -1565,6 +1606,21 @@
         pltpu.make_async_copy(w_key_ref, w_qkv.at[1], load_sems.at[6]),
         pltpu.make_async_copy(w_out_ref, w_qkv.at[2], load_sems.at[4]),
     ]
+    fetches = [
+        pltpu.make_async_copy(source, target, load_sems.at[12 + i])
+        for i, (source, target) in enumerate(
+            (
+                (key_in, key_ref),
+                (value_in, value_ref),
+                (normed_in, normed_ref),
+                (hidden_in, hidden_ref),
+                (residual_in, residual_ref),
+                (res_grad_in, res_grad_ref),
+            )
+        )
+    ]
+    for copy in fetches:
+        copy.start()
     load_value = pltpu.make_async_copy(w_value_ref, w_qkv.at[2], load_sems.at[7])
     load_shared = pltpu.make_async_copy(shared_ref.at[place], shared_stage, load_sems.at[9])
     load_shared.start()
@@ -1602,7 +1658,7 @@
     for z in order:
         out_sum.start_first(z)
     kv_path[...] = jnp.zeros(kv_path.shape, f32)
-    for copy in loads:
+    for copy in loads + fetches:
         copy.wait()
 
     out_line = LineSum(lambda z: out_mine.at[z, north, east], out_z, out_sems)
@@ -1958,10 +2014,10 @@
             shape((16, tok_rows), f32),
             shape((16, HEAD_DIM), f32),
         ],
-        in_specs=[vmem, vmem, vmem, anywhere, anywhere, vmem]
-        + [vmem] * 3
+        in_specs=[anywhere, anywhere, vmem, anywhere, anywhere, vmem]
+        + [vmem, anywhere, anywhere]
         + [smem]
-        + [vmem] * 7
+        + [vmem, vmem, anywhere, anywhere, vmem, vmem, vmem]
         + [anywhere] * 4,
         out_specs=[anywhere] * 2 + [vmem] * 4 + [anywhere] + [vmem] * 2,
         scratch_shapes=[
@@ -1983,6 +2039,12 @@
             pltpu.VMEM((8, 16, 2 * HEAD_DIM + HEAD_DIM), f32),
             pltpu.VMEM((8, 16, 2 * HEAD_DIM + HEAD_DIM), f32),
             pltpu.VMEM((4, 16, 2 * HEAD_DIM), f32),
+            pltpu.VMEM(residual.shape, f32),
+            pltpu.VMEM(res_grad.shape, f32),
+            pltpu.VMEM(key.shape, bf16),
+            pltpu.VMEM(value.shape, bf16),
+            pltpu.VMEM(normed.shape, bf16),
+            pltpu.VMEM(hidden.shape, bf16),
         ]
         + plane_scratch(4, rows, width)[1:5]
         + plane_scratch(4, rows, width)[6:]
@@ -1990,7 +2052,7 @@
         + plane_scratch(2, tok_rows, local_width)
         + plane_scratch(2, tok_rows // 2, 2 * local_width)[5:]
         + [
-            dma((12,)),
+            dma((18,)),
             dma((2, 4)),
             dma((2, 4)),
             dma((2, 2, 4)),
@@ -2341,14 +2403,8 @@
     layout = (shared_units, shared_pad, expert_units, experts, units_pad)
     part_rows = tok_rows // columns
 
-    side = jnp.pad(
-        jnp.concatenate([w_router.T, shared_gate[None, :]], 0), ((0, 16 - experts - 1), (0, 0))
-    )
-    hits = jnp.any(
-        routes.T[:, None, :] == jnp.arange(16, dtype=jnp.int32)[None, :, None], 0
-    ).astype(f32)
-    freqs = rope_base ** (-jnp.arange(0, HEAD_DIM, 2, dtype=f32) / HEAD_DIM)
-    biases = jnp.stack([b_query.reshape(-1), b_key.reshape(-1), b_value.reshape(-1)])
+    powers = np.arange(0, HEAD_DIM, 2, dtype=np.float32) / np.float32(HEAD_DIM)
+    freqs = np.float32(rope_base) ** -powers
     (
         residual,
         query_rot,
@@ -2369,9 +2425,11 @@
             parents,
             hidden_in,
             attn_gain[None, :],
-            biases,
-            jnp.concatenate([freqs, freqs])[None, :],
-            hits,
+            b_query,
+            b_key,
+            b_value,
+            np.concatenate([freqs, freqs])[None, :],
+            routes.T,
             out_grad.reshape(columns, part_rows, model_width),
             w_query,
             w_key,
@@ -2396,7 +2454,8 @@
         ffn_gain[None, :],
         hits_all,
         grad_all.reshape(2, 2, 2, columns, part_rows, model_width),
-        side,
+        w_router.T,
+        shared_gate[None, :],
         shared_w,
         (expert_w_gate[0].T, expert_w_up[0].T, expert_w_down[0].T),
         layout,

time: 309 us -> 305 us (0.987)
  other arithmetic: 3.88 us -> 0 us
where the time goes in v7:
time: 305 us; the launch traced here: 303 us
  Pallas kernels  301 us (99%)
    pallas_call x1, Pallas kernels, back_layer(): pl.pallas_call(functools.partial(back_kernel, score_scale, gain_row), out...  120 us
    pallas_call x1, Pallas kernels, ffn_layer(): pl.pallas_call(functools.partial(ffn_kernel, (shared_units, shared_pad, e...  104 us
    pallas_call x1, Pallas kernels, front_layer(): pl.pallas_call(functools.partial(front_kernel, score_scale, shared_units)...  67.1 us
    pallas_call x1, Pallas kernels, finish_layer(): pl.pallas_call(finish_kernel, grid=(steps,), in_specs=[row(width)] * 2 +...  9.16 us

profile of v7, /device:TPU:0, one launch (start us, length us, event | category | flops | bytes accessed | tf_op | source)
XLA Modules:
  0.0 302.9 jit_solution(8778036116894133969)
XLA Ops:
  0.7 0.0 copy-start.1
  0.7 67.1 %shard_map.357 = (f32[64,2048]{1,0:T(8,128)}, bf16[256,512]{1,0:T(8,128)(2,1)}, bf16[1024,512]{1,0:T(8,128)(2,1)}, bf16[1024,512]{1,0:T(8,128)(2,1)}, f32[4,256,...) custom-call(s32[8]{0:T(128)} %parents_ref.3, ...), custom_call_target="tpu_custom_call" | custom-call | flops 4294967296 | bytes 41943040 | tf_op jit(solution)/shard_map/pallas_call | solution.py:1338
  67.8 0.0 copy-done.1
  67.8 0.6 broadcast_in_dim.21.shared_gate_ref
  68.4 104.2 %shard_map.358 = (f32[64,2048]{1,0:T(8,128)}, bf16[64,2048]{1,0:T(8,128)(2,1)}, bf16[4,2,2,64,2048]{4,3,2,1,0:T(8,128)(2,1)}, bf16[352,2048]{1,0:T(8,128)(2,1)},...) custom-call(f32[64,2048]{1,0:T(8,128)} %get-tuple-element.64.residua, ...), custom_call_target="tpu_custom_call" | custom-call | flops 51539607552 | bytes 62914560 | tf_op jit(solution)/shard_map/pallas_call | solution.py:800
  172.7 120.4 %shard_map.359 = (bf16[4,2,32,2048]{3,2,1,0:T(8,128)(2,1)}, bf16[4,2,32,2048]{3,2,1,0:T(8,128)(2,1)}, bf16[256,512]{1,0:T(8,128)(2,1)}, bf16[256,512]{1,0:T(8,12...) custom-call(f32[64,2048]{1,0:T(8,128)} %get-tuple-element.64.residua, ...), custom_call_target="tpu_custom_call" | custom-call | flops 25769803776 | bytes 41943040 | tf_op jit(solution)/shard_map/pallas_call | solution.py:2004
  293.1 0.0 copy-start
  293.1 9.2 %shard_map.360 = (bf16[256,2048]{1,0:T(8,128)(2,1)}, bf16[256,2048]{1,0:T(8,128)(2,1)}, f32[256,512]{1,0:T(8,128)}, f32[256,512]{1,0:T(8,128)}, f32[256,512]{1,0...) custom-call(bf16[256,2048]{1,0:T(8,128)(2,1)} %bitcast.38, ...), custom_call_target="tpu_custom_call" | custom-call | bytes 27262976 | tf_op jit(solution)/shard_map/pallas_call | solution.py:2343
  302.3 0.0 copy-done
  302.3 0.7 dynamic-slice_bitcast_fusion
  (1 shorter events, 0.0 us)
Async XLA Ops:
  0.7 67.2 %copy-start.1 = (bf16[2048]{0:T(1024)(128)(2,1)S(1)}, bf16[2048]{0:T(1024)(128)(2,1)}, u32[]{:S(2)}) copy-start(bf16[2048]{0:T(1024)(128)(2,1)} %param.36) | copy-start | bytes 12292
  293.1 9.2 %copy-start = (f32[16,128]{1,0:T(8,128)S(1)}, f32[16,128]{1,0:T(8,128)}, u32[]{:S(2)}) copy-start(f32[16,128]{1,0:T(8,128)} %get-tuple-element.98) | copy-start | bytes 24580

commit v8 on v7

--- a/solution.py
+++ b/solution.py
@@ -512,9 +512,9 @@
             def _():
                 level_copy(k, levels[level]).start()
 
+    start_direct(0)
     for k in (1, 2, 3):
         z_copy(k).start()
-    start_direct(0)
 
     tokens_dev = 4 * rows
     expert_id = lax.broadcasted_iota(jnp.int32, hits_ref.shape, 1)

time: 305 us -> 305 us (level)
  no operation moved by 1% of the time
where the time goes in v8:
time: 305 us; the launch traced here: 303 us
  Pallas kernels  301 us (99%)
    pallas_call x1, Pallas kernels, back_layer(): pl.pallas_call(functools.partial(back_kernel, score_scale, gain_row), out...  120 us
    pallas_call x1, Pallas kernels, ffn_layer(): pl.pallas_call(functools.partial(ffn_kernel, (shared_units, shared_pad, e...  104 us
    pallas_call x1, Pallas kernels, front_layer(): pl.pallas_call(functools.partial(front_kernel, score_scale, shared_units)...  67.1 us
    pallas_call x1, Pallas kernels, finish_layer(): pl.pallas_call(finish_kernel, grid=(steps,), in_specs=[row(width)] * 2 +...  9.16 us

profile of v8, /device:TPU:0, one launch (start us, length us, event | category | flops | bytes accessed | tf_op | source)
XLA Modules:
  0.0 303.0 jit_solution(15141856752026709906)
XLA Ops:
  0.7 0.0 copy-start.1
  0.7 67.1 %shard_map.357 = (f32[64,2048]{1,0:T(8,128)}, bf16[256,512]{1,0:T(8,128)(2,1)}, bf16[1024,512]{1,0:T(8,128)(2,1)}, bf16[1024,512]{1,0:T(8,128)(2,1)}, f32[4,256,...) custom-call(s32[8]{0:T(128)} %parents_ref.3, ...), custom_call_target="tpu_custom_call" | custom-call | flops 4294967296 | bytes 41943040 | tf_op jit(solution)/shard_map/pallas_call | solution.py:1338
  67.8 0.0 copy-done.1
  67.8 0.6 broadcast_in_dim.21.shared_gate_ref
  68.4 104.3 %shard_map.358 = (f32[64,2048]{1,0:T(8,128)}, bf16[64,2048]{1,0:T(8,128)(2,1)}, bf16[4,2,2,64,2048]{4,3,2,1,0:T(8,128)(2,1)}, bf16[352,2048]{1,0:T(8,128)(2,1)},...) custom-call(f32[64,2048]{1,0:T(8,128)} %get-tuple-element.64.residua, ...), custom_call_target="tpu_custom_call" | custom-call | flops 51539607552 | bytes 62914560 | tf_op jit(solution)/shard_map/pallas_call | solution.py:800
  172.7 120.4 %shard_map.359 = (bf16[4,2,32,2048]{3,2,1,0:T(8,128)(2,1)}, bf16[4,2,32,2048]{3,2,1,0:T(8,128)(2,1)}, bf16[256,512]{1,0:T(8,128)(2,1)}, bf16[256,512]{1,0:T(8,12...) custom-call(f32[64,2048]{1,0:T(8,128)} %get-tuple-element.64.residua, ...), custom_call_target="tpu_custom_call" | custom-call | flops 25769803776 | bytes 41943040 | tf_op jit(solution)/shard_map/pallas_call | solution.py:2004
  293.1 0.0 copy-start
  293.1 9.2 %shard_map.360 = (bf16[256,2048]{1,0:T(8,128)(2,1)}, bf16[256,2048]{1,0:T(8,128)(2,1)}, f32[256,512]{1,0:T(8,128)}, f32[256,512]{1,0:T(8,128)}, f32[256,512]{1,0...) custom-call(bf16[256,2048]{1,0:T(8,128)(2,1)} %bitcast.38, ...), custom_call_target="tpu_custom_call" | custom-call | bytes 27262976 | tf_op jit(solution)/shard_map/pallas_call | solution.py:2343
  302.3 0.0 copy-done
  302.3 0.7 dynamic-slice_bitcast_fusion
  (1 shorter events, 0.0 us)
Async XLA Ops:
  0.7 67.2 %copy-start.1 = (bf16[2048]{0:T(1024)(128)(2,1)S(1)}, bf16[2048]{0:T(1024)(128)(2,1)}, u32[]{:S(2)}) copy-start(bf16[2048]{0:T(1024)(128)(2,1)} %param.36) | copy-start | bytes 12292
  293.1 9.2 %copy-start = (f32[16,128]{1,0:T(8,128)S(1)}, f32[16,128]{1,0:T(8,128)}, u32[]{:S(2)}) copy-start(f32[16,128]{1,0:T(8,128)} %get-tuple-element.98) | copy-start | bytes 24580
